TPU v7x, 32 devices: a whole 2x2x4 slice. The times are simulated.
32 devices in a mesh: atom: 8 (over z, core), wave: 4 (over y, x).
Axes of the slice: x: 2, y: 2, z: 4, core: 2. Of those that a mesh axis runs over, the one named last changes fastest.
Arguments:
- features: bfloat16 [16384, 128], P(('atom', 'wave')), may hold values from -6 to 6
- species: int32 [16384], P(('atom', 'wave')), may hold values from 0 to 15
- coords: float32 [3, 16384], P(None, ('atom', 'wave')), may hold values from 0 to 1
- wave_index: int32 [3, 4096], P(None, 'wave'), may hold values from -16 to 16, as said below
- green: float32 [4096], P('wave'), may hold values from 4.8828126e-05 to 0.00048828125
- embed: bfloat16 [16, 128], replicated, may hold values from -3 to 3
- w_charge: bfloat16 [128, 64], replicated, may hold values from -0.5 to 0.5
- w_feat: bfloat16 [128, 256], replicated, may hold values from -0.5 to 0.5
- w_pot: bfloat16 [64, 256], replicated, may hold values from -0.75 to 0.75
- w_out: bfloat16 [256, 128], replicated, may hold values from -0.375 to 0.375
Outputs:
- updated: bfloat16 [16384, 128], P(('atom', 'wave'))
Inputs may be any that keep to these rules, and one draw needn't show every extreme that they name: `wave_index`: the 4096 wave vectors are distinct lattice vectors, and none is zero.
All inputs are finite; a program needn't handle non-finite values.
Results may differ from a plain program's by a relative error of at most 0.0075.
Values may be sent and summed in bfloat16 or wider, within the bound.
No kernel may reach another device: no remote copies, remote signals or barrier semaphores. Data moves between devices by JAX's collectives and lax.ppermute only.
A program may use at most 128 MiB of HBM per device.

v0:
```python
import math

import jax
import jax.numpy as jnp
from jax import lax
from jax.sharding import PartitionSpec as P

TWO_PI = 2.0 * math.pi
EPS = 1e-06
BLOCK_ROWS = 1024


def phases(points, waves):
    angle = points[0][:, None] * waves[0][None, :] + points[1][:, None] * waves[1][None, :]
    angle = TWO_PI * (angle + points[2][:, None] * waves[2][None, :])
    return jnp.concatenate([jnp.cos(angle), jnp.sin(angle)], axis=1).astype(jnp.bfloat16)


def phase_tile(points, waves):
    rows = points.shape[1]
    step = math.gcd(rows, BLOCK_ROWS)
    count = rows // step
    blocks = points.reshape(3, count, step).transpose(1, 0, 2)
    tiles = lax.map(lambda block: phases(block, waves), blocks)
    return tiles.reshape(rows, 2 * waves.shape[1])


def shards(features, species, coords, wave_index, green, embed, w_charge, w_feat, w_pot, w_out):
    hidden_in = features.astype(jnp.float32)
    scale = lax.rsqrt(jnp.mean(hidden_in * hidden_in, axis=1, keepdims=True) + EPS)
    onehot = (species[:, None] == jnp.arange(embed.shape[0], dtype=jnp.int32)[None, :]).astype(
        jnp.bfloat16
    )
    mixed = hidden_in * scale + jnp.dot(onehot, embed, preferred_element_type=jnp.float32)
    mixed_b = mixed.astype(jnp.bfloat16)
    charges = jnp.dot(mixed_b, w_charge, preferred_element_type=jnp.float32).astype(jnp.bfloat16)
    block_charges = lax.all_gather(charges, "wave", axis=0, tiled=True)
    block_points = lax.all_gather(coords, "wave", axis=1, tiled=True)
    waves = wave_index.astype(jnp.float32)
    kcount = waves.shape[1]
    tile = phase_tile(block_points, waves)
    green_both = jnp.concatenate([green, green])
    share_rows = 2 * kcount // lax.axis_size("atom")
    share = lax.psum_scatter(
        lax.dot_general(
            tile, block_charges, (((0,), (0,)), ((), ())), preferred_element_type=jnp.float32
        ),
        "atom",
        scatter_dimension=0,
        tiled=True,
    )
    share_green = lax.dynamic_slice_in_dim(
        green_both, lax.axis_index("atom") * share_rows, share_rows, 0
    )
    share_weighted = (share_green[:, None] * share).astype(jnp.bfloat16)
    weighted = lax.all_gather(share_weighted, "atom", axis=0, tiled=True)
    potential = lax.psum_scatter(
        jnp.dot(tile, weighted, preferred_element_type=jnp.float32),
        "wave",
        scatter_dimension=0,
        tiled=True,
    )
    potential_b = potential.astype(jnp.bfloat16)
    pre = jnp.dot(mixed_b, w_feat, preferred_element_type=jnp.float32) + jnp.dot(
        potential_b, w_pot, preferred_element_type=jnp.float32
    )
    activation = jax.nn.silu(pre).astype(jnp.bfloat16)
    return (hidden_in + jnp.dot(activation, w_out, preferred_element_type=jnp.float32)).astype(
        jnp.bfloat16
    )


def solution(mesh):
    placed = (
        P(("atom", "wave"), None),
        P(("atom", "wave")),
        P(None, ("atom", "wave")),
        P(None, "wave"),
        P("wave"),
        P(),
        P(),
        P(),
        P(),
        P(),
    )
    return jax.shard_map(
        shards, mesh=mesh, in_specs=placed, out_specs=P(("atom", "wave"), None), check_vma=False
    )
```

profile of v0, /device:TPU:0, one launch (start us, length us, event | category | flops | bytes accessed | tf_op | source)
XLA Modules:
  0.0 165.2 jit_solution(13967768444284009820)
XLA Ops:
  6.5 0.0 copy-start
  6.5 0.0 reduce-scatter.3.cloned.1.call-start
  6.5 9.9 %all_gather.9 = f32[3,2048]{1,0:T(4,128)S(1)} all-gather(f32[3,512]{1,0:T(4,128)} %param.14), channel_id=1, replica_groups=mesh['atom'=8,'wave'=4] {'wave'}, dimensions={1}, use_global_device_ids=true | all-gather | bytes 30720 | tf_op jit(solution)/shard_map/all_gather | solution.py:38
  16.4 0.7 convert_element_type.35
  17.1 0.0 copy-start.1
  17.1 0.0 copy-start.6
  17.1 0.0 copy-start.7
  17.1 0.0 copy-start.2
  17.2 39.5 %while.10 = (s32[]{:T(128)}, bf16[2,1024,2048]{2,1,0:T(8,128)(2,1)}, f32[2,3,1024]{2,1,0:T(4,128)S(1)}, f32[3,1024]{1,0:T(4,128)S(1)}, s32[]{:T(128)}, /*index=5*/s32[]{:T(128)}, s32[]{}, s32[]{}) while((s32[]{:T(128)}, bf16[2,1024,2048]{2,1,0:T(8,128)(2,1)}, f32[2,3,1024]{2,1,0:T(4,128)S(1)}, f32[3,1024]{1,0:T(4,128)S(1)}, s32[]{:T(128)}, ...), condition=%wide.region_2.3_spmd, body=%wide.region_1.2_spmd.sunk | while | flops 16777220 | bytes 12657273 | solution.py:24
  17.2 17.3 %fusion.29 = (bf16[1,1024,1024]{2,1,0:T(8,128)(2,1)S(1)}, bf16[1,1024,1024]{2,1,0:T(8,128)(2,1)S(1)}) fusion(f32[1024]{0:T(1024)S(1)} %bitcast.43, f32[1024]{0:T(1024)S(1)} %bitcast.41, f32[1024]{0:T(1024)S(1)} %bitcast.44, f32[1024]{0:T(1024)S(1)} %bitcast.40, f32[1024]{0:T(1024)S(1)} %bitcast.42, f32[1024]{0:T(1024)S(1)} %bitcast.39), kind=kLoop, calls=%fused_computation.4.clone.1 | loop fusion | flops 8388608 | bytes 4218880 | tf_op jit(solution)/shard_map/while/body/eval_jaxpr/concatenate | solution.py:16
  34.5 2.4 %maximum_dynamic-update-slice_fusion.2 = bf16[2,1024,2048]{2,1,0:T(8,128)(2,1)} fusion(bf16[2,1024,2048]{2,1,0:T(8,128)(2,1)} %get-tuple-element.94, s32[]{:T(128)} %get-tuple-element.93, bf16[1,1024,1024]{2,1,0:T(8,128)(2,1)S(1)} %get-tuple-element.83, bf16[1,1024,1024]{2,1,0:T(8,128)(2,1)S(1)} %get-tuple-element.84), kind=kLoop, calls=%fused_computation.clone.1 | loop fusion | flops 8388608 | bytes 8389120 | tf_op jit(solution)/shard_map/while/body/jit(dynamic_update_index_in_dim)/dynamic_update_slice | solution.py:24
  36.9 17.3 %fusion.29 = (bf16[1,1024,1024]{2,1,0:T(8,128)(2,1)S(1)}, bf16[1,1024,1024]{2,1,0:T(8,128)(2,1)S(1)}) fusion(f32[1024]{0:T(1024)S(1)} %bitcast.43, f32[1024]{0:T(1024)S(1)} %bitcast.41, f32[1024]{0:T(1024)S(1)} %bitcast.44, f32[1024]{0:T(1024)S(1)} %bitcast.40, f32[1024]{0:T(1024)S(1)} %bitcast.42, f32[1024]{0:T(1024)S(1)} %bitcast.39), kind=kLoop, calls=%fused_computation.4.clone.1 | loop fusion | flops 8388608 | bytes 4218880 | tf_op jit(solution)/shard_map/while/body/eval_jaxpr/concatenate | solution.py:16
  54.2 2.4 %maximum_dynamic-update-slice_fusion.2 = bf16[2,1024,2048]{2,1,0:T(8,128)(2,1)} fusion(bf16[2,1024,2048]{2,1,0:T(8,128)(2,1)} %get-tuple-element.94, s32[]{:T(128)} %get-tuple-element.93, bf16[1,1024,1024]{2,1,0:T(8,128)(2,1)S(1)} %get-tuple-element.83, bf16[1,1024,1024]{2,1,0:T(8,128)(2,1)S(1)} %get-tuple-element.84), kind=kLoop, calls=%fused_computation.clone.1 | loop fusion | flops 8388608 | bytes 8389120 | tf_op jit(solution)/shard_map/while/body/jit(dynamic_update_index_in_dim)/dynamic_update_slice | solution.py:24
  56.6 0.0 copy-done.1
  56.6 0.1 fusion.4
  56.8 0.0 copy-done.6
  56.8 0.0 copy-done.7
  56.8 0.3 fusion.3
  57.1 0.0 copy-done.2
  57.1 0.2 convolution_convert_fusion
  57.3 10.5 %all_gather.10 = bf16[2048,64]{1,0:T(8,128)(2,1)S(1)} all-gather(bf16[512,64]{1,0:T(8,128)(2,1)S(1)} %convolution_convert_fusion), channel_id=1, replica_groups=mesh['atom'=8,'wave'=4] {'wave'}, dimensions={0}, use_global_device_ids=true | all-gather | bytes 327680 | tf_op jit(solution)/shard_map/all_gather | solution.py:37
  67.7 0.0 copy-start.3
  67.7 6.8 %fusion.13 = f32[2048,64]{1,0:T(8,128)} fusion(bf16[2048,2048]{1,0:T(8,128)(2,1)} %bitcast.46, bf16[2048,64]{1,0:T(8,128)(2,1)S(1)} %all_gather.10), kind=kOutput, calls=%fused_computation.31 | convolution fusion | flops 536870912 | bytes 9175040 | tf_op jit(solution)/shard_map/dot_general | solution.py:45
  74.6 0.0 reduce-scatter.3.cloned.1.call-update
  74.6 0.0 reduce-scatter.5.cloned.1.call-start
  74.6 0.0 copy-done.3
  74.7 0.1 fusion.9
  74.7 32.7 %reduce-scatter.3.cloned.1.call-done = f32[256,64]{1,0:T(8,128)} async-done(((f32[2048,64]{1,0:T(8,128)}), f32[256,64]{1,0:T(8,128)}) %reduce-scatter.3.cloned.1.call-update) | async-done | bytes 65552 | tf_op jit(solution)/shard_map/reduce_scatter | solution.py:44
  107.4 1.0 multiply_convert_fusion.1
  108.5 15.0 %all_gather.11 = bf16[2048,64]{1,0:T(8,128)(2,1)S(1)} all-gather(bf16[256,64]{1,0:T(8,128)(2,1)S(1)} %multiply_convert_fusion.1), channel_id=1, replica_groups=mesh['atom'=8,'wave'=4] {'atom'}, dimensions={0}, use_global_device_ids=true | all-gather | bytes 294912 | tf_op jit(solution)/shard_map/all_gather | solution.py:56
  123.5 0.0 copy-start.4
  123.5 0.0 copy-start.5
  123.5 6.8 %fusion.14 = f32[2048,64]{1,0:T(8,128)} fusion(bf16[2048,2048]{1,0:T(8,128)(2,1)} %bitcast.47, bf16[2048,64]{1,0:T(8,128)(2,1)S(1)} %all_gather.11), kind=kOutput, calls=%fused_computation.32 | convolution fusion | flops 536870912 | bytes 9175040 | tf_op jit(solution)/shard_map/dot_general | solution.py:58
  130.3 0.0 reduce-scatter.5.cloned.1.call-update
  130.3 0.0 copy-done
  130.3 0.2 fusion.12
  130.5 25.8 %reduce-scatter.5.cloned.1.call-done = f32[512,64]{1,0:T(8,128)} async-done(((f32[2048,64]{1,0:T(8,128)}), f32[512,64]{1,0:T(8,128)}) %reduce-scatter.5.cloned.1.call-update) | async-done | bytes 131088 | tf_op jit(solution)/shard_map/reduce_scatter | solution.py:57
  156.3 0.0 copy-done.4
  156.3 0.0 copy-done.5
  156.3 2.0 %fusion.2 = bf16[512,128]{1,0:T(8,128)(2,1)} fusion(bf16[256,128]{1,0:T(8,128)(2,1)S(1)} %copy-done.4, f32[512,256]{1,0:T(8,128)S(1)} %fusion.12, bf16[64,256]{1,0:T(8,128)(2,1)S(1)} %copy-done.5, bf16[512,128]{1,0:T(8,128)(2,1)S(1)} %copy-done.1, f32[512,64]{1,0:T(8,128)} %reduce-scatter.5.cloned.1.call-done), kind=kOutput, calls=%fused_computation.12 | convolution fusion | flops 51347456 | bytes 1015808 | tf_op jit(solution)/shard_map/dot_general | solution.py:68
  (6 shorter events, 0.1 us)
Async XLA Ops:
  6.5 123.8 %copy-start = (bf16[128,256]{1,0:T(8,128)(2,1)S(1)}, bf16[128,256]{1,0:T(8,128)(2,1)}, u32[]{:S(2)}) copy-start(bf16[128,256]{1,0:T(8,128)(2,1)} %param.19) | copy-start | bytes 196612
  6.5 100.9 %reduce-scatter.3.cloned.1.call-start = ((), (), s32[]{:S(2)}) async-start(), calls=%async_computation.2 | async-start | bytes 1179648 | tf_op jit(solution)/shard_map/reduce_scatter | solution.py:44
  17.1 39.5 %copy-start.1 = (bf16[512,128]{1,0:T(8,128)(2,1)S(1)}, bf16[512,128]{1,0:T(8,128)(2,1)}, u32[]{:S(2)}) copy-start(bf16[512,128]{1,0:T(8,128)(2,1)} %param.12) | copy-start | bytes 393220
  17.1 39.6 %copy-start.6 = (bf16[16,128]{1,0:T(8,128)(2,1)S(1)}, bf16[16,128]{1,0:T(8,128)(2,1)}, u32[]{:S(2)}) copy-start(bf16[16,128]{1,0:T(8,128)(2,1)} %param.17) | copy-start | bytes 12292
  17.1 39.7 %copy-start.7 = (s32[512]{0:T(512)S(1)}, s32[512]{0:T(512)}, u32[]{:S(2)}) copy-start(s32[512]{0:T(512)} %param.13) | copy-start | bytes 6148
  17.1 39.9 %copy-start.2 = (bf16[128,64]{0,1:T(8,128)(2,1)S(1)}, bf16[128,64]{0,1:T(8,128)(2,1)}, u32[]{:S(2)}) copy-start(bf16[128,64]{0,1:T(8,128)(2,1)} %param.18) | copy-start | bytes 49156
  67.7 6.9 %copy-start.3 = (f32[1024]{0:T(1024)S(1)}, f32[1024]{0:T(1024)}, u32[]{:S(2)}) copy-start(f32[1024]{0:T(1024)} %param.16) | copy-start | bytes 12292
  74.6 81.7 %reduce-scatter.5.cloned.1.call-start = ((), (), s32[]{:S(2)}) async-start(), calls=%async_computation.3 | async-start | bytes 1310720 | tf_op jit(solution)/shard_map/reduce_scatter | solution.py:57
  123.5 32.9 %copy-start.4 = (bf16[256,128]{1,0:T(8,128)(2,1)S(1)}, bf16[256,128]{1,0:T(8,128)(2,1)}, u32[]{:S(2)}) copy-start(bf16[256,128]{1,0:T(8,128)(2,1)} %param.21) | copy-start | bytes 196612
  123.5 32.9 %copy-start.5 = (bf16[64,256]{1,0:T(8,128)(2,1)S(1)}, bf16[64,256]{1,0:T(8,128)(2,1)}, u32[]{:S(2)}) copy-start(bf16[64,256]{1,0:T(8,128)(2,1)} %param.20) | copy-start | bytes 98308
Sparse Core Ops, SparseCore 0:
  74.7 32.6 reduce-scatter.2
  130.4 25.8 reduce-scatter.4
where the time goes:
time: 166 us; the launch traced here: 165 us
  waiting for transfers between devices  58.5 us (35%)
  other arithmetic  41.3 us (25%)
  blocking collectives  35.4 us (21%)
  matrix products  16.3 us (10%)
  between operations  13.5 us (8%)
    concatenate x2, other arithmetic, phases(): jnp.concatenate([jnp.cos(angle), jnp.sin(angle)], axis=1)  34.5 us
    reduce_scatter x1, waiting for transfers between devices, shards(): lax.psum_scatter(lax.dot_general(tile, block_charges, (((0,), (0,)), ((),...  32.7 us
    reduce_scatter x1, waiting for transfers between devices, shards(): lax.psum_scatter(jnp.dot(tile, weighted, preferred_element_type=jnp.float...  25.8 us
    all_gather x1, blocking collectives, shards(): weighted = lax.all_gather(share_weighted, 'atom', axis=0, tiled=True)  15 us
    all_gather x1, blocking collectives, shards(): block_charges = lax.all_gather(charges, 'wave', axis=0, tiled=True)  10.5 us
    all_gather x1, blocking collectives, shards(): block_points = lax.all_gather(coords, 'wave', axis=1, tiled=True)  9.87 us
    dot_general x1, matrix products, shards(): lax.dot_general(tile, block_charges, (((0,), (0,)), ((), ())), preferred_...  6.84 us
    dot_general x1, matrix products, shards(): jnp.dot(tile, weighted, preferred_element_type=jnp.float32)  6.82 us
  transfers between devices with their start and end apart: 2, of which 2 were waited for; matrix products, arithmetic and copies ran while one was open for 0% of the time, Pallas kernels for 0%

commit v1 on v0

v1 whole, which is shorter than its diff:
```python
import functools
import math

import jax
import jax.numpy as jnp
import numpy as np
from jax import lax
from jax.experimental import pallas as pl
from jax.experimental.pallas import tpu as pltpu
from jax.sharding import PartitionSpec as P

EPS = 1e-06
F32 = jnp.float32
BF16 = jnp.bfloat16
VMEM = pl.BlockSpec(memory_space=pltpu.VMEM)
POINT_ROWS = 16
CORES = 2


def fit(values, degree, count=4000):
    u = (np.cos(np.pi * (np.arange(count) + 0.5) / count) + 1) / 8
    cheb = np.polynomial.chebyshev.Chebyshev.fit(u, values(np.sqrt(u)), degree, domain=[0, 0.25])
    return [float(c) for c in cheb.convert(kind=np.polynomial.Polynomial).coef]


HALF_SIN = fit(lambda r: math.sqrt(2) * np.sin(np.pi * r) / r, 3)
HALF_COS = fit(lambda r: math.sqrt(2) * np.cos(np.pi * r), 3)


def horner(coefs, u):
    total = coefs[-1]
    for c in coefs[-2::-1]:
        total = total * u + c
    return total


def phase_rows(n, x):
    turns = jnp.dot(n, x, preferred_element_type=F32)
    r = turns - jnp.round(turns)
    u = r * r
    s = horner(HALF_SIN, u) * r
    c = horner(HALF_COS, u)
    return jnp.concatenate([1.0 - s * s, s * c], axis=0).astype(BF16)


def nt(a, b):
    return lax.dot_general(a, b, (((1,), (1,)), ((), ())), preferred_element_type=F32)


def tn(a, b):
    return lax.dot_general(a, b, (((0,), (0,)), ((), ())), preferred_element_type=F32)


def triple_rows(values, width):
    row = lax.broadcasted_iota(jnp.int32, (POINT_ROWS, width), 0)
    part = row % 3
    picked = jnp.where(part == 0, values[0:1], jnp.where(part == 1, values[1:2], values[2:3]))
    return row, picked


def pre_kernel(features_ref, species_ref, coords_ref, embed_ref, w_charge_ref, mixed_ref, message_ref):
    rows = features_ref.shape[0]
    q = w_charge_ref.shape[1]
    hidden = features_ref[...].astype(F32)
    scale = lax.rsqrt(jnp.mean(hidden * hidden, axis=1, keepdims=True) + EPS)
    kinds = embed_ref.shape[0]
    onehot = (
        lax.broadcasted_iota(jnp.int32, (kinds, rows), 0) == species_ref[...]
    ).astype(F32).astype(BF16)
    mixed = (hidden * scale + tn(onehot, embed_ref[...])).astype(BF16)
    mixed_ref[...] = mixed
    charges = lax.dot_general(
        w_charge_ref[...], mixed, (((0,), (1,)), ((), ())), preferred_element_type=F32
    )
    message_ref[0:q, :] = charges.astype(BF16)
    row, point = triple_rows(coords_ref[...], rows)
    high = point.astype(BF16).astype(F32)
    middle = (point - high).astype(BF16).astype(F32)
    low = point - high - middle
    parts = jnp.where(row < 3, high, jnp.where(row < 6, middle, jnp.where(row < 9, low, 0.0)))
    message_ref[q:, :] = parts.astype(BF16)


def own_kernel(zcount, kchunk, waves_ref, message_ref, n_ref, p_own_ref, p_other_ref, s_own_ref, s_other_ref, all_n):
    width = waves_ref.shape[1]
    q = message_ref.shape[0] - POINT_ROWS
    row, index = triple_rows(waves_ref[...].astype(F32), width)
    all_n[...] = jnp.where(row < 9, index, 0.0).T
    me = lax.axis_index("atom")
    z, core = me // CORES, me % CORES
    x = message_ref[q:, :]
    charges = message_ref[0:q, :]
    for half, (p_ref, s_ref) in enumerate(((p_own_ref, s_own_ref), (p_other_ref, s_other_ref))):
        for r in range(zcount):
            j = (z ^ r) * CORES + (core ^ half)
            n = all_n[pl.ds(pl.multiple_of(j * kchunk, kchunk), kchunk), :].astype(BF16)
            at = (half * zcount + r) * kchunk
            n_ref[at : at + kchunk, :] = n
            rows = phase_rows(n, x)
            lo = r * 2 * kchunk
            p_ref[lo : lo + 2 * kchunk, :] = rows
            s_ref[:, lo : lo + 2 * kchunk] = nt(charges, rows)


def half_kernel(half, zcount, kchunk, rounded, count, *refs):
    n_ref, s_in_ref = refs[0], refs[1]
    messages = refs[2 : 2 + count]
    p_ref, s_ref = refs[2 + count :]
    q = messages[0].shape[0] - POINT_ROWS
    atoms = messages[0].shape[1]
    for r in range(zcount):
        at = (half * zcount + r) * kchunk
        n = n_ref[at : at + kchunk, :]
        lo = r * 2 * kchunk
        total = s_in_ref[:, lo : lo + 2 * kchunk]
        for b, message_ref in enumerate(messages):
            rows = phase_rows(n, message_ref[q:, :])
            p_ref[lo : lo + 2 * kchunk, b * atoms : (b + 1) * atoms] = rows
            total = total + nt(message_ref[0:q, :], rows)
        s_ref[:, lo : lo + 2 * kchunk] = total.astype(s_ref.dtype)


def share_kernel(s_ref, got_ref, mine_ref, *send_refs):
    width = mine_ref.shape[1]
    for r, ref in enumerate((mine_ref,) + send_refs):
        part = s_ref[:, r * width : (r + 1) * width] + got_ref[:, r * width : (r + 1) * width].astype(F32)
        ref[...] = part.astype(ref.dtype)


def weight_kernel(mine_ref, green_ref, *refs):
    out_ref = refs[-1]
    total = mine_ref[...]
    for ref in refs[:-1]:
        total = total + ref[...].astype(F32)
    me = lax.axis_index("atom")
    green = green_ref[pl.ds(me, 1), :]
    out_ref[...] = (total * jnp.concatenate([green, green], axis=1)).astype(BF16)


def first_half_kernel(w_ref, p0_ref, p_ref, own_ref, rest_ref):
    own_ref[...] = jnp.dot(w_ref[...], p0_ref[...], preferred_element_type=F32)
    rest_ref[...] = jnp.dot(w_ref[...], p_ref[...], preferred_element_type=F32)


def send_half_kernel(w_ref, p_ref, rest_ref, *send_refs):
    atoms = send_refs[0].shape[1]
    for b, ref in enumerate(send_refs):
        part = jnp.dot(w_ref[...], p_ref[:, b * atoms : (b + 1) * atoms], preferred_element_type=F32)
        ref[...] = (rest_ref[:, b * atoms : (b + 1) * atoms] + part).astype(BF16)


def keep_half_kernel(w_ref, p0_ref, own_ref, mixed_ref, w_feat_ref, total_ref, pre_ref):
    total_ref[...] = own_ref[...] + jnp.dot(w_ref[...], p0_ref[...], preferred_element_type=F32)
    pre_ref[...] = jnp.dot(mixed_ref[...], w_feat_ref[...], preferred_element_type=F32)


def last_kernel(features_ref, total_ref, pre_ref, w_pot_ref, w_out_ref, *refs):
    out_ref = refs[-1]
    potential = total_ref[...]
    for ref in refs[:-1]:
        potential = potential + ref[...].astype(F32)
    pre = pre_ref[...] + tn(potential.astype(BF16), w_pot_ref[...])
    activation = (pre / (1.0 + jnp.exp(-pre))).astype(BF16)
    out = features_ref[...].astype(F32) + jnp.dot(activation, w_out_ref[...], preferred_element_type=F32)
    out_ref[...] = out.astype(BF16)


def call(kernel, outs, *args, scratch=(), flops=0):
    size = sum(math.prod(a.shape) * a.dtype.itemsize for a in (*args, *outs))
    limit = min(max(4 * size, 16 << 20), 56 << 20)
    return pl.pallas_call(
        kernel,
        out_shape=outs,
        in_specs=[VMEM] * len(args),
        out_specs=[VMEM] * len(outs),
        scratch_shapes=list(scratch),
        compiler_params=pltpu.CompilerParams(vmem_limit_bytes=limit),
        cost_estimate=pl.CostEstimate(flops=flops, bytes_accessed=size, transcendentals=0),
    )(*args)


def swap(value, axis, bit):
    count = lax.axis_size(axis)
    return lax.ppermute(value, axis, [(i, i ^ bit) for i in range(count)])


def shards(features, species, coords, wave_index, green, embed, w_charge, w_feat, w_pot, w_out):
    array = jax.ShapeDtypeStruct
    atoms = features.shape[0]
    q = w_charge.shape[1]
    hidden = w_feat.shape[1]
    waves = wave_index.shape[1]
    wcount = lax.axis_size("wave")
    acount = lax.axis_size("atom")
    zcount = acount // CORES
    kchunk = waves // acount
    half_rows = 2 * kchunk * zcount
    rest = (wcount - 1) * atoms

    mixed, message = call(
        pre_kernel,
        [array(features.shape, BF16), array((q + POINT_ROWS, atoms), BF16)],
        features, species.reshape(1, atoms), coords, embed, w_charge,
    )
    messages = [swap(message, "wave", b) for b in range(1, wcount)]
    n, p_own0, p_other0, s_own0, s_other0 = call(
        functools.partial(own_kernel, zcount, kchunk),
        [
            array((waves, POINT_ROWS), BF16),
            array((half_rows, atoms), BF16),
            array((half_rows, atoms), BF16),
            array((q, half_rows), F32),
            array((q, half_rows), F32),
        ],
        wave_index, message,
        scratch=[pltpu.VMEM((waves, POINT_ROWS), F32)],
        flops=4 * half_rows * atoms * q,
    )

    def half_call(half, s_in, dtype):
        return call(
            functools.partial(half_kernel, half, zcount, kchunk, None, wcount - 1),
            [array((half_rows, rest), BF16), array((q, half_rows), dtype)],
            n, s_in, *messages,
            flops=2 * half_rows * rest * q,
        )

    p_other, s_other = half_call(1, s_other0, BF16)
    got = swap(s_other, "atom", 1)
    p_own, s_own = half_call(0, s_own0, F32)
    chunk = (q, 2 * kchunk)
    mine, *shares = call(
        share_kernel,
        [array(chunk, F32)] + [array(chunk, BF16)] * (zcount - 1),
        s_own, got,
    )
    shares = [swap(value, "atom", CORES * (r + 1)) for r, value in enumerate(shares)]
    (weighted,) = call(
        weight_kernel, [array(chunk, BF16)], mine, green.reshape(acount, kchunk), *shares
    )
    w_own = jnp.concatenate(
        [weighted] + [swap(weighted, "atom", CORES * r) for r in range(1, zcount)], axis=1
    )
    w_other = swap(w_own, "atom", 1)
    own_a, rest_a = call(
        first_half_kernel,
        [array((q, atoms), F32), array((q, rest), F32)],
        w_own, p_own0, p_own,
        flops=2 * half_rows * (rest + atoms) * q,
    )
    sends = call(
        send_half_kernel, [array((q, atoms), BF16)] * (wcount - 1), w_other, p_other, rest_a,
        flops=2 * half_rows * rest * q,
    )
    parts = [swap(value, "wave", b + 1) for b, value in enumerate(sends)]
    total, pre = call(
        keep_half_kernel,
        [array((q, atoms), F32), array((atoms, hidden), F32)],
        w_other, p_other0, own_a, mixed, w_feat,
        flops=2 * half_rows * atoms * q,
    )
    (out,) = call(
        last_kernel, [array(features.shape, BF16)],
        features, total, pre, w_pot, w_out, *parts,
    )
    return out


def solution(mesh):
    placed = (
        P(("atom", "wave"), None),
        P(("atom", "wave")),
        P(None, ("atom", "wave")),
        P(None, "wave"),
        P("wave"),
        P(),
        P(),
        P(),
        P(),
        P(),
    )
    return jax.shard_map(
        shards, mesh=mesh, in_specs=placed, out_specs=P(("atom", "wave"), None), check_vma=False
    )
```

time: 166 us -> 47.9 us (0.29)
  waiting for transfers between devices: 58.5 us -> 12.6 us
  other arithmetic: 41.3 us -> 0.01 us
  blocking collectives: 35.4 us -> 0 us
  starting transfers between devices: 0.04 us -> 17.2 us
  matrix products: 16.3 us -> 0 us
  between operations: 13.5 us -> 0.15 us
  Pallas kernels: 0 us -> 12.2 us
  local copies, waits for them, and re-layouts: 0.09 us -> 5.22 us
    reduce_scatter x2 -> x0, waiting for transfers between devices: 58.5 us -> none  [the longest x1 32.7 us: shards(): lax.psum_scatter(lax.dot_general(tile, block_charges, (((0,), (0,)), ((),...]
    all_gather x3 -> x0, blocking collectives: 35.4 us -> none  [the longest x1 15 us: shards(): weighted = lax.all_gather(share_weighted, 'atom', axis=0, tiled=True)]
    concatenate x3 -> x1, other arithmetic: 34.6 us -> 0.01 us  [shards(): jnp.concatenate([weighted] + [swap(weighted, 'atom', CORES * r) for r in...]
    ppermute x0 -> x14, starting transfers between devices: none -> 17.2 us  [swap(): return lax.ppermute(value, axis, [(i, i ^ bit) for i in range(count)])]
    dot_general x6 -> x0, matrix products: 16.3 us -> none  [the longest x1 6.84 us: shards(): lax.dot_general(tile, block_charges, (((0,), (0,)), ((), ())), preferred_...]
    ppermute x0 -> x14, waiting for transfers between devices: none -> 12.6 us  [swap(): return lax.ppermute(value, axis, [(i, i ^ bit) for i in range(count)])]
    pallas_call x0 -> x10, Pallas kernels: none -> 12.2 us  [call(): pl.pallas_call(kernel, out_shape=outs, in_specs=[VMEM] * len(args), out_s...]
    unnamed x16 -> x21, local copies, waits for them, and re-layouts: 0.03 us -> 5.22 us
  transfers between devices with their start and end apart: 2 -> 14, of which waited for: 2 -> 10; matrix products, arithmetic and copies ran while one was open for 0% -> 0% of each run, Pallas kernels for 0% -> 15%
where the time goes in v1:
time: 47.9 us; the launch traced here: 47.4 us
  starting transfers between devices  17.2 us (36%)
  waiting for transfers between devices  12.6 us (26%)
  Pallas kernels  12.2 us (25%)
  local copies, waits for them, and re-layouts  5.22 us (11%)
    ppermute x14, starting transfers between devices, swap(): return lax.ppermute(value, axis, [(i, i ^ bit) for i in range(count)])  17.2 us
    ppermute x14, waiting for transfers between devices, swap(): return lax.ppermute(value, axis, [(i, i ^ bit) for i in range(count)])  12.6 us
    pallas_call x10, Pallas kernels, call(): pl.pallas_call(kernel, out_shape=outs, in_specs=[VMEM] * len(args), out_s...  12.2 us
    unnamed x21, local copies, waits for them, and re-layouts  5.22 us
  transfers between devices with their start and end apart: 14, of which 10 were waited for; matrix products, arithmetic and copies ran while one was open for 0% of the time, Pallas kernels for 15%

profile of v1, /device:TPU:0, one launch (start us, length us, event | category | flops | bytes accessed | tf_op | source)
XLA Modules:
  0.0 47.4 jit_solution(11982831918725655627)
XLA Ops:
  0.0 0.8 %copy.11.w_charge_ref = bf16[128,64]{1,0:T(8,128)(2,1)S(1)} copy(bf16[128,64]{0,1:T(8,128)(2,1)} %param.16) | data formatting | bytes 32768 | tf_op args[6]
  0.8 0.0 copy-start
  0.8 0.9 %copy-done = bf16[512,128]{1,0:T(8,128)(2,1)S(1)} copy-done((bf16[512,128]{1,0:T(8,128)(2,1)S(1)}, bf16[512,128]{1,0:T(8,128)(2,1)}, u32[]{:S(2)}) %copy-start) | copy-done | bytes 131096
  1.7 0.7 %copy-done.5 = f32[3,512]{1,0:T(4,128)S(1)} copy-done((f32[3,512]{1,0:T(4,128)S(1)}, f32[3,512]{1,0:T(4,128)}, u32[]{:S(2)}) %copy-start.5) | copy-done | bytes 6168
  2.4 0.7 %copy-done.6 = bf16[16,128]{1,0:T(8,128)(2,1)S(1)} copy-done((bf16[16,128]{1,0:T(8,128)(2,1)S(1)}, bf16[16,128]{1,0:T(8,128)(2,1)}, u32[]{:S(2)}) %copy-start.6) | copy-done | bytes 4120
  3.1 0.7 %copy-done.8 = s32[512]{0:T(512)S(1)} copy-done((s32[512]{0:T(512)S(1)}, s32[512]{0:T(512)}, u32[]{:S(2)}) %copy-start.8) | copy-done | bytes 2072
  3.8 0.4 shard_map.100
  4.2 4.0 %collective-permute-start.2 = (bf16[80,512]{1,0:T(8,128)(2,1)S(1)}, bf16[80,512]{1,0:T(8,128)(2,1)S(1)}, u32[]{:S(2)}, u32[]{:S(2)}) collective-permute-start(bf16[80,512]{1,0:T(8,128)(2,1)S(1)} %get-tuple-element.27.message_ref), channel_id=1, source_target_pairs={{0,3},{1,2},{2,1},{3,0},{4,7},{5,6},{6,5},{7,4},{8,11},{9,10},{10,... | collective-permute-start | bytes 245768 | tf_op jit(solution)/shard_map/ppermute | solution.py:184
  8.2 0.5 %collective-permute-start.1 = (bf16[80,512]{1,0:T(8,128)(2,1)S(1)}, bf16[80,512]{1,0:T(8,128)(2,1)S(1)}, u32[]{:S(2)}, u32[]{:S(2)}) collective-permute-start(bf16[80,512]{1,0:T(8,128)(2,1)S(1)} %get-tuple-element.27.message_ref), channel_id=1, source_target_pairs={{0,2},{1,3},{2,0},{3,1},{4,6},{5,7},{6,4},{7,5},{8,10},{9,11},{10,... | collective-permute-start | bytes 245768 | tf_op jit(solution)/shard_map/ppermute | solution.py:184
  8.7 0.1 collective-permute-start
  8.8 0.7 %copy-done.9 = s32[3,1024]{1,0:T(4,128)S(1)} copy-done((s32[3,1024]{1,0:T(4,128)S(1)}, s32[3,1024]{1,0:T(4,128)}, u32[]{:S(2)}) %copy-start.9) | copy-done | bytes 12312
  9.5 2.6 %shard_map.101 = (bf16[1024,16]{1,0:T(8,128)(2,1)S(1)}, bf16[1024,512]{1,0:T(8,128)(2,1)S(1)}, bf16[1024,512]{1,0:T(8,128)(2,1)S(1)}, f32[64,1024]{1,0:T(8,128)S(1)}, f32[64,1024]{1,0:T(8,128)S(1)}) custom-call(s32[3,1024]{1,0:T(4,128)S(1)} %copy-done.9, bf16[80,512]{1,0:T(8,128)(2,1)S(1)} %get-tuple-element.27.message_ref), custom_call_target="tpu_custom_call" | custom-call | flops 134217728 | bytes 2748416 | tf_op jit(solution)/shard_map/pallas_call | solution.py:171
  12.1 0.0 collective-permute-done.2.refs_4_
  12.1 0.5 collective-permute-done.1.refs_3_
  12.6 0.5 %collective-permute-done.refs_2_ = bf16[80,512]{1,0:T(8,128)(2,1)S(1)} collective-permute-done((bf16[80,512]{1,0:T(8,128)(2,1)S(1)}, bf16[80,512]{1,0:T(8,128)(2,1)S(1)}, u32[]{:S(2)}, u32[]{:S(2)}) %collective-permute-start) | collective-permute-done | bytes 81952 | tf_op jit(solution)/shard_map/ppermute | solution.py:184
  13.1 3.1 %shard_map.103 = (bf16[1024,1536]{1,0:T(8,128)(2,1)S(1)}, bf16[64,1024]{1,0:T(8,128)(2,1)S(1)}) custom-call(bf16[1024,16]{1,0:T(8,128)(2,1)S(1)} %get-tuple-element.28.refs_0_, f32[64,1024]{1,0:T(8,128)S(1)} %get-tuple-element.31.refs_1_, bf16[80,512]{1,0:T(8,128)(2,1)S(1)} %collective-permute-done.refs_2_, ...), custom_call_target="tpu_custom_call" | custom-call | flops 201326592 | bytes 3817472 | tf_op jit(solution)/shard_map/pallas_call | solution.py:171
  16.2 0.1 collective-permute-start.3
  16.3 3.1 %shard_map.102 = (bf16[1024,1536]{1,0:T(8,128)(2,1)S(1)}, f32[64,1024]{1,0:T(8,128)S(1)}) custom-call(bf16[1024,16]{1,0:T(8,128)(2,1)S(1)} %get-tuple-element.28.refs_0_, f32[64,1024]{1,0:T(8,128)S(1)} %get-tuple-element.29.refs_1_, bf16[80,512]{1,0:T(8,128)(2,1)S(1)} %collective-permute-done.refs_2_, bf16[80,512]{1,0:T(8,128)(2,1)S(1)} %collective-permute-done.1.refs_3_, ...), custom_call_target="tpu_custom_call" | custom-call | flops 201326592 | bytes 3948544 | tf_op jit(solution)/shard_map/pallas_call | solution.py:171
  19.5 0.0 collective-permute-done.3.got_ref
  19.5 1.6 %collective-permute-start.4 = (bf16[64,256]{1,0:T(8,128)(2,1)S(1)}, bf16[64,256]{1,0:T(8,128)(2,1)S(1)}, u32[]{:S(2)}, u32[]{:S(2)}) collective-permute-start(bf16[64,256]{1,0:T(8,128)(2,1)S(1)} %get-tuple-element.34), channel_id=1, source_target_pairs={{0,8},{4,12},{8,0},{12,4},{16,24},{20,28},{24,16},{28,20},{1,9},{5... | collective-permute-start | bytes 98312 | tf_op jit(solution)/shard_map/ppermute | solution.py:184
  21.1 2.6 %collective-permute-start.5 = (bf16[64,256]{1,0:T(8,128)(2,1)S(1)}, bf16[64,256]{1,0:T(8,128)(2,1)S(1)}, u32[]{:S(2)}, u32[]{:S(2)}) collective-permute-start(bf16[64,256]{1,0:T(8,128)(2,1)S(1)} %get-tuple-element.35), channel_id=1, source_target_pairs={{0,16},{4,20},{8,24},{12,28},{16,0},{20,4},{24,8},{28,12},{1,17},{... | collective-permute-start | bytes 98312 | tf_op jit(solution)/shard_map/ppermute | solution.py:184
  23.7 0.2 collective-permute-start.6
  24.0 0.0 collective-permute-done.4.refs_0_
  24.0 2.6 %collective-permute-done.5.refs_1_ = bf16[64,256]{1,0:T(8,128)(2,1)S(1)} collective-permute-done((bf16[64,256]{1,0:T(8,128)(2,1)S(1)}, bf16[64,256]{1,0:T(8,128)(2,1)S(1)}, u32[]{:S(2)}, u32[]{:S(2)}) %collective-permute-start.5) | collective-permute-done | bytes 32800 | tf_op jit(solution)/shard_map/ppermute | solution.py:184
  26.5 2.9 %collective-permute-done.6.refs_2_ = bf16[64,256]{1,0:T(8,128)(2,1)S(1)} collective-permute-done((bf16[64,256]{1,0:T(8,128)(2,1)S(1)}, bf16[64,256]{1,0:T(8,128)(2,1)S(1)}, u32[]{:S(2)}, u32[]{:S(2)}) %collective-permute-start.6) | collective-permute-done | bytes 32800 | tf_op jit(solution)/shard_map/ppermute | solution.py:184
  29.4 0.7 %copy-done.7 = f32[1024]{0:T(1024)S(1)} copy-done((f32[1024]{0:T(1024)S(1)}, f32[1024]{0:T(1024)}, u32[]{:S(2)}) %copy-start.7) | copy-done | bytes 4120
  30.2 0.5 %collective-permute-start.9 = (bf16[64,256]{1,0:T(8,128)(2,1)S(1)}, bf16[64,256]{1,0:T(8,128)(2,1)S(1)}, u32[]{:S(2)}, u32[]{:S(2)}) collective-permute-start(bf16[64,256]{1,0:T(8,128)(2,1)S(1)} %shard_map.105), channel_id=1, source_target_pairs={{0,24},{4,28},{8,16},{12,20},{16,8},{20,12},{24,0},{28,4},{1,25},{... | collective-permute-start | bytes 98312 | tf_op jit(solution)/shard_map/ppermute | solution.py:184
  30.6 0.0 collective-permute-start.8
  30.6 4.0 %collective-permute-start.7 = (bf16[64,256]{1,0:T(8,128)(2,1)S(1)}, bf16[64,256]{1,0:T(8,128)(2,1)S(1)}, u32[]{:S(2)}, u32[]{:S(2)}) collective-permute-start(bf16[64,256]{1,0:T(8,128)(2,1)S(1)} %shard_map.105), channel_id=1, source_target_pairs={{0,8},{4,12},{8,0},{12,4},{16,24},{20,28},{24,16},{28,20},{1,9},{5... | collective-permute-start | bytes 98312 | tf_op jit(solution)/shard_map/ppermute | solution.py:184
  34.6 1.3 %collective-permute-done.9 = bf16[64,256]{1,0:T(8,128)(2,1)S(1)} collective-permute-done((bf16[64,256]{1,0:T(8,128)(2,1)S(1)}, bf16[64,256]{1,0:T(8,128)(2,1)S(1)}, u32[]{:S(2)}, u32[]{:S(2)}) %collective-permute-start.9) | collective-permute-done | bytes 32800 | tf_op jit(solution)/shard_map/ppermute | solution.py:184
  35.9 0.0 collective-permute-done.8
  35.9 0.6 %collective-permute-done.7 = bf16[64,256]{1,0:T(8,128)(2,1)S(1)} collective-permute-done((bf16[64,256]{1,0:T(8,128)(2,1)S(1)}, bf16[64,256]{1,0:T(8,128)(2,1)S(1)}, u32[]{:S(2)}, u32[]{:S(2)}) %collective-permute-start.7) | collective-permute-done | bytes 32800 | tf_op jit(solution)/shard_map/ppermute | solution.py:184
  36.5 0.1 collective-permute-start.10
  36.6 0.0 copy-start.2
  36.6 0.8 %shard_map.106 = (f32[64,512]{1,0:T(8,128)S(1)}, f32[64,1536]{1,0:T(8,128)S(1)}) custom-call(bf16[64,1024]{1,0:T(8,128)(2,1)S(1)} %pad_maximum_fusion.w_ref, bf16[1024,512]{1,0:T(8,128)(2,1)S(1)} %get-tuple-element.38.p0_ref, bf16[1024,1536]{1,0:T(8,128)(2,1)S(1)} %get-tuple-element.39.p_ref), custom_call_target="tpu_custom_call" | custom-call | flops 268435456 | bytes 4849664 | tf_op jit(solution)/shard_map/pallas_call | solution.py:171
  37.4 0.0 copy-start.1
  37.5 0.0 copy-start.3
  37.5 0.0 copy-start.4
  37.5 0.5 collective-permute-done.10.w_ref
  37.9 0.7 %shard_map.108 = (bf16[64,512]{1,0:T(8,128)(2,1)S(1)}, bf16[64,512]{1,0:T(8,128)(2,1)S(1)}, bf16[64,512]{1,0:T(8,128)(2,1)S(1)}) custom-call(bf16[64,1024]{1,0:T(8,128)(2,1)S(1)} %collective-permute-done.10.w_ref, bf16[1024,1536]{1,0:T(8,128)(2,1)S(1)} %get-tuple-element.44.p_ref, f32[64,1536]{1,0:T(8,128)S(1)} %get-tuple-element.45.rest_ref), custom_call_target="tpu_custom_call" | custom-call | flops 201326592 | bytes 3866624 | tf_op jit(solution)/shard_map/pallas_call | solution.py:171
  38.6 1.1 %collective-permute-start.11 = (bf16[64,512]{1,0:T(8,128)(2,1)S(1)}, bf16[64,512]{1,0:T(8,128)(2,1)S(1)}, u32[]{:S(2)}, u32[]{:S(2)}) collective-permute-start(bf16[64,512]{1,0:T(8,128)(2,1)S(1)} %get-tuple-element.46), channel_id=1, source_target_pairs={{0,1},{1,0},{2,3},{3,2},{4,5},{5,4},{6,7},{7,6},{8,9},{9,8},{10,11... | collective-permute-start | bytes 196616 | tf_op jit(solution)/shard_map/ppermute | solution.py:184
  39.6 1.5 %collective-permute-start.12 = (bf16[64,512]{1,0:T(8,128)(2,1)S(1)}, bf16[64,512]{1,0:T(8,128)(2,1)S(1)}, u32[]{:S(2)}, u32[]{:S(2)}) collective-permute-start(bf16[64,512]{1,0:T(8,128)(2,1)S(1)} %get-tuple-element.47), channel_id=1, source_target_pairs={{0,2},{1,3},{2,0},{3,1},{4,6},{5,7},{6,4},{7,5},{8,10},{9,11},{10,... | collective-permute-start | bytes 196616 | tf_op jit(solution)/shard_map/ppermute | solution.py:184
  41.1 1.0 %collective-permute-start.13 = (bf16[64,512]{1,0:T(8,128)(2,1)S(1)}, bf16[64,512]{1,0:T(8,128)(2,1)S(1)}, u32[]{:S(2)}, u32[]{:S(2)}) collective-permute-start(bf16[64,512]{1,0:T(8,128)(2,1)S(1)} %get-tuple-element.48), channel_id=1, source_target_pairs={{0,3},{1,2},{2,1},{3,0},{4,7},{5,6},{6,5},{7,4},{8,11},{9,10},{10,... | collective-permute-start | bytes 196616 | tf_op jit(solution)/shard_map/ppermute | solution.py:184
  42.1 0.4 shard_map.107
  42.5 0.4 collective-permute-done.11.refs_0_
  42.9 1.0 %collective-permute-done.12.refs_1_ = bf16[64,512]{1,0:T(8,128)(2,1)S(1)} collective-permute-done((bf16[64,512]{1,0:T(8,128)(2,1)S(1)}, bf16[64,512]{1,0:T(8,128)(2,1)S(1)}, u32[]{:S(2)}, u32[]{:S(2)}) %collective-permute-start.12) | collective-permute-done | bytes 65568 | tf_op jit(solution)/shard_map/ppermute | solution.py:184
  43.9 2.4 %collective-permute-done.13.refs_2_ = bf16[64,512]{1,0:T(8,128)(2,1)S(1)} collective-permute-done((bf16[64,512]{1,0:T(8,128)(2,1)S(1)}, bf16[64,512]{1,0:T(8,128)(2,1)S(1)}, u32[]{:S(2)}, u32[]{:S(2)}) %collective-permute-start.13) | collective-permute-done | bytes 65568 | tf_op jit(solution)/shard_map/ppermute | solution.py:184
  46.3 1.1 %shard_map.109 = bf16[512,128]{1,0:T(8,128)(2,1)} custom-call(bf16[512,128]{1,0:T(8,128)(2,1)S(1)} %copy-done.1, f32[64,512]{1,0:T(8,128)S(1)} %get-tuple-element.42.total_ref, f32[512,256]{1,0:T(8,128)S(1)} %get-tuple-element.43.pre_ref, bf16[64,256]{1,0:T(8,128)(2,1)S(1)} %copy-done.4, bf16[256,128]{1,0:T(8,128)(2,1)S(1)} %copy-done.3, ...), custom_call_target="tpu_custom_call" | custom-call | bytes 1212416 | tf_op jit(solution)/shard_map/pallas_call | solution.py:171
  (12 shorter events, 0.1 us)
Async XLA Ops:
  0.8 0.9 %copy-start = (bf16[512,128]{1,0:T(8,128)(2,1)S(1)}, bf16[512,128]{1,0:T(8,128)(2,1)}, u32[]{:S(2)}) copy-start(bf16[512,128]{1,0:T(8,128)(2,1)} %features_ref.3) | copy-start | bytes 393220
  1.7 0.7 %copy-start.5 = (f32[3,512]{1,0:T(4,128)S(1)}, f32[3,512]{1,0:T(4,128)}, u32[]{:S(2)}) copy-start(f32[3,512]{1,0:T(4,128)} %coords_ref.1) | copy-start | bytes 18436
  2.4 0.7 %copy-start.6 = (bf16[16,128]{1,0:T(8,128)(2,1)S(1)}, bf16[16,128]{1,0:T(8,128)(2,1)}, u32[]{:S(2)}) copy-start(bf16[16,128]{1,0:T(8,128)(2,1)} %embed_ref.1) | copy-start | bytes 12292
  3.1 0.7 %copy-start.8 = (s32[512]{0:T(512)S(1)}, s32[512]{0:T(512)}, u32[]{:S(2)}) copy-start(s32[512]{0:T(512)} %param.11) | copy-start | bytes 6148
  4.2 7.9 %collective-permute-start.2 = (bf16[80,512]{1,0:T(8,128)(2,1)S(1)}, bf16[80,512]{1,0:T(8,128)(2,1)S(1)}, u32[]{:S(2)}, u32[]{:S(2)}) collective-permute-start(bf16[80,512]{1,0:T(8,128)(2,1)S(1)} %get-tuple-element.27.message_ref), channel_id=1, source_target_pairs={{0,3},{1,2},{2,1},{3,0},{4,7},{5,6},{6,5},{7,4},{8,11},{9,10},{10,... | collective-permute-start | bytes 245768 | tf_op jit(solution)/shard_map/ppermute | solution.py:184
  8.2 4.4 %collective-permute-start.1 = (bf16[80,512]{1,0:T(8,128)(2,1)S(1)}, bf16[80,512]{1,0:T(8,128)(2,1)S(1)}, u32[]{:S(2)}, u32[]{:S(2)}) collective-permute-start(bf16[80,512]{1,0:T(8,128)(2,1)S(1)} %get-tuple-element.27.message_ref), channel_id=1, source_target_pairs={{0,2},{1,3},{2,0},{3,1},{4,6},{5,7},{6,4},{7,5},{8,10},{9,11},{10,... | collective-permute-start | bytes 245768 | tf_op jit(solution)/shard_map/ppermute | solution.py:184
  8.7 4.4 %collective-permute-start = (bf16[80,512]{1,0:T(8,128)(2,1)S(1)}, bf16[80,512]{1,0:T(8,128)(2,1)S(1)}, u32[]{:S(2)}, u32[]{:S(2)}) collective-permute-start(bf16[80,512]{1,0:T(8,128)(2,1)S(1)} %get-tuple-element.27.message_ref), channel_id=1, source_target_pairs={{0,1},{1,0},{2,3},{3,2},{4,5},{5,4},{6,7},{7,6},{8,9},{9,8},{10,11... | collective-permute-start | bytes 245768 | tf_op jit(solution)/shard_map/ppermute | solution.py:184
  8.8 0.7 %copy-start.9 = (s32[3,1024]{1,0:T(4,128)S(1)}, s32[3,1024]{1,0:T(4,128)}, u32[]{:S(2)}) copy-start(s32[3,1024]{1,0:T(4,128)} %waves_ref.1) | copy-start | bytes 36868
  16.2 3.2 %collective-permute-start.3 = (bf16[64,1024]{1,0:T(8,128)(2,1)S(1)}, bf16[64,1024]{1,0:T(8,128)(2,1)S(1)}, u32[]{:S(2)}, u32[]{:S(2)}) collective-permute-start(bf16[64,1024]{1,0:T(8,128)(2,1)S(1)} %get-tuple-element.32), channel_id=1, source_target_pairs={{0,4},{4,0},{8,12},{12,8},{16,20},{20,16},{24,28},{28,24},{1,5},{5... | collective-permute-start | bytes 393224 | tf_op jit(solution)/shard_map/ppermute | solution.py:184
  19.5 4.5 %collective-permute-start.4 = (bf16[64,256]{1,0:T(8,128)(2,1)S(1)}, bf16[64,256]{1,0:T(8,128)(2,1)S(1)}, u32[]{:S(2)}, u32[]{:S(2)}) collective-permute-start(bf16[64,256]{1,0:T(8,128)(2,1)S(1)} %get-tuple-element.34), channel_id=1, source_target_pairs={{0,8},{4,12},{8,0},{12,4},{16,24},{20,28},{24,16},{28,20},{1,9},{5... | collective-permute-start | bytes 98312 | tf_op jit(solution)/shard_map/ppermute | solution.py:184
  21.1 5.4 %collective-permute-start.5 = (bf16[64,256]{1,0:T(8,128)(2,1)S(1)}, bf16[64,256]{1,0:T(8,128)(2,1)S(1)}, u32[]{:S(2)}, u32[]{:S(2)}) collective-permute-start(bf16[64,256]{1,0:T(8,128)(2,1)S(1)} %get-tuple-element.35), channel_id=1, source_target_pairs={{0,16},{4,20},{8,24},{12,28},{16,0},{20,4},{24,8},{28,12},{1,17},{... | collective-permute-start | bytes 98312 | tf_op jit(solution)/shard_map/ppermute | solution.py:184
  23.7 5.7 %collective-permute-start.6 = (bf16[64,256]{1,0:T(8,128)(2,1)S(1)}, bf16[64,256]{1,0:T(8,128)(2,1)S(1)}, u32[]{:S(2)}, u32[]{:S(2)}) collective-permute-start(bf16[64,256]{1,0:T(8,128)(2,1)S(1)} %get-tuple-element.36), channel_id=1, source_target_pairs={{0,24},{4,28},{8,16},{12,20},{16,8},{20,12},{24,0},{28,4},{1,25},{... | collective-permute-start | bytes 98312 | tf_op jit(solution)/shard_map/ppermute | solution.py:184
  29.4 0.7 %copy-start.7 = (f32[1024]{0:T(1024)S(1)}, f32[1024]{0:T(1024)}, u32[]{:S(2)}) copy-start(f32[1024]{0:T(1024)} %param.14) | copy-start | bytes 12292
  30.2 5.8 %collective-permute-start.9 = (bf16[64,256]{1,0:T(8,128)(2,1)S(1)}, bf16[64,256]{1,0:T(8,128)(2,1)S(1)}, u32[]{:S(2)}, u32[]{:S(2)}) collective-permute-start(bf16[64,256]{1,0:T(8,128)(2,1)S(1)} %shard_map.105), channel_id=1, source_target_pairs={{0,24},{4,28},{8,16},{12,20},{16,8},{20,12},{24,0},{28,4},{1,25},{... | collective-permute-start | bytes 98312 | tf_op jit(solution)/shard_map/ppermute | solution.py:184
  30.6 5.3 %collective-permute-start.8 = (bf16[64,256]{1,0:T(8,128)(2,1)S(1)}, bf16[64,256]{1,0:T(8,128)(2,1)S(1)}, u32[]{:S(2)}, u32[]{:S(2)}) collective-permute-start(bf16[64,256]{1,0:T(8,128)(2,1)S(1)} %shard_map.105), channel_id=1, source_target_pairs={{0,16},{4,20},{8,24},{12,28},{16,0},{20,4},{24,8},{28,12},{1,17},{... | collective-permute-start | bytes 98312 | tf_op jit(solution)/shard_map/ppermute | solution.py:184
  30.6 5.9 %collective-permute-start.7 = (bf16[64,256]{1,0:T(8,128)(2,1)S(1)}, bf16[64,256]{1,0:T(8,128)(2,1)S(1)}, u32[]{:S(2)}, u32[]{:S(2)}) collective-permute-start(bf16[64,256]{1,0:T(8,128)(2,1)S(1)} %shard_map.105), channel_id=1, source_target_pairs={{0,8},{4,12},{8,0},{12,4},{16,24},{20,28},{24,16},{28,20},{1,9},{5... | collective-permute-start | bytes 98312 | tf_op jit(solution)/shard_map/ppermute | solution.py:184
  36.5 1.4 %collective-permute-start.10 = (bf16[64,1024]{1,0:T(8,128)(2,1)S(1)}, bf16[64,1024]{1,0:T(8,128)(2,1)S(1)}, u32[]{:S(2)}, u32[]{:S(2)}) collective-permute-start(bf16[64,1024]{1,0:T(8,128)(2,1)S(1)} %pad_maximum_fusion.w_ref), channel_id=1, source_target_pairs={{0,4},{4,0},{8,12},{12,8},{16,20},{20,16},{24,28},{28,24},{1,5},{5... | collective-permute-start | bytes 393224 | tf_op jit(solution)/shard_map/ppermute | solution.py:184
  36.6 5.6 %copy-start.2 = (bf16[128,256]{1,0:T(8,128)(2,1)S(1)}, bf16[128,256]{1,0:T(8,128)(2,1)}, u32[]{:S(2)}) copy-start(bf16[128,256]{1,0:T(8,128)(2,1)} %w_feat_ref.1) | copy-start | bytes 196612
  37.4 8.8 %copy-start.1 = (bf16[512,128]{1,0:T(8,128)(2,1)S(1)}, bf16[512,128]{1,0:T(8,128)(2,1)}, u32[]{:S(2)}) copy-start(bf16[512,128]{1,0:T(8,128)(2,1)} %features_ref.3) | copy-start | bytes 393220
  37.5 8.8 %copy-start.3 = (bf16[256,128]{1,0:T(8,128)(2,1)S(1)}, bf16[256,128]{1,0:T(8,128)(2,1)}, u32[]{:S(2)}) copy-start(bf16[256,128]{1,0:T(8,128)(2,1)} %w_out_ref.1) | copy-start | bytes 196612
  37.5 8.8 %copy-start.4 = (bf16[64,256]{1,0:T(8,128)(2,1)S(1)}, bf16[64,256]{1,0:T(8,128)(2,1)}, u32[]{:S(2)}) copy-start(bf16[64,256]{1,0:T(8,128)(2,1)} %w_pot_ref.1) | copy-start | bytes 98308
  38.6 4.3 %collective-permute-start.11 = (bf16[64,512]{1,0:T(8,128)(2,1)S(1)}, bf16[64,512]{1,0:T(8,128)(2,1)S(1)}, u32[]{:S(2)}, u32[]{:S(2)}) collective-permute-start(bf16[64,512]{1,0:T(8,128)(2,1)S(1)} %get-tuple-element.46), channel_id=1, source_target_pairs={{0,1},{1,0},{2,3},{3,2},{4,5},{5,4},{6,7},{7,6},{8,9},{9,8},{10,11... | collective-permute-start | bytes 196616 | tf_op jit(solution)/shard_map/ppermute | solution.py:184
  39.6 4.3 %collective-permute-start.12 = (bf16[64,512]{1,0:T(8,128)(2,1)S(1)}, bf16[64,512]{1,0:T(8,128)(2,1)S(1)}, u32[]{:S(2)}, u32[]{:S(2)}) collective-permute-start(bf16[64,512]{1,0:T(8,128)(2,1)S(1)} %get-tuple-element.47), channel_id=1, source_target_pairs={{0,2},{1,3},{2,0},{3,1},{4,6},{5,7},{6,4},{7,5},{8,10},{9,11},{10,... | collective-permute-start | bytes 196616 | tf_op jit(solution)/shard_map/ppermute | solution.py:184
  41.1 5.2 %collective-permute-start.13 = (bf16[64,512]{1,0:T(8,128)(2,1)S(1)}, bf16[64,512]{1,0:T(8,128)(2,1)S(1)}, u32[]{:S(2)}, u32[]{:S(2)}) collective-permute-start(bf16[64,512]{1,0:T(8,128)(2,1)S(1)} %get-tuple-element.48), channel_id=1, source_target_pairs={{0,3},{1,2},{2,1},{3,0},{4,7},{5,6},{6,5},{7,4},{8,11},{9,10},{10,... | collective-permute-start | bytes 196616 | tf_op jit(solution)/shard_map/ppermute | solution.py:184

commit v2 on v1

v2 whole, which is shorter than its diff:
```python
import functools
import math

import jax
import jax.numpy as jnp
import numpy as np
from jax import lax
from jax.experimental import pallas as pl
from jax.experimental.pallas import tpu as pltpu
from jax.sharding import PartitionSpec as P

EPS = 1e-06
F32 = jnp.float32
BF16 = jnp.bfloat16
VMEM = pl.BlockSpec(memory_space=pltpu.VMEM)
POINT_ROWS = 16
CORES = 2
TILE = 128
PIECES = 2


def fit(values, degree, count=4000):
    u = (np.cos(np.pi * (np.arange(count) + 0.5) / count) + 1) / 8
    cheb = np.polynomial.chebyshev.Chebyshev.fit(u, values(np.sqrt(u)), degree, domain=[0, 0.25])
    return [float(c) for c in cheb.convert(kind=np.polynomial.Polynomial).coef]


HALF_SIN = fit(lambda r: math.sqrt(2) * np.sin(np.pi * r) / r, 3)
HALF_COS = fit(lambda r: math.sqrt(2) * np.cos(np.pi * r), 3)


def horner(coefs, u):
    total = coefs[-1]
    for c in coefs[-2::-1]:
        total = total * u + c
    return total


def phase_rows(n, x):
    turns = jnp.dot(n, x, preferred_element_type=F32)
    r = turns - jnp.round(turns)
    u = r * r
    s = horner(HALF_SIN, u) * r
    c = horner(HALF_COS, u)
    return jnp.concatenate([1.0 - s * s, s * c], axis=0).astype(BF16)


def nt(a, b):
    return lax.dot_general(a, b, (((1,), (1,)), ((), ())), preferred_element_type=F32)


def tn(a, b):
    return lax.dot_general(a, b, (((0,), (0,)), ((), ())), preferred_element_type=F32)


def triple_rows(values, width):
    row = lax.broadcasted_iota(jnp.int32, (POINT_ROWS, width), 0)
    part = row % 3
    picked = jnp.where(part == 0, values[0:1], jnp.where(part == 1, values[1:2], values[2:3]))
    return row, picked


def fetch_kernel(
    features_ref, species_ref, coords_ref, waves_ref, green_ref, embed_ref, w_charge_ref,
    hidden_ref, mixed_ref, message_ref, waves_out, green_out,
    species_v, coords_v, embed_v, w_charge_v, sems,
):
    pairs = (
        (features_ref, hidden_ref), (embed_ref, embed_v), (species_ref, species_v),
        (w_charge_ref, w_charge_v), (coords_ref, coords_v), (waves_ref, waves_out), (green_ref, green_out),
    )
    copies = [pltpu.make_async_copy(a, b, sems.at[i]) for i, (a, b) in enumerate(pairs)]
    for copy in copies:
        copy.start()
    for copy in copies:
        copy.wait()
    rows = hidden_ref.shape[0]
    q = w_charge_v.shape[0]
    hidden = hidden_ref[...].astype(F32)
    scale = lax.rsqrt(jnp.mean(hidden * hidden, axis=1, keepdims=True) + EPS)
    kinds = embed_v.shape[0]
    onehot = (
        lax.broadcasted_iota(jnp.int32, (kinds, rows), 0) == species_v[...]
    ).astype(F32).astype(BF16)
    mixed = (hidden * scale + tn(onehot, embed_v[...])).astype(BF16)
    mixed_ref[...] = mixed
    message_ref[0:q, :] = nt(w_charge_v[...], mixed).astype(BF16)
    row, point = triple_rows(coords_v[...], rows)
    high = point.astype(BF16).astype(F32)
    middle = (point - high).astype(BF16).astype(F32)
    low = point - high - middle
    parts = jnp.where(row < 3, high, jnp.where(row < 6, middle, jnp.where(row < 9, low, 0.0)))
    message_ref[q:, :] = parts.astype(BF16)


def own_kernel(
    waves_ref, green_ref, message_ref,
    n_ref, g_ref, p_own_ref, p_other_ref, s_own_ref, s_other_ref,
):
    width = waves_ref.shape[1]
    half = width // CORES
    q = message_ref.shape[0] - POINT_ROWS
    core = lax.axis_index("atom") % CORES
    row, index = triple_rows(waves_ref[...].astype(F32), width)
    index = jnp.where(row < 9, index, 0.0)
    first, second = index[:, :half], index[:, half:]
    n_ref[0:half, :] = jnp.where(core == 0, first, second).T.astype(BF16)
    n_ref[half:, :] = jnp.where(core == 0, second, first).T.astype(BF16)
    green = jnp.where(core == 0, green_ref[:, :half], green_ref[:, half:])
    tile = min(TILE, half)
    for c in range(half // tile):
        g = green[:, c * tile : (c + 1) * tile]
        g_ref[:, 2 * c * tile : 2 * (c + 1) * tile] = jnp.concatenate([g, g], axis=1)
    x = message_ref[q:, :]
    charges = message_ref[0:q, :]
    for h, (p_ref, s_ref) in enumerate(((p_own_ref, s_own_ref), (p_other_ref, s_other_ref))):
        for c in range(half // tile):
            n = n_ref[h * half + c * tile : h * half + (c + 1) * tile, :]
            rows = phase_rows(n, x)
            p_ref[2 * c * tile : 2 * (c + 1) * tile, :] = rows
            s_ref[:, 2 * c * tile : 2 * (c + 1) * tile] = nt(charges, rows)


def rest_kernel(start, span, s_start, count, *refs):
    n_ref, s_in_ref = refs[0], refs[1]
    messages = refs[2 : 2 + count]
    p_ref, s_ref = refs[2 + count :]
    q = messages[0].shape[0] - POINT_ROWS
    atoms = messages[0].shape[1]
    tile = min(TILE, span)
    for c in range(span // tile):
        n = n_ref[start + c * tile : start + (c + 1) * tile, :]
        lo, hi = 2 * c * tile, 2 * (c + 1) * tile
        total = s_in_ref[:, s_start + lo : s_start + hi]
        for b, message_ref in enumerate(messages):
            rows = phase_rows(n, message_ref[q:, :])
            p_ref[lo:hi, b * atoms : (b + 1) * atoms] = rows
            total = total + nt(message_ref[0:q, :], rows)
        s_ref[:, lo:hi] = total.astype(s_ref.dtype)


def join_kernel(offset, mine_ref, got_ref, sum_ref, send_ref):
    width = mine_ref.shape[1]
    total = mine_ref[...] + got_ref[:, offset : offset + width].astype(F32)
    sum_ref[...] = total
    send_ref[...] = total.astype(BF16)


def weight_kernel(count, *refs):
    g_ref, out_ref = refs[0], refs[-1]
    at = 0
    for i in range(count):
        mine_ref, got_ref = refs[1 + 2 * i : 3 + 2 * i]
        width = mine_ref.shape[1]
        total = mine_ref[...] + got_ref[...].astype(F32)
        out_ref[:, at : at + width] = (total * g_ref[:, at : at + width]).astype(BF16)
        at += width


def first_half_kernel(pieces, w_ref, p0_ref, *refs):
    own_ref, rest_ref = refs[pieces:]
    own_ref[...] = jnp.dot(w_ref[...], p0_ref[...], preferred_element_type=F32)
    at, total = 0, None
    for p_ref in refs[:pieces]:
        height = p_ref.shape[0]
        part = jnp.dot(w_ref[:, at : at + height], p_ref[...], preferred_element_type=F32)
        total = part if total is None else total + part
        at += height
    rest_ref[...] = total


def send_half_kernel(w_ref, p_ref, rest_ref, *send_refs):
    atoms = send_refs[0].shape[1]
    for b, ref in enumerate(send_refs):
        part = jnp.dot(w_ref[...], p_ref[:, b * atoms : (b + 1) * atoms], preferred_element_type=F32)
        ref[...] = (rest_ref[:, b * atoms : (b + 1) * atoms] + part).astype(BF16)


def keep_half_kernel(w_ref, p0_ref, own_ref, mixed_ref, w_feat_ref, total_ref, pre_ref):
    total_ref[...] = own_ref[...] + jnp.dot(w_ref[...], p0_ref[...], preferred_element_type=F32)
    pre_ref[...] = jnp.dot(mixed_ref[...], w_feat_ref[...], preferred_element_type=F32)


def last_kernel(features_ref, total_ref, pre_ref, w_pot_ref, w_out_ref, *refs):
    out_ref = refs[-1]
    potential = total_ref[...]
    for ref in refs[:-1]:
        potential = potential + ref[...].astype(F32)
    pre = pre_ref[...] + tn(potential.astype(BF16), w_pot_ref[...])
    activation = (pre / (1.0 + jnp.exp(-pre))).astype(BF16)
    out = features_ref[...].astype(F32) + jnp.dot(activation, w_out_ref[...], preferred_element_type=F32)
    out_ref[...] = out.astype(BF16)


def call(kernel, outs, *args, scratch=(), flops=0, space=pltpu.VMEM):
    size = sum(math.prod(a.shape) * a.dtype.itemsize for a in (*args, *outs))
    limit = min(max(4 * size, 16 << 20), 56 << 20)
    if space == pltpu.HBM:
        args = [pltpu.with_memory_space_constraint(a, pltpu.HBM) for a in args]
    return pl.pallas_call(
        kernel,
        out_shape=outs,
        in_specs=[pl.BlockSpec(memory_space=space)] * len(args),
        out_specs=[VMEM] * len(outs),
        scratch_shapes=list(scratch),
        compiler_params=pltpu.CompilerParams(vmem_limit_bytes=limit),
        cost_estimate=pl.CostEstimate(flops=flops, bytes_accessed=size, transcendentals=0),
    )(*args)


def swap(value, axis, bit):
    count = lax.axis_size(axis)
    return lax.ppermute(value, axis, [(i, i ^ bit) for i in range(count)])


def shards(features, species, coords, wave_index, green, embed, w_charge, w_feat, w_pot, w_out):
    array = jax.ShapeDtypeStruct
    atoms = features.shape[0]
    q = w_charge.shape[1]
    hidden = w_feat.shape[1]
    waves = wave_index.shape[1]
    wcount = lax.axis_size("wave")
    acount = lax.axis_size("atom")
    zcount = acount // CORES
    half_rows = 2 * (waves // CORES)
    rest = (wcount - 1) * atoms

    half = waves // CORES
    tile = min(TILE, half)
    pieces = PIECES if (half // tile) % PIECES == 0 else 1
    span = half // pieces

    hidden_v, mixed, message, waves_v, green_v = call(
        fetch_kernel,
        [
            array(features.shape, BF16), array(features.shape, BF16), array((q + POINT_ROWS, atoms), BF16),
            array(wave_index.shape, jnp.int32), array((1, waves), F32),
        ],
        features, species.reshape(1, atoms), coords, wave_index, green.reshape(1, waves), embed, w_charge.T,
        scratch=[
            pltpu.VMEM((1, atoms), jnp.int32), pltpu.VMEM(coords.shape, F32),
            pltpu.VMEM(embed.shape, BF16), pltpu.VMEM((q, features.shape[1]), BF16),
            pltpu.SemaphoreType.DMA((7,)),
        ],
        space=pltpu.HBM,
    )
    messages = [swap(message, "wave", b) for b in range(1, wcount)]
    n, g, p_own0, p_other0, s_own0, s_other0 = call(
        own_kernel,
        [
            array((waves, POINT_ROWS), BF16),
            array((1, half_rows), F32),
            array((half_rows, atoms), BF16),
            array((half_rows, atoms), BF16),
            array((q, half_rows), F32),
            array((q, half_rows), F32),
        ],
        waves_v, green_v, message,
        flops=4 * half_rows * atoms * q,
    )

    def rest_call(start, size, s_start, n, s_in, dtype):
        return call(
            functools.partial(rest_kernel, start, size, s_start, wcount - 1),
            [array((2 * size, rest), BF16), array((q, 2 * size), dtype)],
            n, s_in, *messages,
            flops=4 * size * rest * q,
        )

    def join(mine, got, offset=0):
        shape = mine.shape
        return call(functools.partial(join_kernel, offset), [array(shape, F32), array(shape, BF16)], mine, got)

    p_other, s_other = rest_call(half, half, 0, n, s_other0, BF16)
    got = swap(s_other, "atom", 1)
    p_own, sums, arrived = [], [], []
    for i in range(pieces):
        p, s = rest_call(i * span, span, 2 * i * span, n, s_own0, F32)
        total, send = join(s, got, 2 * i * span)
        p_own.append(p)
        sums.append(total)
        arrived.append(swap(send, "atom", CORES))
        n, sums[-1] = lax.optimization_barrier((n, sums[-1]))
    bit = 2
    while bit < zcount:
        for i in range(pieces):
            sums[i], send = join(sums[i], arrived[i])
            arrived[i] = swap(send, "atom", CORES * bit)
        bit *= 2
    (w_own,) = call(
        functools.partial(weight_kernel, pieces), [array((q, half_rows), BF16)],
        g, *[value for pair in zip(sums, arrived) for value in pair],
    )
    w_other = swap(w_own, "atom", 1)
    own_a, rest_a = call(
        functools.partial(first_half_kernel, pieces),
        [array((q, atoms), F32), array((q, rest), F32)],
        w_own, p_own0, *p_own,
        flops=2 * half_rows * (rest + atoms) * q,
    )
    sends = call(
        send_half_kernel, [array((q, atoms), BF16)] * (wcount - 1), w_other, p_other, rest_a,
        flops=2 * half_rows * rest * q,
    )
    parts = [swap(value, "wave", b + 1) for b, value in enumerate(sends)]
    total, pre = call(
        keep_half_kernel,
        [array((q, atoms), F32), array((atoms, hidden), F32)],
        w_other, p_other0, own_a, mixed, w_feat,
        flops=2 * half_rows * atoms * q,
    )
    (out,) = call(
        last_kernel, [array(features.shape, BF16)],
        hidden_v, total, pre, w_pot, w_out, *parts,
    )
    return out


def solution(mesh):
    placed = (
        P(("atom", "wave"), None),
        P(("atom", "wave")),
        P(None, ("atom", "wave")),
        P(None, "wave"),
        P("wave"),
        P(),
        P(),
        P(),
        P(),
        P(),
    )
    return jax.shard_map(
        shards, mesh=mesh, in_specs=placed, out_specs=P(("atom", "wave"), None), check_vma=False
    )
```

time: 47.9 us -> 39.9 us (0.83)
  local copies, waits for them, and re-layouts: 5.22 us -> 0.01 us
  waiting for transfers between devices: 12.6 us -> 9.71 us
  Pallas kernels: 12.2 us -> 13.5 us
  starting transfers between devices: 17.2 us -> 16.4 us
    unnamed x21 -> x6, local copies, waits for them, and re-layouts: 5.22 us -> 0.01 us
    ppermute x14 -> x12, waiting for transfers between devices: 12.6 us -> 9.71 us  [swap(): return lax.ppermute(value, axis, [(i, i ^ bit) for i in range(count)])]
    pallas_call x10 -> x14, Pallas kernels: 12.2 us -> 13.5 us  [call(): pl.pallas_call(kernel, out_shape=outs, in_specs=[pl.BlockSpec(memory_spac...]
    ppermute x14 -> x12, starting transfers between devices: 17.2 us -> 16.4 us  [swap(): return lax.ppermute(value, axis, [(i, i ^ bit) for i in range(count)])]
  transfers between devices with their start and end apart: 14 -> 12, of which waited for: 10 -> 10; matrix products, arithmetic and copies ran while one was open for 0% -> 0% of each run, Pallas kernels for 15% -> 18%
where the time goes in v2:
time: 39.9 us; the launch traced here: 39.7 us
  starting transfers between devices  16.4 us (41%)
  Pallas kernels  13.5 us (34%)
  waiting for transfers between devices  9.71 us (24%)
    ppermute x12, starting transfers between devices, swap(): return lax.ppermute(value, axis, [(i, i ^ bit) for i in range(count)])  16.4 us
    pallas_call x14, Pallas kernels, call(): pl.pallas_call(kernel, out_shape=outs, in_specs=[pl.BlockSpec(memory_spac...  13.5 us
    ppermute x12, waiting for transfers between devices, swap(): return lax.ppermute(value, axis, [(i, i ^ bit) for i in range(count)])  9.71 us
  transfers between devices with their start and end apart: 12, of which 10 were waited for; matrix products, arithmetic and copies ran while one was open for 0% of the time, Pallas kernels for 18%

profile of v2, /device:TPU:0, one launch (start us, length us, event | category | flops | bytes accessed | tf_op | source)
XLA Modules:
  0.0 39.7 jit_solution(16793209863262816557)
XLA Ops:
  0.0 1.4 %shard_map.100 = (bf16[512,128]{1,0:T(8,128)(2,1)S(1)}, bf16[512,128]{1,0:T(8,128)(2,1)S(1)}, bf16[80,512]{1,0:T(8,128)(2,1)S(1)}, s32[3,1024]{1,0:T(4,128)S(1)}, f32[1,1024]{1,0:T(1,128)S(1)}) custom-call(bf16[512,128]{1,0:T(8,128)(2,1)} %features_ref.1, s32[1,512]{1,0:T(1,128)} %bitcast.5, f32[3,512]{1,0:T(4,128)} %coords_ref.1, s32[3,1024]{1,0:T(4,128)} %waves_ref.1, ...), custom_call_target="tpu_custom_call" | custom-call | bytes 536576 | tf_op jit(solution)/shard_map/pallas_call | solution.py:200
  1.4 4.0 %collective-permute-start.2 = (bf16[80,512]{1,0:T(8,128)(2,1)S(1)}, bf16[80,512]{1,0:T(8,128)(2,1)S(1)}, u32[]{:S(2)}, u32[]{:S(2)}) collective-permute-start(bf16[80,512]{1,0:T(8,128)(2,1)S(1)} %get-tuple-element.43.message_ref), channel_id=1, source_target_pairs={{0,3},{1,2},{2,1},{3,0},{4,7},{5,6},{6,5},{7,4},{8,11},{9,10},{10,... | collective-permute-start | bytes 245768 | tf_op jit(solution)/shard_map/ppermute | solution.py:213
  5.3 0.5 %collective-permute-start.1 = (bf16[80,512]{1,0:T(8,128)(2,1)S(1)}, bf16[80,512]{1,0:T(8,128)(2,1)S(1)}, u32[]{:S(2)}, u32[]{:S(2)}) collective-permute-start(bf16[80,512]{1,0:T(8,128)(2,1)S(1)} %get-tuple-element.43.message_ref), channel_id=1, source_target_pairs={{0,2},{1,3},{2,0},{3,1},{4,6},{5,7},{6,4},{7,5},{8,10},{9,11},{10,... | collective-permute-start | bytes 245768 | tf_op jit(solution)/shard_map/ppermute | solution.py:213
  5.8 0.1 collective-permute-start
  6.0 2.5 %shard_map.101 = (bf16[1024,16]{1,0:T(8,128)(2,1)S(1)}, f32[1,1024]{1,0:T(1,128)S(1)}, bf16[1024,512]{1,0:T(8,128)(2,1)S(1)}, bf16[1024,512]{1,0:T(8,128)(2,1)S(...) custom-call(s32[3,1024]{1,0:T(4,128)S(1)} %get-tuple-element.41.waves_ref, ...), custom_call_target="tpu_custom_call" | custom-call | flops 134217728 | bytes 2756608 | tf_op jit(solution)/shard_map/pallas_call | solution.py:200
  8.5 0.0 collective-permute-done.2.refs_4_
  8.5 1.3 %collective-permute-done.1.refs_3_ = bf16[80,512]{1,0:T(8,128)(2,1)S(1)} collective-permute-done((bf16[80,512]{1,0:T(8,128)(2,1)S(1)}, bf16[80,512]{1,0:T(8,128)(2,1)S(1)}, u32[]{:S(2)}, u32[]{:S(2)}) %collective-permute-start.1) | collective-permute-done | bytes 81952 | tf_op jit(solution)/shard_map/ppermute | solution.py:213
  9.8 0.5 %collective-permute-done.refs_2_ = bf16[80,512]{1,0:T(8,128)(2,1)S(1)} collective-permute-done((bf16[80,512]{1,0:T(8,128)(2,1)S(1)}, bf16[80,512]{1,0:T(8,128)(2,1)S(1)}, u32[]{:S(2)}, u32[]{:S(2)}) %collective-permute-start) | collective-permute-done | bytes 81952 | tf_op jit(solution)/shard_map/ppermute | solution.py:213
  10.3 3.1 %shard_map.103 = (bf16[1024,1536]{1,0:T(8,128)(2,1)S(1)}, bf16[64,1024]{1,0:T(8,128)(2,1)S(1)}) custom-call(bf16[1024,16]{1,0:T(8,128)(2,1)S(1)} %get-tuple-element.55.refs_0_, f32[64,1024]{1,0:T(8,128)S(1)} %get-tuple-element.48.refs_1_, bf16[80,512]{1,0:T(8,128)(2,1)S(1)} %collective-permute-done.refs_2_, ...), custom_call_target="tpu_custom_call" | custom-call | flops 201326592 | bytes 3817472 | tf_op jit(solution)/shard_map/pallas_call | solution.py:200
  13.4 0.1 collective-permute-start.3
  13.5 1.7 %shard_map.102 = (bf16[512,1536]{1,0:T(8,128)(2,1)S(1)}, f32[64,512]{1,0:T(8,128)S(1)}) custom-call(bf16[1024,16]{1,0:T(8,128)(2,1)S(1)} %get-tuple-element.55.refs_0_, f32[64,1024]{1,0:T(8,128)S(1)} %get-tuple-element.46.refs_1_, bf16[80,512]{1,0:T(8,128)(2,1)S(1)} %collective-permute-done.refs_2_, bf16[80,512]{1,0:T(8,128)(2,1)S(1)} %collective-permute-done.1.refs_3_, ...), custom_call_target="tpu_custom_call" | custom-call | flops 100663296 | bytes 2244608 | tf_op jit(solution)/shard_map/pallas_call | solution.py:200
  15.2 0.0 collective-permute-done.3.got_ref
  15.2 1.6 %collective-permute-start.4 = (bf16[64,512]{1,0:T(8,128)(2,1)S(1)}, bf16[64,512]{1,0:T(8,128)(2,1)S(1)}, u32[]{:S(2)}, u32[]{:S(2)}) collective-permute-start(bf16[64,512]{1,0:T(8,128)(2,1)S(1)} %get-tuple-element.52), channel_id=1, source_target_pairs={{0,8},{4,12},{8,0},{12,4},{16,24},{20,28},{24,16},{28,20},{1,9},{5... | collective-permute-start | bytes 196616 | tf_op jit(solution)/shard_map/ppermute | solution.py:213
  16.9 1.7 %shard_map.106 = (bf16[512,1536]{1,0:T(8,128)(2,1)S(1)}, f32[64,512]{1,0:T(8,128)S(1)}) custom-call(bf16[1024,16]{1,0:T(8,128)(2,1)S(1)} %get-tuple-element.55.refs_0_, f32[64,1024]{1,0:T(8,128)S(1)} %get-tuple-element.46.refs_1_, bf16[80,512]{1,0:T(8,128)(2,1)S(1)} %collective-permute-done.refs_2_, bf16[80,512]{1,0:T(8,128)(2,1)S(1)} %collective-permute-done.1.refs_3_, ...), custom_call_target="tpu_custom_call" | custom-call | flops 100663296 | bytes 2244608 | tf_op jit(solution)/shard_map/pallas_call | solution.py:200
  18.6 0.5 %collective-permute-start.6 = (bf16[64,512]{1,0:T(8,128)(2,1)S(1)}, bf16[64,512]{1,0:T(8,128)(2,1)S(1)}, u32[]{:S(2)}, u32[]{:S(2)}) collective-permute-start(bf16[64,512]{1,0:T(8,128)(2,1)S(1)} %get-tuple-element.59), channel_id=1, source_target_pairs={{0,8},{4,12},{8,0},{12,4},{16,24},{20,28},{24,16},{28,20},{1,9},{5... | collective-permute-start | bytes 196616 | tf_op jit(solution)/shard_map/ppermute | solution.py:213
  19.1 0.7 %collective-permute-done.4.got_ref = bf16[64,512]{1,0:T(8,128)(2,1)S(1)} collective-permute-done((bf16[64,512]{1,0:T(8,128)(2,1)S(1)}, bf16[64,512]{1,0:T(8,128)(2,1)S(1)}, u32[]{:S(2)}, u32[]{:S(2)}) %collective-permute-start.4) | collective-permute-done | bytes 65568 | tf_op jit(solution)/shard_map/ppermute | solution.py:213
  19.8 2.7 %collective-permute-start.5 = (bf16[64,512]{1,0:T(8,128)(2,1)S(1)}, bf16[64,512]{1,0:T(8,128)(2,1)S(1)}, u32[]{:S(2)}, u32[]{:S(2)}) collective-permute-start(bf16[64,512]{1,0:T(8,128)(2,1)S(1)} %get-tuple-element.54), channel_id=1, source_target_pairs={{0,16},{4,20},{8,24},{12,28},{16,0},{20,4},{24,8},{28,12},{1,17},{... | collective-permute-start | bytes 196616 | tf_op jit(solution)/shard_map/ppermute | solution.py:213
  22.5 0.5 %collective-permute-done.6.got_ref = bf16[64,512]{1,0:T(8,128)(2,1)S(1)} collective-permute-done((bf16[64,512]{1,0:T(8,128)(2,1)S(1)}, bf16[64,512]{1,0:T(8,128)(2,1)S(1)}, u32[]{:S(2)}, u32[]{:S(2)}) %collective-permute-start.6) | collective-permute-done | bytes 65568 | tf_op jit(solution)/shard_map/ppermute | solution.py:213
  22.9 3.3 %collective-permute-start.7 = (bf16[64,512]{1,0:T(8,128)(2,1)S(1)}, bf16[64,512]{1,0:T(8,128)(2,1)S(1)}, u32[]{:S(2)}, u32[]{:S(2)}) collective-permute-start(bf16[64,512]{1,0:T(8,128)(2,1)S(1)} %get-tuple-element.61), channel_id=1, source_target_pairs={{0,16},{4,20},{8,24},{12,28},{16,0},{20,4},{24,8},{28,12},{1,17},{... | collective-permute-start | bytes 196616 | tf_op jit(solution)/shard_map/ppermute | solution.py:213
  26.2 0.2 collective-permute-done.5.refs_2_
  26.4 2.8 %collective-permute-done.7.refs_4_ = bf16[64,512]{1,0:T(8,128)(2,1)S(1)} collective-permute-done((bf16[64,512]{1,0:T(8,128)(2,1)S(1)}, bf16[64,512]{1,0:T(8,128)(2,1)S(1)}, u32[]{:S(2)}, u32[]{:S(2)}) %collective-permute-start.7) | collective-permute-done | bytes 65568 | tf_op jit(solution)/shard_map/ppermute | solution.py:213
  29.2 0.1 collective-permute-start.8
  29.3 0.8 %shard_map.110 = (f32[64,512]{1,0:T(8,128)S(1)}, f32[64,1536]{1,0:T(8,128)S(1)}) custom-call(bf16[64,1024]{1,0:T(8,128)(2,1)S(1)} %shard_map.109.w_ref, bf16[1024,512]{1,0:T(8,128)(2,1)S(1)} %get-tuple-element.63.p0_ref, bf16[512,1536]{1,0:T(8,128)(2,1)S(1)} %get-tuple-element.64.refs_0_, bf16[512,1536]{1,0:T(8,128)(2,1)S(1)} %get-tuple-element.65.refs_1_), custom_call_target="tpu_custom_call" | custom-call | flops 268435456 | bytes 4849664 | tf_op jit(solution)/shard_map/pallas_call | solution.py:200
  30.1 0.5 %collective-permute-done.8.w_ref = bf16[64,1024]{1,0:T(8,128)(2,1)S(1)} collective-permute-done((bf16[64,1024]{1,0:T(8,128)(2,1)S(1)}, bf16[64,1024]{1,0:T(8,128)(2,1)S(1)}, u32[]{:S(2)}, u32[]{:S(2)}) %collective-permute-start.8) | collective-permute-done | bytes 131104 | tf_op jit(solution)/shard_map/ppermute | solution.py:213
  30.6 0.0 copy-start
  30.6 0.0 copy-start.1
  30.6 0.0 copy-start.2
  30.6 0.7 %shard_map.112 = (bf16[64,512]{1,0:T(8,128)(2,1)S(1)}, bf16[64,512]{1,0:T(8,128)(2,1)S(1)}, bf16[64,512]{1,0:T(8,128)(2,1)S(1)}) custom-call(bf16[64,1024]{1,0:T(8,128)(2,1)S(1)} %collective-permute-done.8.w_ref, bf16[1024,1536]{1,0:T(8,128)(2,1)S(1)} %get-tuple-element.70.p_ref, f32[64,1536]{1,0:T(8,128)S(1)} %get-tuple-element.71.rest_ref), custom_call_target="tpu_custom_call" | custom-call | flops 201326592 | bytes 3866624 | tf_op jit(solution)/shard_map/pallas_call | solution.py:200
  31.3 1.1 %collective-permute-start.9 = (bf16[64,512]{1,0:T(8,128)(2,1)S(1)}, bf16[64,512]{1,0:T(8,128)(2,1)S(1)}, u32[]{:S(2)}, u32[]{:S(2)}) collective-permute-start(bf16[64,512]{1,0:T(8,128)(2,1)S(1)} %get-tuple-element.72), channel_id=1, source_target_pairs={{0,1},{1,0},{2,3},{3,2},{4,5},{5,4},{6,7},{7,6},{8,9},{9,8},{10,11... | collective-permute-start | bytes 196616 | tf_op jit(solution)/shard_map/ppermute | solution.py:213
  32.4 1.1 %collective-permute-start.10 = (bf16[64,512]{1,0:T(8,128)(2,1)S(1)}, bf16[64,512]{1,0:T(8,128)(2,1)S(1)}, u32[]{:S(2)}, u32[]{:S(2)}) collective-permute-start(bf16[64,512]{1,0:T(8,128)(2,1)S(1)} %get-tuple-element.73), channel_id=1, source_target_pairs={{0,2},{1,3},{2,0},{3,1},{4,6},{5,7},{6,4},{7,5},{8,10},{9,11},{10,... | collective-permute-start | bytes 196616 | tf_op jit(solution)/shard_map/ppermute | solution.py:213
  33.4 1.4 %collective-permute-start.11 = (bf16[64,512]{1,0:T(8,128)(2,1)S(1)}, bf16[64,512]{1,0:T(8,128)(2,1)S(1)}, u32[]{:S(2)}, u32[]{:S(2)}) collective-permute-start(bf16[64,512]{1,0:T(8,128)(2,1)S(1)} %get-tuple-element.74), channel_id=1, source_target_pairs={{0,3},{1,2},{2,1},{3,0},{4,7},{5,6},{6,5},{7,4},{8,11},{9,10},{10,... | collective-permute-start | bytes 196616 | tf_op jit(solution)/shard_map/ppermute | solution.py:213
  34.9 0.0 copy-done
  34.9 0.4 shard_map.111
  35.2 0.4 collective-permute-done.9.refs_0_
  35.6 1.2 %collective-permute-done.10.refs_1_ = bf16[64,512]{1,0:T(8,128)(2,1)S(1)} collective-permute-done((bf16[64,512]{1,0:T(8,128)(2,1)S(1)}, bf16[64,512]{1,0:T(8,128)(2,1)S(1)}, u32[]{:S(2)}, u32[]{:S(2)}) %collective-permute-start.10) | collective-permute-done | bytes 65568 | tf_op jit(solution)/shard_map/ppermute | solution.py:213
  36.8 1.8 %collective-permute-done.11.refs_2_ = bf16[64,512]{1,0:T(8,128)(2,1)S(1)} collective-permute-done((bf16[64,512]{1,0:T(8,128)(2,1)S(1)}, bf16[64,512]{1,0:T(8,128)(2,1)S(1)}, u32[]{:S(2)}, u32[]{:S(2)}) %collective-permute-start.11) | collective-permute-done | bytes 65568 | tf_op jit(solution)/shard_map/ppermute | solution.py:213
  38.6 0.0 copy-done.1
  38.6 0.0 copy-done.2
  38.6 1.1 %shard_map.113 = bf16[512,128]{1,0:T(8,128)(2,1)} custom-call(bf16[512,128]{1,0:T(8,128)(2,1)S(1)} %get-tuple-element.40.features_ref, f32[64,512]{1,0:T(8,128)S(1)} %get-tuple-element.68.total_ref, f32[512,256]{1,0:T(8,128)S(1)} %get-tuple-element.69.pre_ref, bf16[64,256]{1,0:T(8,128)(2,1)S(1)} %copy-done.2, bf16[256,128]{1,0:T(8,128)(2,1)S(1)} %copy-done.1, ...), custom_call_target="tpu_custom_call" | custom-call | bytes 1212416 | tf_op jit(solution)/shard_map/pallas_call | solution.py:200
  (5 shorter events, 0.1 us)
Async XLA Ops:
  1.4 7.1 %collective-permute-start.2 = (bf16[80,512]{1,0:T(8,128)(2,1)S(1)}, bf16[80,512]{1,0:T(8,128)(2,1)S(1)}, u32[]{:S(2)}, u32[]{:S(2)}) collective-permute-start(bf16[80,512]{1,0:T(8,128)(2,1)S(1)} %get-tuple-element.43.message_ref), channel_id=1, source_target_pairs={{0,3},{1,2},{2,1},{3,0},{4,7},{5,6},{6,5},{7,4},{8,11},{9,10},{10,... | collective-permute-start | bytes 245768 | tf_op jit(solution)/shard_map/ppermute | solution.py:213
  5.3 4.4 %collective-permute-start.1 = (bf16[80,512]{1,0:T(8,128)(2,1)S(1)}, bf16[80,512]{1,0:T(8,128)(2,1)S(1)}, u32[]{:S(2)}, u32[]{:S(2)}) collective-permute-start(bf16[80,512]{1,0:T(8,128)(2,1)S(1)} %get-tuple-element.43.message_ref), channel_id=1, source_target_pairs={{0,2},{1,3},{2,0},{3,1},{4,6},{5,7},{6,4},{7,5},{8,10},{9,11},{10,... | collective-permute-start | bytes 245768 | tf_op jit(solution)/shard_map/ppermute | solution.py:213
  5.8 4.4 %collective-permute-start = (bf16[80,512]{1,0:T(8,128)(2,1)S(1)}, bf16[80,512]{1,0:T(8,128)(2,1)S(1)}, u32[]{:S(2)}, u32[]{:S(2)}) collective-permute-start(bf16[80,512]{1,0:T(8,128)(2,1)S(1)} %get-tuple-element.43.message_ref), channel_id=1, source_target_pairs={{0,1},{1,0},{2,3},{3,2},{4,5},{5,4},{6,7},{7,6},{8,9},{9,8},{10,11... | collective-permute-start | bytes 245768 | tf_op jit(solution)/shard_map/ppermute | solution.py:213
  13.4 1.8 %collective-permute-start.3 = (bf16[64,1024]{1,0:T(8,128)(2,1)S(1)}, bf16[64,1024]{1,0:T(8,128)(2,1)S(1)}, u32[]{:S(2)}, u32[]{:S(2)}) collective-permute-start(bf16[64,1024]{1,0:T(8,128)(2,1)S(1)} %get-tuple-element.49), channel_id=1, source_target_pairs={{0,4},{4,0},{8,12},{12,8},{16,20},{20,16},{24,28},{28,24},{1,5},{5... | collective-permute-start | bytes 393224 | tf_op jit(solution)/shard_map/ppermute | solution.py:213
  15.2 4.6 %collective-permute-start.4 = (bf16[64,512]{1,0:T(8,128)(2,1)S(1)}, bf16[64,512]{1,0:T(8,128)(2,1)S(1)}, u32[]{:S(2)}, u32[]{:S(2)}) collective-permute-start(bf16[64,512]{1,0:T(8,128)(2,1)S(1)} %get-tuple-element.52), channel_id=1, source_target_pairs={{0,8},{4,12},{8,0},{12,4},{16,24},{20,28},{24,16},{28,20},{1,9},{5... | collective-permute-start | bytes 196616 | tf_op jit(solution)/shard_map/ppermute | solution.py:213
  18.6 4.3 %collective-permute-start.6 = (bf16[64,512]{1,0:T(8,128)(2,1)S(1)}, bf16[64,512]{1,0:T(8,128)(2,1)S(1)}, u32[]{:S(2)}, u32[]{:S(2)}) collective-permute-start(bf16[64,512]{1,0:T(8,128)(2,1)S(1)} %get-tuple-element.59), channel_id=1, source_target_pairs={{0,8},{4,12},{8,0},{12,4},{16,24},{20,28},{24,16},{28,20},{1,9},{5... | collective-permute-start | bytes 196616 | tf_op jit(solution)/shard_map/ppermute | solution.py:213
  19.8 6.6 %collective-permute-start.5 = (bf16[64,512]{1,0:T(8,128)(2,1)S(1)}, bf16[64,512]{1,0:T(8,128)(2,1)S(1)}, u32[]{:S(2)}, u32[]{:S(2)}) collective-permute-start(bf16[64,512]{1,0:T(8,128)(2,1)S(1)} %get-tuple-element.54), channel_id=1, source_target_pairs={{0,16},{4,20},{8,24},{12,28},{16,0},{20,4},{24,8},{28,12},{1,17},{... | collective-permute-start | bytes 196616 | tf_op jit(solution)/shard_map/ppermute | solution.py:213
  22.9 6.2 %collective-permute-start.7 = (bf16[64,512]{1,0:T(8,128)(2,1)S(1)}, bf16[64,512]{1,0:T(8,128)(2,1)S(1)}, u32[]{:S(2)}, u32[]{:S(2)}) collective-permute-start(bf16[64,512]{1,0:T(8,128)(2,1)S(1)} %get-tuple-element.61), channel_id=1, source_target_pairs={{0,16},{4,20},{8,24},{12,28},{16,0},{20,4},{24,8},{28,12},{1,17},{... | collective-permute-start | bytes 196616 | tf_op jit(solution)/shard_map/ppermute | solution.py:213
  29.2 1.4 %collective-permute-start.8 = (bf16[64,1024]{1,0:T(8,128)(2,1)S(1)}, bf16[64,1024]{1,0:T(8,128)(2,1)S(1)}, u32[]{:S(2)}, u32[]{:S(2)}) collective-permute-start(bf16[64,1024]{1,0:T(8,128)(2,1)S(1)} %shard_map.109.w_ref), channel_id=1, source_target_pairs={{0,4},{4,0},{8,12},{12,8},{16,20},{20,16},{24,28},{28,24},{1,5},{5... | collective-permute-start | bytes 393224 | tf_op jit(solution)/shard_map/ppermute | solution.py:213
  30.6 4.2 %copy-start = (bf16[128,256]{1,0:T(8,128)(2,1)S(1)}, bf16[128,256]{1,0:T(8,128)(2,1)}, u32[]{:S(2)}) copy-start(bf16[128,256]{1,0:T(8,128)(2,1)} %w_feat_ref.1) | copy-start | bytes 196612
  30.6 8.0 %copy-start.1 = (bf16[256,128]{1,0:T(8,128)(2,1)S(1)}, bf16[256,128]{1,0:T(8,128)(2,1)}, u32[]{:S(2)}) copy-start(bf16[256,128]{1,0:T(8,128)(2,1)} %w_out_ref.1) | copy-start | bytes 196612
  30.6 8.0 %copy-start.2 = (bf16[64,256]{1,0:T(8,128)(2,1)S(1)}, bf16[64,256]{1,0:T(8,128)(2,1)}, u32[]{:S(2)}) copy-start(bf16[64,256]{1,0:T(8,128)(2,1)} %w_pot_ref.1) | copy-start | bytes 98308
  31.3 4.3 %collective-permute-start.9 = (bf16[64,512]{1,0:T(8,128)(2,1)S(1)}, bf16[64,512]{1,0:T(8,128)(2,1)S(1)}, u32[]{:S(2)}, u32[]{:S(2)}) collective-permute-start(bf16[64,512]{1,0:T(8,128)(2,1)S(1)} %get-tuple-element.72), channel_id=1, source_target_pairs={{0,1},{1,0},{2,3},{3,2},{4,5},{5,4},{6,7},{7,6},{8,9},{9,8},{10,11... | collective-permute-start | bytes 196616 | tf_op jit(solution)/shard_map/ppermute | solution.py:213
  32.4 4.5 %collective-permute-start.10 = (bf16[64,512]{1,0:T(8,128)(2,1)S(1)}, bf16[64,512]{1,0:T(8,128)(2,1)S(1)}, u32[]{:S(2)}, u32[]{:S(2)}) collective-permute-start(bf16[64,512]{1,0:T(8,128)(2,1)S(1)} %get-tuple-element.73), channel_id=1, source_target_pairs={{0,2},{1,3},{2,0},{3,1},{4,6},{5,7},{6,4},{7,5},{8,10},{9,11},{10,... | collective-permute-start | bytes 196616 | tf_op jit(solution)/shard_map/ppermute | solution.py:213
  33.4 5.2 %collective-permute-start.11 = (bf16[64,512]{1,0:T(8,128)(2,1)S(1)}, bf16[64,512]{1,0:T(8,128)(2,1)S(1)}, u32[]{:S(2)}, u32[]{:S(2)}) collective-permute-start(bf16[64,512]{1,0:T(8,128)(2,1)S(1)} %get-tuple-element.74), channel_id=1, source_target_pairs={{0,3},{1,2},{2,1},{3,0},{4,7},{5,6},{6,5},{7,4},{8,11},{9,10},{10,... | collective-permute-start | bytes 196616 | tf_op jit(solution)/shard_map/ppermute | solution.py:213

commit v3 on v2

v3 whole, which is shorter than its diff:
```python
import functools
import math

import jax
import jax.numpy as jnp
import numpy as np
from jax import lax
from jax.experimental import pallas as pl
from jax.experimental.pallas import tpu as pltpu
from jax.sharding import PartitionSpec as P

EPS = 1e-06
F32 = jnp.float32
BF16 = jnp.bfloat16
POINT_ROWS = 16
CORES = 2
TILE = 128
MARGIN = 2e-6
PIECES = 2
OUT_PARTS = 4


def half_sine():
    u = (np.cos(np.pi * np.arange(4) / 3) + 1) / 8
    r = np.sqrt(np.maximum(u, 1e-16))
    return [float(c) for c in np.polynomial.polynomial.polyfit(u, math.sqrt(2) * np.sin(np.pi * r) / r, 3)]


HALF_SINE = half_sine()


def phases(turns):
    r = turns - jnp.round(turns)
    u = r * r
    total = HALF_SINE[-1]
    for c in HALF_SINE[-2::-1]:
        total = total * u + c
    s = total * r
    q = s * s
    rest = (2.0 + MARGIN) - q
    return (1.0 - q).astype(BF16), (s * (rest * lax.rsqrt(rest))).astype(BF16)


def put_phases(p_ref, lo, tile, left, n, x):
    cosine, sine = phases(jnp.dot(n, x, preferred_element_type=F32))
    right = left + x.shape[1]
    p_ref[lo : lo + tile, left:right] = cosine
    p_ref[lo + tile : lo + 2 * tile, left:right] = sine


def nt(a, b):
    return lax.dot_general(a, b, (((1,), (1,)), ((), ())), preferred_element_type=F32)


def tn(a, b):
    return lax.dot_general(a, b, (((0,), (0,)), ((), ())), preferred_element_type=F32)


def triple_rows(values, width):
    row = lax.broadcasted_iota(jnp.int32, (POINT_ROWS, width), 0)
    part = row % 3
    picked = jnp.where(part == 0, values[0:1], jnp.where(part == 1, values[1:2], values[2:3]))
    return row, picked


def fetch_kernel(
    features_ref, species_ref, coords_ref, waves_ref, green_ref, embed_ref, w_charge_ref,
    hidden_ref, mixed_ref, message_ref, waves_out, green_out,
    species_v, coords_v, embed_v, w_charge_v, sems,
):
    pairs = (
        (features_ref, hidden_ref), (embed_ref, embed_v), (species_ref, species_v),
        (w_charge_ref, w_charge_v), (coords_ref, coords_v), (waves_ref, waves_out), (green_ref, green_out),
    )
    copies = [pltpu.make_async_copy(a, b, sems.at[i]) for i, (a, b) in enumerate(pairs)]
    for copy in copies:
        copy.start()
    for copy in copies:
        copy.wait()
    rows = hidden_ref.shape[0]
    q = w_charge_v.shape[0]
    hidden = hidden_ref[...].astype(F32)
    scale = lax.rsqrt(jnp.mean(hidden * hidden, axis=1, keepdims=True) + EPS)
    kinds = embed_v.shape[0]
    onehot = (
        lax.broadcasted_iota(jnp.int32, (kinds, rows), 0) == species_v[...]
    ).astype(F32).astype(BF16)
    mixed = (hidden * scale + tn(onehot, embed_v[...])).astype(BF16)
    mixed_ref[...] = mixed
    message_ref[0:q, :] = nt(w_charge_v[...], mixed).astype(BF16)
    row, point = triple_rows(coords_v[...], rows)
    high = point.astype(BF16).astype(F32)
    middle = (point - high).astype(BF16).astype(F32)
    low = point - high - middle
    parts = jnp.where(row < 3, high, jnp.where(row < 6, middle, jnp.where(row < 9, low, 0.0)))
    message_ref[q:, :] = parts.astype(BF16)


def own_kernel(
    pieces, waves_ref, green_ref, message_ref,
    n_ref, g_ref, p_own_ref, p_other_ref, s_own_ref, s_other_ref,
):
    width = waves_ref.shape[1]
    half = width // CORES
    span = half // pieces
    tile = min(TILE, span)
    q = message_ref.shape[0] - POINT_ROWS
    core = lax.axis_index("atom") % CORES
    row, index = triple_rows(waves_ref[...].astype(F32), width)
    index = jnp.where(row < 9, index, 0.0)

    def pick(values, h, i):
        at = i * span
        first, second = values[:, at : at + span], values[:, half + at : half + at + span]
        return jnp.where(core == h, first, second)

    for h in range(CORES):
        for i in range(pieces):
            at = h * half + i * span
            n_ref[at : at + span, :] = pick(index, h, i).T.astype(BF16)
    for i in range(pieces):
        green = pick(green_ref[...], 0, i)
        for c in range(span // tile):
            g = green[:, c * tile : (c + 1) * tile]
            lo = 2 * (i * span + c * tile)
            g_ref[:, lo : lo + 2 * tile] = jnp.concatenate([g, g], axis=1)
    x = message_ref[q:, :]
    for h, (p_ref, s_ref) in enumerate(((p_own_ref, s_own_ref), (p_other_ref, s_other_ref))):
        for c in range(half // tile):
            lo = 2 * c * tile
            put_phases(p_ref, lo, tile, 0, n_ref[h * half + c * tile : h * half + (c + 1) * tile, :], x)
            s_ref[:, lo : lo + 2 * tile] = nt(message_ref[0:q, :], p_ref[lo : lo + 2 * tile, :])


def rest_kernel(start, span, tile, s_start, count, *refs):
    n_ref, s_in_ref = refs[0], refs[1]
    messages = refs[2 : 2 + count]
    p_ref, s_ref, charges = refs[2 + count :]
    q = messages[0].shape[0] - POINT_ROWS
    atoms = messages[0].shape[1]
    for b, message_ref in enumerate(messages):
        charges[:, b * atoms : (b + 1) * atoms] = message_ref[0:q, :]
    for c in range(span // tile):
        n = n_ref[start + c * tile : start + (c + 1) * tile, :]
        lo, hi = 2 * c * tile, 2 * (c + 1) * tile
        for b, message_ref in enumerate(messages):
            put_phases(p_ref, lo, tile, b * atoms, n, message_ref[q:, :])
        total = s_in_ref[:, s_start + lo : s_start + hi] + nt(charges[...], p_ref[lo:hi, :])
        s_ref[:, lo:hi] = total.astype(s_ref.dtype)


def join_kernel(offset, count, *refs):
    outs = refs[1 + count :]
    width = refs[0].shape[1]
    total = refs[0][...]
    for i, ref in enumerate(refs[1 : 1 + count]):
        at = offset if i == 0 else 0
        total = total + ref[:, at : at + width].astype(F32)
    for ref in outs:
        ref[...] = total.astype(ref.dtype)


def weight_kernel(count, *refs):
    g_ref, out_ref = refs[0], refs[-1]
    at = 0
    for i in range(count):
        mine_ref, got_ref = refs[1 + 2 * i : 3 + 2 * i]
        width = mine_ref.shape[1]
        total = mine_ref[...] + got_ref[...].astype(F32)
        out_ref[:, at : at + width] = (total * g_ref[:, at : at + width]).astype(BF16)
        at += width


def potential_kernel(pieces, w_ref, p0_ref, *refs):
    own_ref, rest_ref = refs[pieces:]
    own_ref[...] = jnp.dot(w_ref[...], p0_ref[...], preferred_element_type=F32)
    at, total = 0, None
    for p_ref in refs[:pieces]:
        height = p_ref.shape[0]
        part = jnp.dot(w_ref[:, at : at + height], p_ref[...], preferred_element_type=F32)
        total = part if total is None else total + part
        at += height
    rest_ref[...] = total


def send_kernel(w_ref, p_ref, rest_ref, *send_refs):
    atoms = send_refs[0].shape[1]
    for b, ref in enumerate(send_refs):
        part = jnp.dot(w_ref[...], p_ref[:, b * atoms : (b + 1) * atoms], preferred_element_type=F32)
        ref[...] = (rest_ref[:, b * atoms : (b + 1) * atoms] + part).astype(BF16)


def keep_kernel(w_ref, p0_ref, own_ref, mixed_ref, w_feat_ref, total_ref, pre_ref):
    total_ref[...] = own_ref[...] + jnp.dot(w_ref[...], p0_ref[...], preferred_element_type=F32)
    pre_ref[...] = jnp.dot(mixed_ref[...], w_feat_ref[...], preferred_element_type=F32)


def last_kernel(count, hidden_ref, total_ref, pre_ref, w_pot_ref, w_out_ref, *refs):
    out_ref, out_v, sems = refs[count:]
    atoms = hidden_ref.shape[0]
    step = atoms // OUT_PARTS
    copies = []
    for i in range(OUT_PARTS):
        at = i * step
        potential = total_ref[:, at : at + step]
        for ref in refs[:count]:
            potential = potential + ref[:, at : at + step].astype(F32)
        pre = pre_ref[at : at + step, :] + tn(potential.astype(BF16), w_pot_ref[...])
        activation = (0.5 * pre * (1.0 + jnp.tanh(0.5 * pre))).astype(BF16)
        out = hidden_ref[at : at + step, :].astype(F32) + jnp.dot(
            activation, w_out_ref[...], preferred_element_type=F32
        )
        out_v[at : at + step, :] = out.astype(BF16)
        copy = pltpu.make_async_copy(out_v.at[at : at + step, :], out_ref.at[at : at + step, :], sems.at[i])
        copy.start()
        copies.append(copy)
    for copy in copies:
        copy.wait()


def call(kernel, outs, *args, scratch=(), flops=0, space=pltpu.VMEM, out_space=pltpu.VMEM):
    size = sum(math.prod(a.shape) * a.dtype.itemsize for a in (*args, *outs))
    limit = min(max(4 * size, 16 << 20), 56 << 20)
    if space == pltpu.HBM:
        args = [pltpu.with_memory_space_constraint(a, pltpu.HBM) for a in args]
    return pl.pallas_call(
        kernel,
        out_shape=outs,
        in_specs=[pl.BlockSpec(memory_space=space)] * len(args),
        out_specs=[pl.BlockSpec(memory_space=out_space)] * len(outs),
        scratch_shapes=list(scratch),
        compiler_params=pltpu.CompilerParams(vmem_limit_bytes=limit),
        cost_estimate=pl.CostEstimate(flops=flops, bytes_accessed=size, transcendentals=0),
    )(*args)


def swap(value, axis, bit):
    count = lax.axis_size(axis)
    return lax.ppermute(value, axis, [(i, i ^ bit) for i in range(count)])


def z_swap(value, step):
    count = lax.axis_size("atom")
    steps = (count // CORES).bit_length() - 1
    bits = [CORES << s for s in range(steps)]
    return lax.ppermute(
        value, "atom", [(i, i ^ bits[step if i % CORES == 0 else steps - 1 - step]) for i in range(count)]
    )


def shards(features, species, coords, wave_index, green, embed, w_charge, w_feat, w_pot, w_out):
    array = jax.ShapeDtypeStruct
    atoms = features.shape[0]
    q = w_charge.shape[1]
    hidden = w_feat.shape[1]
    waves = wave_index.shape[1]
    wcount = lax.axis_size("wave")
    acount = lax.axis_size("atom")
    zcount = acount // CORES
    half_rows = 2 * (waves // CORES)
    rest = (wcount - 1) * atoms

    half = waves // CORES
    pieces = PIECES if (half // min(TILE, half)) % PIECES == 0 else 1
    span = half // pieces
    tile = min(TILE, span)

    hidden_v, mixed, message, waves_v, green_v = call(
        fetch_kernel,
        [
            array(features.shape, BF16), array(features.shape, BF16), array((q + POINT_ROWS, atoms), BF16),
            array(wave_index.shape, jnp.int32), array((1, waves), F32),
        ],
        features, species.reshape(1, atoms), coords, wave_index, green.reshape(1, waves), embed, w_charge.T,
        scratch=[
            pltpu.VMEM((1, atoms), jnp.int32), pltpu.VMEM(coords.shape, F32),
            pltpu.VMEM(embed.shape, BF16), pltpu.VMEM((q, features.shape[1]), BF16),
            pltpu.SemaphoreType.DMA((7,)),
        ],
        space=pltpu.HBM,
    )
    messages = [swap(message, "wave", b) for b in range(1, wcount)]
    n, g, p_own0, p_other0, s_own0, s_other0 = call(
        functools.partial(own_kernel, pieces),
        [
            array((waves, POINT_ROWS), BF16),
            array((1, half_rows), F32),
            array((half_rows, atoms), BF16),
            array((half_rows, atoms), BF16),
            array((q, half_rows), F32),
            array((q, half_rows), F32),
        ],
        waves_v, green_v, message,
        flops=4 * half_rows * atoms * q,
    )

    def rest_call(start, size, s_start, n, s_in, dtype):
        return call(
            functools.partial(rest_kernel, start, size, tile, s_start, wcount - 1),
            [array((2 * size, rest), BF16), array((q, 2 * size), dtype)],
            n, s_in, *messages,
            scratch=[pltpu.VMEM((q, rest), BF16)],
            flops=4 * size * rest * q,
        )

    def join(outs, mine, *got, offset=0):
        return call(
            functools.partial(join_kernel, offset, len(got)), [array(mine.shape, dtype) for dtype in outs], mine, *got
        )

    rows = 2 * span
    p_other, s_other = rest_call(half, half, 0, n, s_other0, BF16)
    got = swap(s_other, "atom", 1)
    p_own, sums, arrived = [], [], []
    for i in range(pieces):
        p, total = rest_call(i * span, span, i * rows, n, s_own0, F32)
        p_own.append(p)
        total, send = join([F32, BF16], total, got, offset=i * rows)
        sums.append(total)
        arrived.append(z_swap(send, 0))
        n, sums[-1] = lax.optimization_barrier((n, sums[-1]))
    for step in range(1, zcount.bit_length() - 1):
        for i in range(pieces):
            sums[i], send = join([F32, BF16], sums[i], arrived[i])
            arrived[i] = z_swap(send, step)
    (w_own,) = call(
        functools.partial(weight_kernel, pieces), [array((q, half_rows), BF16)],
        g, *[value for pair in zip(sums, arrived) for value in pair],
    )
    w_other = swap(w_own, "atom", 1)
    own, others = call(
        functools.partial(potential_kernel, pieces), [array((q, atoms), F32), array((q, rest), F32)],
        w_own, p_own0, *p_own,
        flops=2 * half_rows * (rest + atoms) * q,
    )
    sends = call(
        send_kernel, [array((q, atoms), BF16)] * (wcount - 1), w_other, p_other, others,
        flops=2 * half_rows * rest * q,
    )
    order = sorted(range(wcount - 1), key=lambda b: -bin(b + 1).count("1"))
    parts = [swap(sends[b], "wave", b + 1) for b in order]
    total, pre = call(
        keep_kernel,
        [array((q, atoms), F32), array((atoms, hidden), F32)],
        w_other, p_other0, own, mixed, w_feat,
        flops=2 * half_rows * atoms * q,
    )
    (out,) = call(
        functools.partial(last_kernel, wcount - 1), [array(features.shape, BF16)],
        hidden_v, total, pre, w_pot, w_out, *parts,
        scratch=[pltpu.VMEM(features.shape, BF16), pltpu.SemaphoreType.DMA((OUT_PARTS,))],
        out_space=pl.ANY,
    )
    return out


def solution(mesh):
    placed = (
        P(("atom", "wave"), None),
        P(("atom", "wave")),
        P(None, ("atom", "wave")),
        P(None, "wave"),
        P("wave"),
        P(),
        P(),
        P(),
        P(),
        P(),
    )
    return jax.shard_map(
        shards, mesh=mesh, in_specs=placed, out_specs=P(("atom", "wave"), None), check_vma=False
    )
```

time: 39.9 us -> 37.7 us (0.945)
  Pallas kernels: 13.5 us -> 11.7 us
  starting transfers between devices: 16.4 us -> 15.7 us
    ppermute x12 -> x8, starting transfers between devices: 16.4 us -> 8.3 us  [swap(): return lax.ppermute(value, axis, [(i, i ^ bit) for i in range(count)])]
    ppermute x0 -> x4, starting transfers between devices: none -> 7.43 us  [z_swap(): lax.ppermute(value, 'atom', [(i, i ^ bits[step if i % CORES == 0 else ste...]
    ppermute x0 -> x4, waiting for transfers between devices: none -> 4.06 us  [z_swap(): lax.ppermute(value, 'atom', [(i, i ^ bits[step if i % CORES == 0 else ste...]
    ppermute x12 -> x8, waiting for transfers between devices: 9.71 us -> 5.94 us  [swap(): return lax.ppermute(value, axis, [(i, i ^ bit) for i in range(count)])]
    pallas_call x14, Pallas kernels: 13.5 us -> 11.7 us  [call(): pl.pallas_call(kernel, out_shape=outs, in_specs=[pl.BlockSpec(memory_spac...]
  transfers between devices with their start and end apart: 12 -> 12, of which waited for: 10 -> 10; matrix products, arithmetic and copies ran while one was open for 0% -> 0% of each run, Pallas kernels for 18% -> 16%
where the time goes in v3:
time: 37.7 us; the launch traced here: 37.5 us
  starting transfers between devices  15.7 us (42%)
  Pallas kernels  11.7 us (31%)
  waiting for transfers between devices  10 us (27%)
    pallas_call x14, Pallas kernels, call(): pl.pallas_call(kernel, out_shape=outs, in_specs=[pl.BlockSpec(memory_spac...  11.7 us
    ppermute x8, starting transfers between devices, swap(): return lax.ppermute(value, axis, [(i, i ^ bit) for i in range(count)])  8.3 us
    ppermute x4, starting transfers between devices, z_swap(): lax.ppermute(value, 'atom', [(i, i ^ bits[step if i % CORES == 0 else ste...  7.43 us
    ppermute x8, waiting for transfers between devices, swap(): return lax.ppermute(value, axis, [(i, i ^ bit) for i in range(count)])  5.94 us
    ppermute x4, waiting for transfers between devices, z_swap(): lax.ppermute(value, 'atom', [(i, i ^ bits[step if i % CORES == 0 else ste...  4.06 us
  transfers between devices with their start and end apart: 12, of which 10 were waited for; matrix products, arithmetic and copies ran while one was open for 0% of the time, Pallas kernels for 16%

profile of v3, /device:TPU:0, one launch (start us, length us, event | category | flops | bytes accessed | tf_op | source)
XLA Modules:
  0.0 37.5 jit_solution(4353055710857412965)
XLA Ops:
  0.0 1.4 %shard_map.100 = (bf16[512,128]{1,0:T(8,128)(2,1)S(1)}, bf16[512,128]{1,0:T(8,128)(2,1)S(1)}, bf16[80,512]{1,0:T(8,128)(2,1)S(1)}, s32[3,1024]{1,0:T(4,128)S(1)}, f32[1,1024]{1,0:T(1,128)S(1)}) custom-call(bf16[512,128]{1,0:T(8,128)(2,1)} %features_ref.1, s32[1,512]{1,0:T(1,128)} %bitcast.5, f32[3,512]{1,0:T(4,128)} %coords_ref.1, s32[3,1024]{1,0:T(4,128)} %waves_ref.1, ...), custom_call_target="tpu_custom_call" | custom-call | bytes 536576 | tf_op jit(solution)/shard_map/pallas_call | solution.py:226
  1.4 4.0 %collective-permute-start.2 = (bf16[80,512]{1,0:T(8,128)(2,1)S(1)}, bf16[80,512]{1,0:T(8,128)(2,1)S(1)}, u32[]{:S(2)}, u32[]{:S(2)}) collective-permute-start(bf16[80,512]{1,0:T(8,128)(2,1)S(1)} %get-tuple-element.43.message_ref), channel_id=1, source_target_pairs={{0,3},{1,2},{2,1},{3,0},{4,7},{5,6},{6,5},{7,4},{8,11},{9,10},{10,... | collective-permute-start | bytes 245768 | tf_op jit(solution)/shard_map/ppermute | solution.py:239
  5.3 0.5 %collective-permute-start.1 = (bf16[80,512]{1,0:T(8,128)(2,1)S(1)}, bf16[80,512]{1,0:T(8,128)(2,1)S(1)}, u32[]{:S(2)}, u32[]{:S(2)}) collective-permute-start(bf16[80,512]{1,0:T(8,128)(2,1)S(1)} %get-tuple-element.43.message_ref), channel_id=1, source_target_pairs={{0,2},{1,3},{2,0},{3,1},{4,6},{5,7},{6,4},{7,5},{8,10},{9,11},{10,... | collective-permute-start | bytes 245768 | tf_op jit(solution)/shard_map/ppermute | solution.py:239
  5.8 0.1 collective-permute-start
  6.0 2.3 %shard_map.101 = (bf16[1024,16]{1,0:T(8,128)(2,1)S(1)}, f32[1,1024]{1,0:T(1,128)S(1)}, bf16[1024,512]{1,0:T(8,128)(2,1)S(1)}, bf16[1024,512]{1,0:T(8,128)(2,1)S(...) custom-call(s32[3,1024]{1,0:T(4,128)S(1)} %get-tuple-element.41.waves_ref, ...), custom_call_target="tpu_custom_call" | custom-call | flops 134217728 | bytes 2756608 | tf_op jit(solution)/shard_map/pallas_call | solution.py:226
  8.2 0.0 collective-permute-done.2.refs_4_
  8.3 1.5 %collective-permute-done.1.refs_3_ = bf16[80,512]{1,0:T(8,128)(2,1)S(1)} collective-permute-done((bf16[80,512]{1,0:T(8,128)(2,1)S(1)}, bf16[80,512]{1,0:T(8,128)(2,1)S(1)}, u32[]{:S(2)}, u32[]{:S(2)}) %collective-permute-start.1) | collective-permute-done | bytes 81952 | tf_op jit(solution)/shard_map/ppermute | solution.py:239
  9.8 0.5 %collective-permute-done.refs_2_ = bf16[80,512]{1,0:T(8,128)(2,1)S(1)} collective-permute-done((bf16[80,512]{1,0:T(8,128)(2,1)S(1)}, bf16[80,512]{1,0:T(8,128)(2,1)S(1)}, u32[]{:S(2)}, u32[]{:S(2)}) %collective-permute-start) | collective-permute-done | bytes 81952 | tf_op jit(solution)/shard_map/ppermute | solution.py:239
  10.3 2.4 %shard_map.103 = (bf16[1024,1536]{1,0:T(8,128)(2,1)S(1)}, bf16[64,1024]{1,0:T(8,128)(2,1)S(1)}) custom-call(bf16[1024,16]{1,0:T(8,128)(2,1)S(1)} %get-tuple-element.55.refs_0_, f32[64,1024]{1,0:T(8,128)S(1)} %get-tuple-element.48.refs_1_, bf16[80,512]{1,0:T(8,128)(2,1)S(1)} %collective-permute-done.refs_2_, ...), custom_call_target="tpu_custom_call" | custom-call | flops 201326592 | bytes 3817472 | tf_op jit(solution)/shard_map/pallas_call | solution.py:226
  12.6 0.1 collective-permute-start.3
  12.7 1.3 %shard_map.102 = (bf16[512,1536]{1,0:T(8,128)(2,1)S(1)}, f32[64,512]{1,0:T(8,128)S(1)}) custom-call(bf16[1024,16]{1,0:T(8,128)(2,1)S(1)} %get-tuple-element.55.refs_0_, f32[64,1024]{1,0:T(8,128)S(1)} %get-tuple-element.46.refs_1_, bf16[80,512]{1,0:T(8,128)(2,1)S(1)} %collective-permute-done.refs_2_, bf16[80,512]{1,0:T(8,128)(2,1)S(1)} %collective-permute-done.1.refs_3_, ...), custom_call_target="tpu_custom_call" | custom-call | flops 100663296 | bytes 2244608 | tf_op jit(solution)/shard_map/pallas_call | solution.py:226
  14.0 0.0 collective-permute-done.3.refs_1_
  14.1 1.6 %collective-permute-start.4 = (bf16[64,512]{1,0:T(8,128)(2,1)S(1)}, bf16[64,512]{1,0:T(8,128)(2,1)S(1)}, u32[]{:S(2)}, u32[]{:S(2)}) collective-permute-start(bf16[64,512]{1,0:T(8,128)(2,1)S(1)} %get-tuple-element.52), channel_id=1, source_target_pairs={{0,8},{4,20},{8,0},{12,28},{16,24},{20,4},{24,16},{28,12},{1,9},{5... | collective-permute-start | bytes 196616 | tf_op jit(solution)/shard_map/ppermute | solution.py:246
  15.7 1.3 %shard_map.106 = (bf16[512,1536]{1,0:T(8,128)(2,1)S(1)}, f32[64,512]{1,0:T(8,128)S(1)}) custom-call(bf16[1024,16]{1,0:T(8,128)(2,1)S(1)} %get-tuple-element.55.refs_0_, f32[64,1024]{1,0:T(8,128)S(1)} %get-tuple-element.46.refs_1_, bf16[80,512]{1,0:T(8,128)(2,1)S(1)} %collective-permute-done.refs_2_, bf16[80,512]{1,0:T(8,128)(2,1)S(1)} %collective-permute-done.1.refs_3_, ...), custom_call_target="tpu_custom_call" | custom-call | flops 100663296 | bytes 2244608 | tf_op jit(solution)/shard_map/pallas_call | solution.py:226
  17.1 0.5 %collective-permute-start.6 = (bf16[64,512]{1,0:T(8,128)(2,1)S(1)}, bf16[64,512]{1,0:T(8,128)(2,1)S(1)}, u32[]{:S(2)}, u32[]{:S(2)}) collective-permute-start(bf16[64,512]{1,0:T(8,128)(2,1)S(1)} %get-tuple-element.59), channel_id=1, source_target_pairs={{0,8},{4,20},{8,0},{12,28},{16,24},{20,4},{24,16},{28,12},{1,9},{5... | collective-permute-start | bytes 196616 | tf_op jit(solution)/shard_map/ppermute | solution.py:246
  17.6 1.5 %collective-permute-done.4.refs_1_ = bf16[64,512]{1,0:T(8,128)(2,1)S(1)} collective-permute-done((bf16[64,512]{1,0:T(8,128)(2,1)S(1)}, bf16[64,512]{1,0:T(8,128)(2,1)S(1)}, u32[]{:S(2)}, u32[]{:S(2)}) %collective-permute-start.4) | collective-permute-done | bytes 65568 | tf_op jit(solution)/shard_map/ppermute | solution.py:246
  19.1 2.1 %collective-permute-start.5 = (bf16[64,512]{1,0:T(8,128)(2,1)S(1)}, bf16[64,512]{1,0:T(8,128)(2,1)S(1)}, u32[]{:S(2)}, u32[]{:S(2)}) collective-permute-start(bf16[64,512]{1,0:T(8,128)(2,1)S(1)} %get-tuple-element.54), channel_id=1, source_target_pairs={{0,16},{4,12},{8,24},{12,4},{16,0},{20,28},{24,8},{28,20},{1,17},{... | collective-permute-start | bytes 196616 | tf_op jit(solution)/shard_map/ppermute | solution.py:246
  21.2 0.2 collective-permute-done.6.refs_1_
  21.4 3.2 %collective-permute-start.7 = (bf16[64,512]{1,0:T(8,128)(2,1)S(1)}, bf16[64,512]{1,0:T(8,128)(2,1)S(1)}, u32[]{:S(2)}, u32[]{:S(2)}) collective-permute-start(bf16[64,512]{1,0:T(8,128)(2,1)S(1)} %get-tuple-element.61), channel_id=1, source_target_pairs={{0,16},{4,12},{8,24},{12,4},{16,0},{20,28},{24,8},{28,20},{1,17},{... | collective-permute-start | bytes 196616 | tf_op jit(solution)/shard_map/ppermute | solution.py:246
  24.6 0.5 %collective-permute-done.5.refs_2_ = bf16[64,512]{1,0:T(8,128)(2,1)S(1)} collective-permute-done((bf16[64,512]{1,0:T(8,128)(2,1)S(1)}, bf16[64,512]{1,0:T(8,128)(2,1)S(1)}, u32[]{:S(2)}, u32[]{:S(2)}) %collective-permute-start.5) | collective-permute-done | bytes 65568 | tf_op jit(solution)/shard_map/ppermute | solution.py:246
  25.1 1.9 %collective-permute-done.7.refs_4_ = bf16[64,512]{1,0:T(8,128)(2,1)S(1)} collective-permute-done((bf16[64,512]{1,0:T(8,128)(2,1)S(1)}, bf16[64,512]{1,0:T(8,128)(2,1)S(1)}, u32[]{:S(2)}, u32[]{:S(2)}) %collective-permute-start.7) | collective-permute-done | bytes 65568 | tf_op jit(solution)/shard_map/ppermute | solution.py:246
  27.0 0.1 collective-permute-start.8
  27.1 0.8 %shard_map.110 = (f32[64,512]{1,0:T(8,128)S(1)}, f32[64,1536]{1,0:T(8,128)S(1)}) custom-call(bf16[64,1024]{1,0:T(8,128)(2,1)S(1)} %shard_map.109.w_ref, bf16[1024,512]{1,0:T(8,128)(2,1)S(1)} %get-tuple-element.63.p0_ref, bf16[512,1536]{1,0:T(8,128)(2,1)S(1)} %get-tuple-element.64.refs_0_, bf16[512,1536]{1,0:T(8,128)(2,1)S(1)} %get-tuple-element.65.refs_1_), custom_call_target="tpu_custom_call" | custom-call | flops 268435456 | bytes 4849664 | tf_op jit(solution)/shard_map/pallas_call | solution.py:226
  27.9 0.5 %collective-permute-done.8.w_ref = bf16[64,1024]{1,0:T(8,128)(2,1)S(1)} collective-permute-done((bf16[64,1024]{1,0:T(8,128)(2,1)S(1)}, bf16[64,1024]{1,0:T(8,128)(2,1)S(1)}, u32[]{:S(2)}, u32[]{:S(2)}) %collective-permute-start.8) | collective-permute-done | bytes 131104 | tf_op jit(solution)/shard_map/ppermute | solution.py:239
  28.4 0.0 copy-start
  28.4 0.0 copy-start.1
  28.4 0.0 copy-start.2
  28.4 0.7 %shard_map.112 = (bf16[64,512]{1,0:T(8,128)(2,1)S(1)}, bf16[64,512]{1,0:T(8,128)(2,1)S(1)}, bf16[64,512]{1,0:T(8,128)(2,1)S(1)}) custom-call(bf16[64,1024]{1,0:T(8,128)(2,1)S(1)} %collective-permute-done.8.w_ref, bf16[1024,1536]{1,0:T(8,128)(2,1)S(1)} %get-tuple-element.70.p_ref, f32[64,1536]{1,0:T(8,128)S(1)} %get-tuple-element.71.rest_ref), custom_call_target="tpu_custom_call" | custom-call | flops 201326592 | bytes 3866624 | tf_op jit(solution)/shard_map/pallas_call | solution.py:226
  29.1 1.6 %collective-permute-start.9 = (bf16[64,512]{1,0:T(8,128)(2,1)S(1)}, bf16[64,512]{1,0:T(8,128)(2,1)S(1)}, u32[]{:S(2)}, u32[]{:S(2)}) collective-permute-start(bf16[64,512]{1,0:T(8,128)(2,1)S(1)} %get-tuple-element.72), channel_id=1, source_target_pairs={{0,3},{1,2},{2,1},{3,0},{4,7},{5,6},{6,5},{7,4},{8,11},{9,10},{10,... | collective-permute-start | bytes 196616 | tf_op jit(solution)/shard_map/ppermute | solution.py:239
  30.6 1.5 %collective-permute-start.10 = (bf16[64,512]{1,0:T(8,128)(2,1)S(1)}, bf16[64,512]{1,0:T(8,128)(2,1)S(1)}, u32[]{:S(2)}, u32[]{:S(2)}) collective-permute-start(bf16[64,512]{1,0:T(8,128)(2,1)S(1)} %get-tuple-element.73), channel_id=1, source_target_pairs={{0,1},{1,0},{2,3},{3,2},{4,5},{5,4},{6,7},{7,6},{8,9},{9,8},{10,11... | collective-permute-start | bytes 196616 | tf_op jit(solution)/shard_map/ppermute | solution.py:239
  32.1 0.5 %collective-permute-start.11 = (bf16[64,512]{1,0:T(8,128)(2,1)S(1)}, bf16[64,512]{1,0:T(8,128)(2,1)S(1)}, u32[]{:S(2)}, u32[]{:S(2)}) collective-permute-start(bf16[64,512]{1,0:T(8,128)(2,1)S(1)} %get-tuple-element.74), channel_id=1, source_target_pairs={{0,2},{1,3},{2,0},{3,1},{4,6},{5,7},{6,4},{7,5},{8,10},{9,11},{10,... | collective-permute-start | bytes 196616 | tf_op jit(solution)/shard_map/ppermute | solution.py:239
  32.6 0.0 copy-done
  32.6 0.4 shard_map.111
  33.0 2.0 %collective-permute-done.9.refs_0_ = bf16[64,512]{1,0:T(8,128)(2,1)S(1)} collective-permute-done((bf16[64,512]{1,0:T(8,128)(2,1)S(1)}, bf16[64,512]{1,0:T(8,128)(2,1)S(1)}, u32[]{:S(2)}, u32[]{:S(2)}) %collective-permute-start.9) | collective-permute-done | bytes 65568 | tf_op jit(solution)/shard_map/ppermute | solution.py:239
  35.0 0.6 %collective-permute-done.10.refs_1_ = bf16[64,512]{1,0:T(8,128)(2,1)S(1)} collective-permute-done((bf16[64,512]{1,0:T(8,128)(2,1)S(1)}, bf16[64,512]{1,0:T(8,128)(2,1)S(1)}, u32[]{:S(2)}, u32[]{:S(2)}) %collective-permute-start.10) | collective-permute-done | bytes 65568 | tf_op jit(solution)/shard_map/ppermute | solution.py:239
  35.7 0.7 %collective-permute-done.11.refs_2_ = bf16[64,512]{1,0:T(8,128)(2,1)S(1)} collective-permute-done((bf16[64,512]{1,0:T(8,128)(2,1)S(1)}, bf16[64,512]{1,0:T(8,128)(2,1)S(1)}, u32[]{:S(2)}, u32[]{:S(2)}) %collective-permute-start.11) | collective-permute-done | bytes 65568 | tf_op jit(solution)/shard_map/ppermute | solution.py:239
  36.4 0.0 copy-done.1
  36.4 0.0 copy-done.2
  36.4 1.1 %shard_map.113 = bf16[512,128]{1,0:T(8,128)(2,1)} custom-call(bf16[512,128]{1,0:T(8,128)(2,1)S(1)} %get-tuple-element.40.hidden_ref, f32[64,512]{1,0:T(8,128)S(1)} %get-tuple-element.68.total_ref, f32[512,256]{1,0:T(8,128)S(1)} %get-tuple-element.69.pre_ref, bf16[64,256]{1,0:T(8,128)(2,1)S(1)} %copy-done.2, bf16[256,128]{1,0:T(8,128)(2,1)S(1)} %copy-done.1, ...), custom_call_target="tpu_custom_call" | custom-call | bytes 1212416 | tf_op jit(solution)/shard_map/pallas_call | solution.py:226
  (5 shorter events, 0.1 us)
Async XLA Ops:
  1.4 6.9 %collective-permute-start.2 = (bf16[80,512]{1,0:T(8,128)(2,1)S(1)}, bf16[80,512]{1,0:T(8,128)(2,1)S(1)}, u32[]{:S(2)}, u32[]{:S(2)}) collective-permute-start(bf16[80,512]{1,0:T(8,128)(2,1)S(1)} %get-tuple-element.43.message_ref), channel_id=1, source_target_pairs={{0,3},{1,2},{2,1},{3,0},{4,7},{5,6},{6,5},{7,4},{8,11},{9,10},{10,... | collective-permute-start | bytes 245768 | tf_op jit(solution)/shard_map/ppermute | solution.py:239
  5.3 4.4 %collective-permute-start.1 = (bf16[80,512]{1,0:T(8,128)(2,1)S(1)}, bf16[80,512]{1,0:T(8,128)(2,1)S(1)}, u32[]{:S(2)}, u32[]{:S(2)}) collective-permute-start(bf16[80,512]{1,0:T(8,128)(2,1)S(1)} %get-tuple-element.43.message_ref), channel_id=1, source_target_pairs={{0,2},{1,3},{2,0},{3,1},{4,6},{5,7},{6,4},{7,5},{8,10},{9,11},{10,... | collective-permute-start | bytes 245768 | tf_op jit(solution)/shard_map/ppermute | solution.py:239
  5.8 4.4 %collective-permute-start = (bf16[80,512]{1,0:T(8,128)(2,1)S(1)}, bf16[80,512]{1,0:T(8,128)(2,1)S(1)}, u32[]{:S(2)}, u32[]{:S(2)}) collective-permute-start(bf16[80,512]{1,0:T(8,128)(2,1)S(1)} %get-tuple-element.43.message_ref), channel_id=1, source_target_pairs={{0,1},{1,0},{2,3},{3,2},{4,5},{5,4},{6,7},{7,6},{8,9},{9,8},{10,11... | collective-permute-start | bytes 245768 | tf_op jit(solution)/shard_map/ppermute | solution.py:239
  12.6 1.4 %collective-permute-start.3 = (bf16[64,1024]{1,0:T(8,128)(2,1)S(1)}, bf16[64,1024]{1,0:T(8,128)(2,1)S(1)}, u32[]{:S(2)}, u32[]{:S(2)}) collective-permute-start(bf16[64,1024]{1,0:T(8,128)(2,1)S(1)} %get-tuple-element.49), channel_id=1, source_target_pairs={{0,4},{4,0},{8,12},{12,8},{16,20},{20,16},{24,28},{28,24},{1,5},{5... | collective-permute-start | bytes 393224 | tf_op jit(solution)/shard_map/ppermute | solution.py:239
  14.1 5.0 %collective-permute-start.4 = (bf16[64,512]{1,0:T(8,128)(2,1)S(1)}, bf16[64,512]{1,0:T(8,128)(2,1)S(1)}, u32[]{:S(2)}, u32[]{:S(2)}) collective-permute-start(bf16[64,512]{1,0:T(8,128)(2,1)S(1)} %get-tuple-element.52), channel_id=1, source_target_pairs={{0,8},{4,20},{8,0},{12,28},{16,24},{20,4},{24,16},{28,12},{1,9},{5... | collective-permute-start | bytes 196616 | tf_op jit(solution)/shard_map/ppermute | solution.py:246
  17.1 4.3 %collective-permute-start.6 = (bf16[64,512]{1,0:T(8,128)(2,1)S(1)}, bf16[64,512]{1,0:T(8,128)(2,1)S(1)}, u32[]{:S(2)}, u32[]{:S(2)}) collective-permute-start(bf16[64,512]{1,0:T(8,128)(2,1)S(1)} %get-tuple-element.59), channel_id=1, source_target_pairs={{0,8},{4,20},{8,0},{12,28},{16,24},{20,4},{24,16},{28,12},{1,9},{5... | collective-permute-start | bytes 196616 | tf_op jit(solution)/shard_map/ppermute | solution.py:246
  19.1 6.0 %collective-permute-start.5 = (bf16[64,512]{1,0:T(8,128)(2,1)S(1)}, bf16[64,512]{1,0:T(8,128)(2,1)S(1)}, u32[]{:S(2)}, u32[]{:S(2)}) collective-permute-start(bf16[64,512]{1,0:T(8,128)(2,1)S(1)} %get-tuple-element.54), channel_id=1, source_target_pairs={{0,16},{4,12},{8,24},{12,4},{16,0},{20,28},{24,8},{28,20},{1,17},{... | collective-permute-start | bytes 196616 | tf_op jit(solution)/shard_map/ppermute | solution.py:246
  21.4 5.5 %collective-permute-start.7 = (bf16[64,512]{1,0:T(8,128)(2,1)S(1)}, bf16[64,512]{1,0:T(8,128)(2,1)S(1)}, u32[]{:S(2)}, u32[]{:S(2)}) collective-permute-start(bf16[64,512]{1,0:T(8,128)(2,1)S(1)} %get-tuple-element.61), channel_id=1, source_target_pairs={{0,16},{4,12},{8,24},{12,4},{16,0},{20,28},{24,8},{28,20},{1,17},{... | collective-permute-start | bytes 196616 | tf_op jit(solution)/shard_map/ppermute | solution.py:246
  27.0 1.4 %collective-permute-start.8 = (bf16[64,1024]{1,0:T(8,128)(2,1)S(1)}, bf16[64,1024]{1,0:T(8,128)(2,1)S(1)}, u32[]{:S(2)}, u32[]{:S(2)}) collective-permute-start(bf16[64,1024]{1,0:T(8,128)(2,1)S(1)} %shard_map.109.w_ref), channel_id=1, source_target_pairs={{0,4},{4,0},{8,12},{12,8},{16,20},{20,16},{24,28},{28,24},{1,5},{5... | collective-permute-start | bytes 393224 | tf_op jit(solution)/shard_map/ppermute | solution.py:239
  28.4 4.2 %copy-start = (bf16[128,256]{1,0:T(8,128)(2,1)S(1)}, bf16[128,256]{1,0:T(8,128)(2,1)}, u32[]{:S(2)}) copy-start(bf16[128,256]{1,0:T(8,128)(2,1)} %w_feat_ref.1) | copy-start | bytes 196612
  28.4 8.0 %copy-start.1 = (bf16[256,128]{1,0:T(8,128)(2,1)S(1)}, bf16[256,128]{1,0:T(8,128)(2,1)}, u32[]{:S(2)}) copy-start(bf16[256,128]{1,0:T(8,128)(2,1)} %w_out_ref.1) | copy-start | bytes 196612
  28.4 8.0 %copy-start.2 = (bf16[64,256]{1,0:T(8,128)(2,1)S(1)}, bf16[64,256]{1,0:T(8,128)(2,1)}, u32[]{:S(2)}) copy-start(bf16[64,256]{1,0:T(8,128)(2,1)} %w_pot_ref.1) | copy-start | bytes 98308
  29.1 5.9 %collective-permute-start.9 = (bf16[64,512]{1,0:T(8,128)(2,1)S(1)}, bf16[64,512]{1,0:T(8,128)(2,1)S(1)}, u32[]{:S(2)}, u32[]{:S(2)}) collective-permute-start(bf16[64,512]{1,0:T(8,128)(2,1)S(1)} %get-tuple-element.72), channel_id=1, source_target_pairs={{0,3},{1,2},{2,1},{3,0},{4,7},{5,6},{6,5},{7,4},{8,11},{9,10},{10,... | collective-permute-start | bytes 196616 | tf_op jit(solution)/shard_map/ppermute | solution.py:239
  30.6 5.0 %collective-permute-start.10 = (bf16[64,512]{1,0:T(8,128)(2,1)S(1)}, bf16[64,512]{1,0:T(8,128)(2,1)S(1)}, u32[]{:S(2)}, u32[]{:S(2)}) collective-permute-start(bf16[64,512]{1,0:T(8,128)(2,1)S(1)} %get-tuple-element.73), channel_id=1, source_target_pairs={{0,1},{1,0},{2,3},{3,2},{4,5},{5,4},{6,7},{7,6},{8,9},{9,8},{10,11... | collective-permute-start | bytes 196616 | tf_op jit(solution)/shard_map/ppermute | solution.py:239
  32.1 4.3 %collective-permute-start.11 = (bf16[64,512]{1,0:T(8,128)(2,1)S(1)}, bf16[64,512]{1,0:T(8,128)(2,1)S(1)}, u32[]{:S(2)}, u32[]{:S(2)}) collective-permute-start(bf16[64,512]{1,0:T(8,128)(2,1)S(1)} %get-tuple-element.74), channel_id=1, source_target_pairs={{0,2},{1,3},{2,0},{3,1},{4,6},{5,7},{6,4},{7,5},{8,10},{9,11},{10,... | collective-permute-start | bytes 196616 | tf_op jit(solution)/shard_map/ppermute | solution.py:239

commit v4 on v3

--- a/solution.py
+++ b/solution.py
@@ -185,9 +185,12 @@
 
 def send_kernel(w_ref, p_ref, rest_ref, *send_refs):
     atoms = send_refs[0].shape[1]
+    core = lax.axis_index("atom") % CORES
     for b, ref in enumerate(send_refs):
-        part = jnp.dot(w_ref[...], p_ref[:, b * atoms : (b + 1) * atoms], preferred_element_type=F32)
-        ref[...] = (rest_ref[:, b * atoms : (b + 1) * atoms] + part).astype(BF16)
+        block = jnp.where(core == 0, len(send_refs) - 1 - b, b)
+        here = pl.ds(pl.multiple_of(block * atoms, atoms), atoms)
+        part = jnp.dot(w_ref[...], p_ref[:, here], preferred_element_type=F32)
+        ref[...] = (rest_ref[:, here] + part).astype(BF16)
 
 
 def keep_kernel(w_ref, p0_ref, own_ref, mixed_ref, w_feat_ref, total_ref, pre_ref):
@@ -239,6 +242,13 @@
     return lax.ppermute(value, axis, [(i, i ^ bit) for i in range(count)])
 
 
+def wave_swap(value, step):
+    rows, count = lax.axis_size("atom"), lax.axis_size("wave")
+    bits = [count - 1 - step, 1 + step]
+    pairs = [(a * count + w, a * count + (w ^ bits[a % CORES])) for a in range(rows) for w in range(count)]
+    return lax.ppermute(value, ("atom", "wave"), pairs)
+
+
 def z_swap(value, step):
     count = lax.axis_size("atom")
     steps = (count // CORES).bit_length() - 1
@@ -337,8 +347,7 @@
         send_kernel, [array((q, atoms), BF16)] * (wcount - 1), w_other, p_other, others,
         flops=2 * half_rows * rest * q,
     )
-    order = sorted(range(wcount - 1), key=lambda b: -bin(b + 1).count("1"))
-    parts = [swap(sends[b], "wave", b + 1) for b in order]
+    parts = [wave_swap(value, b) for b, value in enumerate(sends)]
     total, pre = call(
         keep_kernel,
         [array((q, atoms), F32), array((atoms, hidden), F32)],

time: 37.7 us -> 37.1 us (0.984)
  waiting for transfers between devices: 10 us -> 9.47 us
    ppermute x8 -> x5, starting transfers between devices: 8.3 us -> 4.74 us  [swap(): return lax.ppermute(value, axis, [(i, i ^ bit) for i in range(count)])]
    ppermute x0 -> x3, starting transfers between devices: none -> 3.55 us  [wave_swap(): return lax.ppermute(value, ('atom', 'wave'), pairs)]
    ppermute x8 -> x5, waiting for transfers between devices: 5.94 us -> 2.56 us  [swap(): return lax.ppermute(value, axis, [(i, i ^ bit) for i in range(count)])]
    ppermute x0 -> x3, waiting for transfers between devices: none -> 2.85 us  [wave_swap(): return lax.ppermute(value, ('atom', 'wave'), pairs)]
  transfers between devices with their start and end apart: 12 -> 12, of which waited for: 10 -> 10; matrix products, arithmetic and copies ran while one was open for 0% -> 0% of each run, Pallas kernels for 16% -> 17%
where the time goes in v4:
time: 37.1 us; the launch traced here: 37 us
  starting transfers between devices  15.7 us (42%)
  Pallas kernels  11.7 us (32%)
  waiting for transfers between devices  9.47 us (26%)
    pallas_call x14, Pallas kernels, call(): pl.pallas_call(kernel, out_shape=outs, in_specs=[pl.BlockSpec(memory_spac...  11.7 us
    ppermute x4, starting transfers between devices, z_swap(): lax.ppermute(value, 'atom', [(i, i ^ bits[step if i % CORES == 0 else ste...  7.43 us
    ppermute x5, starting transfers between devices, swap(): return lax.ppermute(value, axis, [(i, i ^ bit) for i in range(count)])  4.74 us
    ppermute x4, waiting for transfers between devices, z_swap(): lax.ppermute(value, 'atom', [(i, i ^ bits[step if i % CORES == 0 else ste...  4.06 us
    ppermute x3, starting transfers between devices, wave_swap(): return lax.ppermute(value, ('atom', 'wave'), pairs)  3.55 us
    ppermute x3, waiting for transfers between devices, wave_swap(): return lax.ppermute(value, ('atom', 'wave'), pairs)  2.85 us
    ppermute x5, waiting for transfers between devices, swap(): return lax.ppermute(value, axis, [(i, i ^ bit) for i in range(count)])  2.56 us
  transfers between devices with their start and end apart: 12, of which 10 were waited for; matrix products, arithmetic and copies ran while one was open for 0% of the time, Pallas kernels for 17%

profile of v4, /device:TPU:0, one launch (start us, length us, event | category | flops | bytes accessed | tf_op | source)
XLA Modules:
  0.0 37.0 jit_solution(3230684189743359388)
XLA Ops:
  0.0 1.4 %shard_map.100 = (bf16[512,128]{1,0:T(8,128)(2,1)S(1)}, bf16[512,128]{1,0:T(8,128)(2,1)S(1)}, bf16[80,512]{1,0:T(8,128)(2,1)S(1)}, s32[3,1024]{1,0:T(4,128)S(1)}, f32[1,1024]{1,0:T(1,128)S(1)}) custom-call(bf16[512,128]{1,0:T(8,128)(2,1)} %features_ref.1, s32[1,512]{1,0:T(1,128)} %bitcast.5, f32[3,512]{1,0:T(4,128)} %coords_ref.1, s32[3,1024]{1,0:T(4,128)} %waves_ref.1, ...), custom_call_target="tpu_custom_call" | custom-call | bytes 536576 | tf_op jit(solution)/shard_map/pallas_call | solution.py:229
  1.4 4.0 %collective-permute-start.2 = (bf16[80,512]{1,0:T(8,128)(2,1)S(1)}, bf16[80,512]{1,0:T(8,128)(2,1)S(1)}, u32[]{:S(2)}, u32[]{:S(2)}) collective-permute-start(bf16[80,512]{1,0:T(8,128)(2,1)S(1)} %get-tuple-element.43.message_ref), channel_id=1, source_target_pairs={{0,3},{1,2},{2,1},{3,0},{4,7},{5,6},{6,5},{7,4},{8,11},{9,10},{10,... | collective-permute-start | bytes 245768 | tf_op jit(solution)/shard_map/ppermute | solution.py:242
  5.3 0.5 %collective-permute-start.1 = (bf16[80,512]{1,0:T(8,128)(2,1)S(1)}, bf16[80,512]{1,0:T(8,128)(2,1)S(1)}, u32[]{:S(2)}, u32[]{:S(2)}) collective-permute-start(bf16[80,512]{1,0:T(8,128)(2,1)S(1)} %get-tuple-element.43.message_ref), channel_id=1, source_target_pairs={{0,2},{1,3},{2,0},{3,1},{4,6},{5,7},{6,4},{7,5},{8,10},{9,11},{10,... | collective-permute-start | bytes 245768 | tf_op jit(solution)/shard_map/ppermute | solution.py:242
  5.8 0.1 collective-permute-start
  6.0 2.3 %shard_map.101 = (bf16[1024,16]{1,0:T(8,128)(2,1)S(1)}, f32[1,1024]{1,0:T(1,128)S(1)}, bf16[1024,512]{1,0:T(8,128)(2,1)S(1)}, bf16[1024,512]{1,0:T(8,128)(2,1)S(...) custom-call(s32[3,1024]{1,0:T(4,128)S(1)} %get-tuple-element.41.waves_ref, ...), custom_call_target="tpu_custom_call" | custom-call | flops 134217728 | bytes 2756608 | tf_op jit(solution)/shard_map/pallas_call | solution.py:229
  8.2 0.0 collective-permute-done.2.refs_4_
  8.3 1.5 %collective-permute-done.1.refs_3_ = bf16[80,512]{1,0:T(8,128)(2,1)S(1)} collective-permute-done((bf16[80,512]{1,0:T(8,128)(2,1)S(1)}, bf16[80,512]{1,0:T(8,128)(2,1)S(1)}, u32[]{:S(2)}, u32[]{:S(2)}) %collective-permute-start.1) | collective-permute-done | bytes 81952 | tf_op jit(solution)/shard_map/ppermute | solution.py:242
  9.8 0.5 %collective-permute-done.refs_2_ = bf16[80,512]{1,0:T(8,128)(2,1)S(1)} collective-permute-done((bf16[80,512]{1,0:T(8,128)(2,1)S(1)}, bf16[80,512]{1,0:T(8,128)(2,1)S(1)}, u32[]{:S(2)}, u32[]{:S(2)}) %collective-permute-start) | collective-permute-done | bytes 81952 | tf_op jit(solution)/shard_map/ppermute | solution.py:242
  10.3 2.4 %shard_map.103 = (bf16[1024,1536]{1,0:T(8,128)(2,1)S(1)}, bf16[64,1024]{1,0:T(8,128)(2,1)S(1)}) custom-call(bf16[1024,16]{1,0:T(8,128)(2,1)S(1)} %get-tuple-element.55.refs_0_, f32[64,1024]{1,0:T(8,128)S(1)} %get-tuple-element.48.refs_1_, bf16[80,512]{1,0:T(8,128)(2,1)S(1)} %collective-permute-done.refs_2_, ...), custom_call_target="tpu_custom_call" | custom-call | flops 201326592 | bytes 3817472 | tf_op jit(solution)/shard_map/pallas_call | solution.py:229
  12.6 0.1 collective-permute-start.3
  12.7 1.3 %shard_map.102 = (bf16[512,1536]{1,0:T(8,128)(2,1)S(1)}, f32[64,512]{1,0:T(8,128)S(1)}) custom-call(bf16[1024,16]{1,0:T(8,128)(2,1)S(1)} %get-tuple-element.55.refs_0_, f32[64,1024]{1,0:T(8,128)S(1)} %get-tuple-element.46.refs_1_, bf16[80,512]{1,0:T(8,128)(2,1)S(1)} %collective-permute-done.refs_2_, bf16[80,512]{1,0:T(8,128)(2,1)S(1)} %collective-permute-done.1.refs_3_, ...), custom_call_target="tpu_custom_call" | custom-call | flops 100663296 | bytes 2244608 | tf_op jit(solution)/shard_map/pallas_call | solution.py:229
  14.0 0.0 collective-permute-done.3.refs_1_
  14.1 1.6 %collective-permute-start.4 = (bf16[64,512]{1,0:T(8,128)(2,1)S(1)}, bf16[64,512]{1,0:T(8,128)(2,1)S(1)}, u32[]{:S(2)}, u32[]{:S(2)}) collective-permute-start(bf16[64,512]{1,0:T(8,128)(2,1)S(1)} %get-tuple-element.52), channel_id=1, source_target_pairs={{0,8},{4,20},{8,0},{12,28},{16,24},{20,4},{24,16},{28,12},{1,9},{5... | collective-permute-start | bytes 196616 | tf_op jit(solution)/shard_map/ppermute | solution.py:256
  15.7 1.3 %shard_map.106 = (bf16[512,1536]{1,0:T(8,128)(2,1)S(1)}, f32[64,512]{1,0:T(8,128)S(1)}) custom-call(bf16[1024,16]{1,0:T(8,128)(2,1)S(1)} %get-tuple-element.55.refs_0_, f32[64,1024]{1,0:T(8,128)S(1)} %get-tuple-element.46.refs_1_, bf16[80,512]{1,0:T(8,128)(2,1)S(1)} %collective-permute-done.refs_2_, bf16[80,512]{1,0:T(8,128)(2,1)S(1)} %collective-permute-done.1.refs_3_, ...), custom_call_target="tpu_custom_call" | custom-call | flops 100663296 | bytes 2244608 | tf_op jit(solution)/shard_map/pallas_call | solution.py:229
  17.1 0.5 %collective-permute-start.6 = (bf16[64,512]{1,0:T(8,128)(2,1)S(1)}, bf16[64,512]{1,0:T(8,128)(2,1)S(1)}, u32[]{:S(2)}, u32[]{:S(2)}) collective-permute-start(bf16[64,512]{1,0:T(8,128)(2,1)S(1)} %get-tuple-element.59), channel_id=1, source_target_pairs={{0,8},{4,20},{8,0},{12,28},{16,24},{20,4},{24,16},{28,12},{1,9},{5... | collective-permute-start | bytes 196616 | tf_op jit(solution)/shard_map/ppermute | solution.py:256
  17.6 1.5 %collective-permute-done.4.refs_1_ = bf16[64,512]{1,0:T(8,128)(2,1)S(1)} collective-permute-done((bf16[64,512]{1,0:T(8,128)(2,1)S(1)}, bf16[64,512]{1,0:T(8,128)(2,1)S(1)}, u32[]{:S(2)}, u32[]{:S(2)}) %collective-permute-start.4) | collective-permute-done | bytes 65568 | tf_op jit(solution)/shard_map/ppermute | solution.py:256
  19.1 2.1 %collective-permute-start.5 = (bf16[64,512]{1,0:T(8,128)(2,1)S(1)}, bf16[64,512]{1,0:T(8,128)(2,1)S(1)}, u32[]{:S(2)}, u32[]{:S(2)}) collective-permute-start(bf16[64,512]{1,0:T(8,128)(2,1)S(1)} %get-tuple-element.54), channel_id=1, source_target_pairs={{0,16},{4,12},{8,24},{12,4},{16,0},{20,28},{24,8},{28,20},{1,17},{... | collective-permute-start | bytes 196616 | tf_op jit(solution)/shard_map/ppermute | solution.py:256
  21.2 0.2 collective-permute-done.6.refs_1_
  21.4 3.2 %collective-permute-start.7 = (bf16[64,512]{1,0:T(8,128)(2,1)S(1)}, bf16[64,512]{1,0:T(8,128)(2,1)S(1)}, u32[]{:S(2)}, u32[]{:S(2)}) collective-permute-start(bf16[64,512]{1,0:T(8,128)(2,1)S(1)} %get-tuple-element.61), channel_id=1, source_target_pairs={{0,16},{4,12},{8,24},{12,4},{16,0},{20,28},{24,8},{28,20},{1,17},{... | collective-permute-start | bytes 196616 | tf_op jit(solution)/shard_map/ppermute | solution.py:256
  24.6 0.5 %collective-permute-done.5.refs_2_ = bf16[64,512]{1,0:T(8,128)(2,1)S(1)} collective-permute-done((bf16[64,512]{1,0:T(8,128)(2,1)S(1)}, bf16[64,512]{1,0:T(8,128)(2,1)S(1)}, u32[]{:S(2)}, u32[]{:S(2)}) %collective-permute-start.5) | collective-permute-done | bytes 65568 | tf_op jit(solution)/shard_map/ppermute | solution.py:256
  25.1 1.9 %collective-permute-done.7.refs_4_ = bf16[64,512]{1,0:T(8,128)(2,1)S(1)} collective-permute-done((bf16[64,512]{1,0:T(8,128)(2,1)S(1)}, bf16[64,512]{1,0:T(8,128)(2,1)S(1)}, u32[]{:S(2)}, u32[]{:S(2)}) %collective-permute-start.7) | collective-permute-done | bytes 65568 | tf_op jit(solution)/shard_map/ppermute | solution.py:256
  27.0 0.1 collective-permute-start.8
  27.1 0.8 %shard_map.110 = (f32[64,512]{1,0:T(8,128)S(1)}, f32[64,1536]{1,0:T(8,128)S(1)}) custom-call(bf16[64,1024]{1,0:T(8,128)(2,1)S(1)} %shard_map.109.w_ref, bf16[1024,512]{1,0:T(8,128)(2,1)S(1)} %get-tuple-element.63.p0_ref, bf16[512,1536]{1,0:T(8,128)(2,1)S(1)} %get-tuple-element.64.refs_0_, bf16[512,1536]{1,0:T(8,128)(2,1)S(1)} %get-tuple-element.65.refs_1_), custom_call_target="tpu_custom_call" | custom-call | flops 268435456 | bytes 4849664 | tf_op jit(solution)/shard_map/pallas_call | solution.py:229
  27.9 0.5 %collective-permute-done.8.w_ref = bf16[64,1024]{1,0:T(8,128)(2,1)S(1)} collective-permute-done((bf16[64,1024]{1,0:T(8,128)(2,1)S(1)}, bf16[64,1024]{1,0:T(8,128)(2,1)S(1)}, u32[]{:S(2)}, u32[]{:S(2)}) %collective-permute-start.8) | collective-permute-done | bytes 131104 | tf_op jit(solution)/shard_map/ppermute | solution.py:242
  28.4 0.0 copy-start
  28.4 0.0 copy-start.1
  28.4 0.0 copy-start.2
  28.4 0.7 %shard_map.112 = (bf16[64,512]{1,0:T(8,128)(2,1)S(1)}, bf16[64,512]{1,0:T(8,128)(2,1)S(1)}, bf16[64,512]{1,0:T(8,128)(2,1)S(1)}) custom-call(bf16[64,1024]{1,0:T(8,128)(2,1)S(1)} %collective-permute-done.8.w_ref, bf16[1024,1536]{1,0:T(8,128)(2,1)S(1)} %get-tuple-element.70.p_ref, f32[64,1536]{1,0:T(8,128)S(1)} %get-tuple-element.71.rest_ref), custom_call_target="tpu_custom_call" | custom-call | flops 201326592 | bytes 3866624 | tf_op jit(solution)/shard_map/pallas_call | solution.py:229
  29.1 1.6 %collective-permute-start.9 = (bf16[64,512]{1,0:T(8,128)(2,1)S(1)}, bf16[64,512]{1,0:T(8,128)(2,1)S(1)}, u32[]{:S(2)}, u32[]{:S(2)}) collective-permute-start(bf16[64,512]{1,0:T(8,128)(2,1)S(1)} %get-tuple-element.72), channel_id=1, source_target_pairs={{0,3},{1,2},{2,1},{3,0},{4,5},{5,4},{6,7},{7,6},{8,11},{9,10},{10,... | collective-permute-start | bytes 196616 | tf_op jit(solution)/shard_map/ppermute | solution.py:249
  30.7 1.0 %collective-permute-start.10 = (bf16[64,512]{1,0:T(8,128)(2,1)S(1)}, bf16[64,512]{1,0:T(8,128)(2,1)S(1)}, u32[]{:S(2)}, u32[]{:S(2)}) collective-permute-start(bf16[64,512]{1,0:T(8,128)(2,1)S(1)} %get-tuple-element.73), channel_id=1, source_target_pairs={{0,2},{1,3},{2,0},{3,1},{4,6},{5,7},{6,4},{7,5},{8,10},{9,11},{10,... | collective-permute-start | bytes 196616 | tf_op jit(solution)/shard_map/ppermute | solution.py:249
  31.6 1.0 %collective-permute-start.11 = (bf16[64,512]{1,0:T(8,128)(2,1)S(1)}, bf16[64,512]{1,0:T(8,128)(2,1)S(1)}, u32[]{:S(2)}, u32[]{:S(2)}) collective-permute-start(bf16[64,512]{1,0:T(8,128)(2,1)S(1)} %get-tuple-element.74), channel_id=1, source_target_pairs={{0,1},{1,0},{2,3},{3,2},{4,7},{5,6},{6,5},{7,4},{8,9},{9,8},{10,11... | collective-permute-start | bytes 196616 | tf_op jit(solution)/shard_map/ppermute | solution.py:249
  32.6 0.0 copy-done
  32.7 0.4 %shard_map.111 = (f32[64,512]{1,0:T(8,128)S(1)}, f32[512,256]{1,0:T(8,128)S(1)}) custom-call(bf16[64,1024]{1,0:T(8,128)(2,1)S(1)} %collective-permute-done.8.w_ref, bf16[1024,512]{1,0:T(8,128)(2,1)S(1)} %get-tuple-element.62.p0_ref, f32[64,512]{1,0:T(8,128)S(1)} %get-tuple-element.66.own_ref, bf16[512,128]{1,0:T(8,128)(2,1)S(1)} %get-tuple-element.67.mixed_ref, ...), custom_call_target="tpu_custom_call" | custom-call | flops 67108864 | bytes 2162688 | tf_op jit(solution)/shard_map/pallas_call | solution.py:229
  33.0 1.4 %collective-permute-done.9.refs_0_ = bf16[64,512]{1,0:T(8,128)(2,1)S(1)} collective-permute-done((bf16[64,512]{1,0:T(8,128)(2,1)S(1)}, bf16[64,512]{1,0:T(8,128)(2,1)S(1)}, u32[]{:S(2)}, u32[]{:S(2)}) %collective-permute-start.9) | collective-permute-done | bytes 65568 | tf_op jit(solution)/shard_map/ppermute | solution.py:249
  34.4 1.3 %collective-permute-done.10.refs_1_ = bf16[64,512]{1,0:T(8,128)(2,1)S(1)} collective-permute-done((bf16[64,512]{1,0:T(8,128)(2,1)S(1)}, bf16[64,512]{1,0:T(8,128)(2,1)S(1)}, u32[]{:S(2)}, u32[]{:S(2)}) %collective-permute-start.10) | collective-permute-done | bytes 65568 | tf_op jit(solution)/shard_map/ppermute | solution.py:249
  35.7 0.2 collective-permute-done.11.refs_2_
  35.9 0.0 copy-done.1
  35.9 0.0 copy-done.2
  35.9 1.1 %shard_map.113 = bf16[512,128]{1,0:T(8,128)(2,1)} custom-call(bf16[512,128]{1,0:T(8,128)(2,1)S(1)} %get-tuple-element.40.hidden_ref, f32[64,512]{1,0:T(8,128)S(1)} %get-tuple-element.68.total_ref, f32[512,256]{1,0:T(8,128)S(1)} %get-tuple-element.69.pre_ref, bf16[64,256]{1,0:T(8,128)(2,1)S(1)} %copy-done.2, bf16[256,128]{1,0:T(8,128)(2,1)S(1)} %copy-done.1, ...), custom_call_target="tpu_custom_call" | custom-call | bytes 1212416 | tf_op jit(solution)/shard_map/pallas_call | solution.py:229
  (5 shorter events, 0.1 us)
Async XLA Ops:
  1.4 6.9 %collective-permute-start.2 = (bf16[80,512]{1,0:T(8,128)(2,1)S(1)}, bf16[80,512]{1,0:T(8,128)(2,1)S(1)}, u32[]{:S(2)}, u32[]{:S(2)}) collective-permute-start(bf16[80,512]{1,0:T(8,128)(2,1)S(1)} %get-tuple-element.43.message_ref), channel_id=1, source_target_pairs={{0,3},{1,2},{2,1},{3,0},{4,7},{5,6},{6,5},{7,4},{8,11},{9,10},{10,... | collective-permute-start | bytes 245768 | tf_op jit(solution)/shard_map/ppermute | solution.py:242
  5.3 4.4 %collective-permute-start.1 = (bf16[80,512]{1,0:T(8,128)(2,1)S(1)}, bf16[80,512]{1,0:T(8,128)(2,1)S(1)}, u32[]{:S(2)}, u32[]{:S(2)}) collective-permute-start(bf16[80,512]{1,0:T(8,128)(2,1)S(1)} %get-tuple-element.43.message_ref), channel_id=1, source_target_pairs={{0,2},{1,3},{2,0},{3,1},{4,6},{5,7},{6,4},{7,5},{8,10},{9,11},{10,... | collective-permute-start | bytes 245768 | tf_op jit(solution)/shard_map/ppermute | solution.py:242
  5.8 4.4 %collective-permute-start = (bf16[80,512]{1,0:T(8,128)(2,1)S(1)}, bf16[80,512]{1,0:T(8,128)(2,1)S(1)}, u32[]{:S(2)}, u32[]{:S(2)}) collective-permute-start(bf16[80,512]{1,0:T(8,128)(2,1)S(1)} %get-tuple-element.43.message_ref), channel_id=1, source_target_pairs={{0,1},{1,0},{2,3},{3,2},{4,5},{5,4},{6,7},{7,6},{8,9},{9,8},{10,11... | collective-permute-start | bytes 245768 | tf_op jit(solution)/shard_map/ppermute | solution.py:242
  12.6 1.4 %collective-permute-start.3 = (bf16[64,1024]{1,0:T(8,128)(2,1)S(1)}, bf16[64,1024]{1,0:T(8,128)(2,1)S(1)}, u32[]{:S(2)}, u32[]{:S(2)}) collective-permute-start(bf16[64,1024]{1,0:T(8,128)(2,1)S(1)} %get-tuple-element.49), channel_id=1, source_target_pairs={{0,4},{4,0},{8,12},{12,8},{16,20},{20,16},{24,28},{28,24},{1,5},{5... | collective-permute-start | bytes 393224 | tf_op jit(solution)/shard_map/ppermute | solution.py:242
  14.1 5.0 %collective-permute-start.4 = (bf16[64,512]{1,0:T(8,128)(2,1)S(1)}, bf16[64,512]{1,0:T(8,128)(2,1)S(1)}, u32[]{:S(2)}, u32[]{:S(2)}) collective-permute-start(bf16[64,512]{1,0:T(8,128)(2,1)S(1)} %get-tuple-element.52), channel_id=1, source_target_pairs={{0,8},{4,20},{8,0},{12,28},{16,24},{20,4},{24,16},{28,12},{1,9},{5... | collective-permute-start | bytes 196616 | tf_op jit(solution)/shard_map/ppermute | solution.py:256
  17.1 4.3 %collective-permute-start.6 = (bf16[64,512]{1,0:T(8,128)(2,1)S(1)}, bf16[64,512]{1,0:T(8,128)(2,1)S(1)}, u32[]{:S(2)}, u32[]{:S(2)}) collective-permute-start(bf16[64,512]{1,0:T(8,128)(2,1)S(1)} %get-tuple-element.59), channel_id=1, source_target_pairs={{0,8},{4,20},{8,0},{12,28},{16,24},{20,4},{24,16},{28,12},{1,9},{5... | collective-permute-start | bytes 196616 | tf_op jit(solution)/shard_map/ppermute | solution.py:256
  19.1 6.0 %collective-permute-start.5 = (bf16[64,512]{1,0:T(8,128)(2,1)S(1)}, bf16[64,512]{1,0:T(8,128)(2,1)S(1)}, u32[]{:S(2)}, u32[]{:S(2)}) collective-permute-start(bf16[64,512]{1,0:T(8,128)(2,1)S(1)} %get-tuple-element.54), channel_id=1, source_target_pairs={{0,16},{4,12},{8,24},{12,4},{16,0},{20,28},{24,8},{28,20},{1,17},{... | collective-permute-start | bytes 196616 | tf_op jit(solution)/shard_map/ppermute | solution.py:256
  21.4 5.5 %collective-permute-start.7 = (bf16[64,512]{1,0:T(8,128)(2,1)S(1)}, bf16[64,512]{1,0:T(8,128)(2,1)S(1)}, u32[]{:S(2)}, u32[]{:S(2)}) collective-permute-start(bf16[64,512]{1,0:T(8,128)(2,1)S(1)} %get-tuple-element.61), channel_id=1, source_target_pairs={{0,16},{4,12},{8,24},{12,4},{16,0},{20,28},{24,8},{28,20},{1,17},{... | collective-permute-start | bytes 196616 | tf_op jit(solution)/shard_map/ppermute | solution.py:256
  27.0 1.4 %collective-permute-start.8 = (bf16[64,1024]{1,0:T(8,128)(2,1)S(1)}, bf16[64,1024]{1,0:T(8,128)(2,1)S(1)}, u32[]{:S(2)}, u32[]{:S(2)}) collective-permute-start(bf16[64,1024]{1,0:T(8,128)(2,1)S(1)} %shard_map.109.w_ref), channel_id=1, source_target_pairs={{0,4},{4,0},{8,12},{12,8},{16,20},{20,16},{24,28},{28,24},{1,5},{5... | collective-permute-start | bytes 393224 | tf_op jit(solution)/shard_map/ppermute | solution.py:242
  28.4 4.2 %copy-start = (bf16[128,256]{1,0:T(8,128)(2,1)S(1)}, bf16[128,256]{1,0:T(8,128)(2,1)}, u32[]{:S(2)}) copy-start(bf16[128,256]{1,0:T(8,128)(2,1)} %w_feat_ref.1) | copy-start | bytes 196612
  28.4 7.5 %copy-start.1 = (bf16[256,128]{1,0:T(8,128)(2,1)S(1)}, bf16[256,128]{1,0:T(8,128)(2,1)}, u32[]{:S(2)}) copy-start(bf16[256,128]{1,0:T(8,128)(2,1)} %w_out_ref.1) | copy-start | bytes 196612
  28.4 7.5 %copy-start.2 = (bf16[64,256]{1,0:T(8,128)(2,1)S(1)}, bf16[64,256]{1,0:T(8,128)(2,1)}, u32[]{:S(2)}) copy-start(bf16[64,256]{1,0:T(8,128)(2,1)} %w_pot_ref.1) | copy-start | bytes 98308
  29.1 5.3 %collective-permute-start.9 = (bf16[64,512]{1,0:T(8,128)(2,1)S(1)}, bf16[64,512]{1,0:T(8,128)(2,1)S(1)}, u32[]{:S(2)}, u32[]{:S(2)}) collective-permute-start(bf16[64,512]{1,0:T(8,128)(2,1)S(1)} %get-tuple-element.72), channel_id=1, source_target_pairs={{0,3},{1,2},{2,1},{3,0},{4,5},{5,4},{6,7},{7,6},{8,11},{9,10},{10,... | collective-permute-start | bytes 196616 | tf_op jit(solution)/shard_map/ppermute | solution.py:249
  30.7 5.1 %collective-permute-start.10 = (bf16[64,512]{1,0:T(8,128)(2,1)S(1)}, bf16[64,512]{1,0:T(8,128)(2,1)S(1)}, u32[]{:S(2)}, u32[]{:S(2)}) collective-permute-start(bf16[64,512]{1,0:T(8,128)(2,1)S(1)} %get-tuple-element.73), channel_id=1, source_target_pairs={{0,2},{1,3},{2,0},{3,1},{4,6},{5,7},{6,4},{7,5},{8,10},{9,11},{10,... | collective-permute-start | bytes 196616 | tf_op jit(solution)/shard_map/ppermute | solution.py:249
  31.6 4.3 %collective-permute-start.11 = (bf16[64,512]{1,0:T(8,128)(2,1)S(1)}, bf16[64,512]{1,0:T(8,128)(2,1)S(1)}, u32[]{:S(2)}, u32[]{:S(2)}) collective-permute-start(bf16[64,512]{1,0:T(8,128)(2,1)S(1)} %get-tuple-element.74), channel_id=1, source_target_pairs={{0,1},{1,0},{2,3},{3,2},{4,7},{5,6},{6,5},{7,4},{8,9},{9,8},{10,11... | collective-permute-start | bytes 196616 | tf_op jit(solution)/shard_map/ppermute | solution.py:249

commit v5 on v4

--- a/solution.py
+++ b/solution.py
@@ -143,9 +143,13 @@
     for c in range(span // tile):
         n = n_ref[start + c * tile : start + (c + 1) * tile, :]
         lo, hi = 2 * c * tile, 2 * (c + 1) * tile
+        total = s_in_ref[:, s_start + lo : s_start + hi]
         for b, message_ref in enumerate(messages):
             put_phases(p_ref, lo, tile, b * atoms, n, message_ref[q:, :])
-        total = s_in_ref[:, s_start + lo : s_start + hi] + nt(charges[...], p_ref[lo:hi, :])
+            if b == len(messages) - 2:
+                total = total + nt(charges[:, : (b + 1) * atoms], p_ref[lo:hi, : (b + 1) * atoms])
+        at = (len(messages) - 1) * atoms
+        total = total + nt(charges[:, at:], p_ref[lo:hi, at:])
         s_ref[:, lo:hi] = total.astype(s_ref.dtype)
 
 

time: 37.1 us -> 37 us (level)
  no operation moved by 1% of the time
where the time goes in v5:
time: 37 us; the launch traced here: 36.9 us
  starting transfers between devices  15.7 us (42%)
  Pallas kernels  11.6 us (31%)
  waiting for transfers between devices  9.45 us (26%)
    pallas_call x14, Pallas kernels, call(): pl.pallas_call(kernel, out_shape=outs, in_specs=[pl.BlockSpec(memory_spac...  11.6 us
    ppermute x4, starting transfers between devices, z_swap(): lax.ppermute(value, 'atom', [(i, i ^ bits[step if i % CORES == 0 else ste...  7.43 us
    ppermute x5, starting transfers between devices, swap(): return lax.ppermute(value, axis, [(i, i ^ bit) for i in range(count)])  4.74 us
    ppermute x4, waiting for transfers between devices, z_swap(): lax.ppermute(value, 'atom', [(i, i ^ bits[step if i % CORES == 0 else ste...  4.05 us
    ppermute x3, starting transfers between devices, wave_swap(): return lax.ppermute(value, ('atom', 'wave'), pairs)  3.55 us
    ppermute x3, waiting for transfers between devices, wave_swap(): return lax.ppermute(value, ('atom', 'wave'), pairs)  2.84 us
    ppermute x5, waiting for transfers between devices, swap(): return lax.ppermute(value, axis, [(i, i ^ bit) for i in range(count)])  2.56 us
  transfers between devices with their start and end apart: 12, of which 10 were waited for; matrix products, arithmetic and copies ran while one was open for 0% of the time, Pallas kernels for 17%

profile of v5, /device:TPU:0, one launch (start us, length us, event | category | flops | bytes accessed | tf_op | source)
XLA Modules:
  0.0 36.9 jit_solution(3443410891993766566)
XLA Ops:
  0.0 1.4 %shard_map.100 = (bf16[512,128]{1,0:T(8,128)(2,1)S(1)}, bf16[512,128]{1,0:T(8,128)(2,1)S(1)}, bf16[80,512]{1,0:T(8,128)(2,1)S(1)}, s32[3,1024]{1,0:T(4,128)S(1)}, f32[1,1024]{1,0:T(1,128)S(1)}) custom-call(bf16[512,128]{1,0:T(8,128)(2,1)} %features_ref.1, s32[1,512]{1,0:T(1,128)} %bitcast.5, f32[3,512]{1,0:T(4,128)} %coords_ref.1, s32[3,1024]{1,0:T(4,128)} %waves_ref.1, ...), custom_call_target="tpu_custom_call" | custom-call | bytes 536576 | tf_op jit(solution)/shard_map/pallas_call | solution.py:233
  1.4 4.0 %collective-permute-start.2 = (bf16[80,512]{1,0:T(8,128)(2,1)S(1)}, bf16[80,512]{1,0:T(8,128)(2,1)S(1)}, u32[]{:S(2)}, u32[]{:S(2)}) collective-permute-start(bf16[80,512]{1,0:T(8,128)(2,1)S(1)} %get-tuple-element.43.message_ref), channel_id=1, source_target_pairs={{0,3},{1,2},{2,1},{3,0},{4,7},{5,6},{6,5},{7,4},{8,11},{9,10},{10,... | collective-permute-start | bytes 245768 | tf_op jit(solution)/shard_map/ppermute | solution.py:246
  5.3 0.5 %collective-permute-start.1 = (bf16[80,512]{1,0:T(8,128)(2,1)S(1)}, bf16[80,512]{1,0:T(8,128)(2,1)S(1)}, u32[]{:S(2)}, u32[]{:S(2)}) collective-permute-start(bf16[80,512]{1,0:T(8,128)(2,1)S(1)} %get-tuple-element.43.message_ref), channel_id=1, source_target_pairs={{0,2},{1,3},{2,0},{3,1},{4,6},{5,7},{6,4},{7,5},{8,10},{9,11},{10,... | collective-permute-start | bytes 245768 | tf_op jit(solution)/shard_map/ppermute | solution.py:246
  5.8 0.1 collective-permute-start
  6.0 2.3 %shard_map.101 = (bf16[1024,16]{1,0:T(8,128)(2,1)S(1)}, f32[1,1024]{1,0:T(1,128)S(1)}, bf16[1024,512]{1,0:T(8,128)(2,1)S(1)}, bf16[1024,512]{1,0:T(8,128)(2,1)S(...) custom-call(s32[3,1024]{1,0:T(4,128)S(1)} %get-tuple-element.41.waves_ref, ...), custom_call_target="tpu_custom_call" | custom-call | flops 134217728 | bytes 2756608 | tf_op jit(solution)/shard_map/pallas_call | solution.py:233
  8.2 0.0 collective-permute-done.2.refs_4_
  8.3 1.5 %collective-permute-done.1.refs_3_ = bf16[80,512]{1,0:T(8,128)(2,1)S(1)} collective-permute-done((bf16[80,512]{1,0:T(8,128)(2,1)S(1)}, bf16[80,512]{1,0:T(8,128)(2,1)S(1)}, u32[]{:S(2)}, u32[]{:S(2)}) %collective-permute-start.1) | collective-permute-done | bytes 81952 | tf_op jit(solution)/shard_map/ppermute | solution.py:246
  9.8 0.5 %collective-permute-done.refs_2_ = bf16[80,512]{1,0:T(8,128)(2,1)S(1)} collective-permute-done((bf16[80,512]{1,0:T(8,128)(2,1)S(1)}, bf16[80,512]{1,0:T(8,128)(2,1)S(1)}, u32[]{:S(2)}, u32[]{:S(2)}) %collective-permute-start) | collective-permute-done | bytes 81952 | tf_op jit(solution)/shard_map/ppermute | solution.py:246
  10.3 2.3 %shard_map.103 = (bf16[1024,1536]{1,0:T(8,128)(2,1)S(1)}, bf16[64,1024]{1,0:T(8,128)(2,1)S(1)}) custom-call(bf16[1024,16]{1,0:T(8,128)(2,1)S(1)} %get-tuple-element.55.refs_0_, f32[64,1024]{1,0:T(8,128)S(1)} %get-tuple-element.48.refs_1_, bf16[80,512]{1,0:T(8,128)(2,1)S(1)} %collective-permute-done.refs_2_, ...), custom_call_target="tpu_custom_call" | custom-call | flops 201326592 | bytes 3817472 | tf_op jit(solution)/shard_map/pallas_call | solution.py:233
  12.6 0.1 collective-permute-start.3
  12.7 1.3 %shard_map.102 = (bf16[512,1536]{1,0:T(8,128)(2,1)S(1)}, f32[64,512]{1,0:T(8,128)S(1)}) custom-call(bf16[1024,16]{1,0:T(8,128)(2,1)S(1)} %get-tuple-element.55.refs_0_, f32[64,1024]{1,0:T(8,128)S(1)} %get-tuple-element.46.refs_1_, bf16[80,512]{1,0:T(8,128)(2,1)S(1)} %collective-permute-done.refs_2_, bf16[80,512]{1,0:T(8,128)(2,1)S(1)} %collective-permute-done.1.refs_3_, ...), custom_call_target="tpu_custom_call" | custom-call | flops 100663296 | bytes 2244608 | tf_op jit(solution)/shard_map/pallas_call | solution.py:233
  14.0 0.0 collective-permute-done.3.refs_1_
  14.0 1.6 %collective-permute-start.4 = (bf16[64,512]{1,0:T(8,128)(2,1)S(1)}, bf16[64,512]{1,0:T(8,128)(2,1)S(1)}, u32[]{:S(2)}, u32[]{:S(2)}) collective-permute-start(bf16[64,512]{1,0:T(8,128)(2,1)S(1)} %get-tuple-element.52), channel_id=1, source_target_pairs={{0,8},{4,20},{8,0},{12,28},{16,24},{20,4},{24,16},{28,12},{1,9},{5... | collective-permute-start | bytes 196616 | tf_op jit(solution)/shard_map/ppermute | solution.py:260
  15.7 1.3 %shard_map.106 = (bf16[512,1536]{1,0:T(8,128)(2,1)S(1)}, f32[64,512]{1,0:T(8,128)S(1)}) custom-call(bf16[1024,16]{1,0:T(8,128)(2,1)S(1)} %get-tuple-element.55.refs_0_, f32[64,1024]{1,0:T(8,128)S(1)} %get-tuple-element.46.refs_1_, bf16[80,512]{1,0:T(8,128)(2,1)S(1)} %collective-permute-done.refs_2_, bf16[80,512]{1,0:T(8,128)(2,1)S(1)} %collective-permute-done.1.refs_3_, ...), custom_call_target="tpu_custom_call" | custom-call | flops 100663296 | bytes 2244608 | tf_op jit(solution)/shard_map/pallas_call | solution.py:233
  17.0 0.5 %collective-permute-start.6 = (bf16[64,512]{1,0:T(8,128)(2,1)S(1)}, bf16[64,512]{1,0:T(8,128)(2,1)S(1)}, u32[]{:S(2)}, u32[]{:S(2)}) collective-permute-start(bf16[64,512]{1,0:T(8,128)(2,1)S(1)} %get-tuple-element.59), channel_id=1, source_target_pairs={{0,8},{4,20},{8,0},{12,28},{16,24},{20,4},{24,16},{28,12},{1,9},{5... | collective-permute-start | bytes 196616 | tf_op jit(solution)/shard_map/ppermute | solution.py:260
  17.5 1.5 %collective-permute-done.4.refs_1_ = bf16[64,512]{1,0:T(8,128)(2,1)S(1)} collective-permute-done((bf16[64,512]{1,0:T(8,128)(2,1)S(1)}, bf16[64,512]{1,0:T(8,128)(2,1)S(1)}, u32[]{:S(2)}, u32[]{:S(2)}) %collective-permute-start.4) | collective-permute-done | bytes 65568 | tf_op jit(solution)/shard_map/ppermute | solution.py:260
  19.1 2.1 %collective-permute-start.5 = (bf16[64,512]{1,0:T(8,128)(2,1)S(1)}, bf16[64,512]{1,0:T(8,128)(2,1)S(1)}, u32[]{:S(2)}, u32[]{:S(2)}) collective-permute-start(bf16[64,512]{1,0:T(8,128)(2,1)S(1)} %get-tuple-element.54), channel_id=1, source_target_pairs={{0,16},{4,12},{8,24},{12,4},{16,0},{20,28},{24,8},{28,20},{1,17},{... | collective-permute-start | bytes 196616 | tf_op jit(solution)/shard_map/ppermute | solution.py:260
  21.1 0.2 collective-permute-done.6.refs_1_
  21.3 3.2 %collective-permute-start.7 = (bf16[64,512]{1,0:T(8,128)(2,1)S(1)}, bf16[64,512]{1,0:T(8,128)(2,1)S(1)}, u32[]{:S(2)}, u32[]{:S(2)}) collective-permute-start(bf16[64,512]{1,0:T(8,128)(2,1)S(1)} %get-tuple-element.61), channel_id=1, source_target_pairs={{0,16},{4,12},{8,24},{12,4},{16,0},{20,28},{24,8},{28,20},{1,17},{... | collective-permute-start | bytes 196616 | tf_op jit(solution)/shard_map/ppermute | solution.py:260
  24.6 0.4 %collective-permute-done.5.refs_2_ = bf16[64,512]{1,0:T(8,128)(2,1)S(1)} collective-permute-done((bf16[64,512]{1,0:T(8,128)(2,1)S(1)}, bf16[64,512]{1,0:T(8,128)(2,1)S(1)}, u32[]{:S(2)}, u32[]{:S(2)}) %collective-permute-start.5) | collective-permute-done | bytes 65568 | tf_op jit(solution)/shard_map/ppermute | solution.py:260
  25.0 1.9 %collective-permute-done.7.refs_4_ = bf16[64,512]{1,0:T(8,128)(2,1)S(1)} collective-permute-done((bf16[64,512]{1,0:T(8,128)(2,1)S(1)}, bf16[64,512]{1,0:T(8,128)(2,1)S(1)}, u32[]{:S(2)}, u32[]{:S(2)}) %collective-permute-start.7) | collective-permute-done | bytes 65568 | tf_op jit(solution)/shard_map/ppermute | solution.py:260
  26.9 0.1 collective-permute-start.8
  27.0 0.8 %shard_map.110 = (f32[64,512]{1,0:T(8,128)S(1)}, f32[64,1536]{1,0:T(8,128)S(1)}) custom-call(bf16[64,1024]{1,0:T(8,128)(2,1)S(1)} %shard_map.109.w_ref, bf16[1024,512]{1,0:T(8,128)(2,1)S(1)} %get-tuple-element.63.p0_ref, bf16[512,1536]{1,0:T(8,128)(2,1)S(1)} %get-tuple-element.64.refs_0_, bf16[512,1536]{1,0:T(8,128)(2,1)S(1)} %get-tuple-element.65.refs_1_), custom_call_target="tpu_custom_call" | custom-call | flops 268435456 | bytes 4849664 | tf_op jit(solution)/shard_map/pallas_call | solution.py:233
  27.8 0.5 %collective-permute-done.8.w_ref = bf16[64,1024]{1,0:T(8,128)(2,1)S(1)} collective-permute-done((bf16[64,1024]{1,0:T(8,128)(2,1)S(1)}, bf16[64,1024]{1,0:T(8,128)(2,1)S(1)}, u32[]{:S(2)}, u32[]{:S(2)}) %collective-permute-start.8) | collective-permute-done | bytes 131104 | tf_op jit(solution)/shard_map/ppermute | solution.py:246
  28.3 0.0 copy-start
  28.3 0.0 copy-start.1
  28.3 0.0 copy-start.2
  28.3 0.7 %shard_map.112 = (bf16[64,512]{1,0:T(8,128)(2,1)S(1)}, bf16[64,512]{1,0:T(8,128)(2,1)S(1)}, bf16[64,512]{1,0:T(8,128)(2,1)S(1)}) custom-call(bf16[64,1024]{1,0:T(8,128)(2,1)S(1)} %collective-permute-done.8.w_ref, bf16[1024,1536]{1,0:T(8,128)(2,1)S(1)} %get-tuple-element.70.p_ref, f32[64,1536]{1,0:T(8,128)S(1)} %get-tuple-element.71.rest_ref), custom_call_target="tpu_custom_call" | custom-call | flops 201326592 | bytes 3866624 | tf_op jit(solution)/shard_map/pallas_call | solution.py:233
  29.0 1.6 %collective-permute-start.9 = (bf16[64,512]{1,0:T(8,128)(2,1)S(1)}, bf16[64,512]{1,0:T(8,128)(2,1)S(1)}, u32[]{:S(2)}, u32[]{:S(2)}) collective-permute-start(bf16[64,512]{1,0:T(8,128)(2,1)S(1)} %get-tuple-element.72), channel_id=1, source_target_pairs={{0,3},{1,2},{2,1},{3,0},{4,5},{5,4},{6,7},{7,6},{8,11},{9,10},{10,... | collective-permute-start | bytes 196616 | tf_op jit(solution)/shard_map/ppermute | solution.py:253
  30.6 1.0 %collective-permute-start.10 = (bf16[64,512]{1,0:T(8,128)(2,1)S(1)}, bf16[64,512]{1,0:T(8,128)(2,1)S(1)}, u32[]{:S(2)}, u32[]{:S(2)}) collective-permute-start(bf16[64,512]{1,0:T(8,128)(2,1)S(1)} %get-tuple-element.73), channel_id=1, source_target_pairs={{0,2},{1,3},{2,0},{3,1},{4,6},{5,7},{6,4},{7,5},{8,10},{9,11},{10,... | collective-permute-start | bytes 196616 | tf_op jit(solution)/shard_map/ppermute | solution.py:253
  31.5 1.0 %collective-permute-start.11 = (bf16[64,512]{1,0:T(8,128)(2,1)S(1)}, bf16[64,512]{1,0:T(8,128)(2,1)S(1)}, u32[]{:S(2)}, u32[]{:S(2)}) collective-permute-start(bf16[64,512]{1,0:T(8,128)(2,1)S(1)} %get-tuple-element.74), channel_id=1, source_target_pairs={{0,1},{1,0},{2,3},{3,2},{4,7},{5,6},{6,5},{7,4},{8,9},{9,8},{10,11... | collective-permute-start | bytes 196616 | tf_op jit(solution)/shard_map/ppermute | solution.py:253
  32.6 0.0 copy-done
  32.6 0.4 %shard_map.111 = (f32[64,512]{1,0:T(8,128)S(1)}, f32[512,256]{1,0:T(8,128)S(1)}) custom-call(bf16[64,1024]{1,0:T(8,128)(2,1)S(1)} %collective-permute-done.8.w_ref, bf16[1024,512]{1,0:T(8,128)(2,1)S(1)} %get-tuple-element.62.p0_ref, f32[64,512]{1,0:T(8,128)S(1)} %get-tuple-element.66.own_ref, bf16[512,128]{1,0:T(8,128)(2,1)S(1)} %get-tuple-element.67.mixed_ref, ...), custom_call_target="tpu_custom_call" | custom-call | flops 67108864 | bytes 2162688 | tf_op jit(solution)/shard_map/pallas_call | solution.py:233
  32.9 1.4 %collective-permute-done.9.refs_0_ = bf16[64,512]{1,0:T(8,128)(2,1)S(1)} collective-permute-done((bf16[64,512]{1,0:T(8,128)(2,1)S(1)}, bf16[64,512]{1,0:T(8,128)(2,1)S(1)}, u32[]{:S(2)}, u32[]{:S(2)}) %collective-permute-start.9) | collective-permute-done | bytes 65568 | tf_op jit(solution)/shard_map/ppermute | solution.py:253
  34.3 1.3 %collective-permute-done.10.refs_1_ = bf16[64,512]{1,0:T(8,128)(2,1)S(1)} collective-permute-done((bf16[64,512]{1,0:T(8,128)(2,1)S(1)}, bf16[64,512]{1,0:T(8,128)(2,1)S(1)}, u32[]{:S(2)}, u32[]{:S(2)}) %collective-permute-start.10) | collective-permute-done | bytes 65568 | tf_op jit(solution)/shard_map/ppermute | solution.py:253
  35.6 0.1 collective-permute-done.11.refs_2_
  35.8 0.0 copy-done.1
  35.8 0.0 copy-done.2
  35.8 1.1 %shard_map.113 = bf16[512,128]{1,0:T(8,128)(2,1)} custom-call(bf16[512,128]{1,0:T(8,128)(2,1)S(1)} %get-tuple-element.40.hidden_ref, f32[64,512]{1,0:T(8,128)S(1)} %get-tuple-element.68.total_ref, f32[512,256]{1,0:T(8,128)S(1)} %get-tuple-element.69.pre_ref, bf16[64,256]{1,0:T(8,128)(2,1)S(1)} %copy-done.2, bf16[256,128]{1,0:T(8,128)(2,1)S(1)} %copy-done.1, ...), custom_call_target="tpu_custom_call" | custom-call | bytes 1212416 | tf_op jit(solution)/shard_map/pallas_call | solution.py:233
  (5 shorter events, 0.1 us)
Async XLA Ops:
  1.4 6.9 %collective-permute-start.2 = (bf16[80,512]{1,0:T(8,128)(2,1)S(1)}, bf16[80,512]{1,0:T(8,128)(2,1)S(1)}, u32[]{:S(2)}, u32[]{:S(2)}) collective-permute-start(bf16[80,512]{1,0:T(8,128)(2,1)S(1)} %get-tuple-element.43.message_ref), channel_id=1, source_target_pairs={{0,3},{1,2},{2,1},{3,0},{4,7},{5,6},{6,5},{7,4},{8,11},{9,10},{10,... | collective-permute-start | bytes 245768 | tf_op jit(solution)/shard_map/ppermute | solution.py:246
  5.3 4.4 %collective-permute-start.1 = (bf16[80,512]{1,0:T(8,128)(2,1)S(1)}, bf16[80,512]{1,0:T(8,128)(2,1)S(1)}, u32[]{:S(2)}, u32[]{:S(2)}) collective-permute-start(bf16[80,512]{1,0:T(8,128)(2,1)S(1)} %get-tuple-element.43.message_ref), channel_id=1, source_target_pairs={{0,2},{1,3},{2,0},{3,1},{4,6},{5,7},{6,4},{7,5},{8,10},{9,11},{10,... | collective-permute-start | bytes 245768 | tf_op jit(solution)/shard_map/ppermute | solution.py:246
  5.8 4.4 %collective-permute-start = (bf16[80,512]{1,0:T(8,128)(2,1)S(1)}, bf16[80,512]{1,0:T(8,128)(2,1)S(1)}, u32[]{:S(2)}, u32[]{:S(2)}) collective-permute-start(bf16[80,512]{1,0:T(8,128)(2,1)S(1)} %get-tuple-element.43.message_ref), channel_id=1, source_target_pairs={{0,1},{1,0},{2,3},{3,2},{4,5},{5,4},{6,7},{7,6},{8,9},{9,8},{10,11... | collective-permute-start | bytes 245768 | tf_op jit(solution)/shard_map/ppermute | solution.py:246
  12.6 1.4 %collective-permute-start.3 = (bf16[64,1024]{1,0:T(8,128)(2,1)S(1)}, bf16[64,1024]{1,0:T(8,128)(2,1)S(1)}, u32[]{:S(2)}, u32[]{:S(2)}) collective-permute-start(bf16[64,1024]{1,0:T(8,128)(2,1)S(1)} %get-tuple-element.49), channel_id=1, source_target_pairs={{0,4},{4,0},{8,12},{12,8},{16,20},{20,16},{24,28},{28,24},{1,5},{5... | collective-permute-start | bytes 393224 | tf_op jit(solution)/shard_map/ppermute | solution.py:246
  14.0 5.0 %collective-permute-start.4 = (bf16[64,512]{1,0:T(8,128)(2,1)S(1)}, bf16[64,512]{1,0:T(8,128)(2,1)S(1)}, u32[]{:S(2)}, u32[]{:S(2)}) collective-permute-start(bf16[64,512]{1,0:T(8,128)(2,1)S(1)} %get-tuple-element.52), channel_id=1, source_target_pairs={{0,8},{4,20},{8,0},{12,28},{16,24},{20,4},{24,16},{28,12},{1,9},{5... | collective-permute-start | bytes 196616 | tf_op jit(solution)/shard_map/ppermute | solution.py:260
  17.0 4.3 %collective-permute-start.6 = (bf16[64,512]{1,0:T(8,128)(2,1)S(1)}, bf16[64,512]{1,0:T(8,128)(2,1)S(1)}, u32[]{:S(2)}, u32[]{:S(2)}) collective-permute-start(bf16[64,512]{1,0:T(8,128)(2,1)S(1)} %get-tuple-element.59), channel_id=1, source_target_pairs={{0,8},{4,20},{8,0},{12,28},{16,24},{20,4},{24,16},{28,12},{1,9},{5... | collective-permute-start | bytes 196616 | tf_op jit(solution)/shard_map/ppermute | solution.py:260
  19.1 5.9 %collective-permute-start.5 = (bf16[64,512]{1,0:T(8,128)(2,1)S(1)}, bf16[64,512]{1,0:T(8,128)(2,1)S(1)}, u32[]{:S(2)}, u32[]{:S(2)}) collective-permute-start(bf16[64,512]{1,0:T(8,128)(2,1)S(1)} %get-tuple-element.54), channel_id=1, source_target_pairs={{0,16},{4,12},{8,24},{12,4},{16,0},{20,28},{24,8},{28,20},{1,17},{... | collective-permute-start | bytes 196616 | tf_op jit(solution)/shard_map/ppermute | solution.py:260
  21.3 5.5 %collective-permute-start.7 = (bf16[64,512]{1,0:T(8,128)(2,1)S(1)}, bf16[64,512]{1,0:T(8,128)(2,1)S(1)}, u32[]{:S(2)}, u32[]{:S(2)}) collective-permute-start(bf16[64,512]{1,0:T(8,128)(2,1)S(1)} %get-tuple-element.61), channel_id=1, source_target_pairs={{0,16},{4,12},{8,24},{12,4},{16,0},{20,28},{24,8},{28,20},{1,17},{... | collective-permute-start | bytes 196616 | tf_op jit(solution)/shard_map/ppermute | solution.py:260
  26.9 1.4 %collective-permute-start.8 = (bf16[64,1024]{1,0:T(8,128)(2,1)S(1)}, bf16[64,1024]{1,0:T(8,128)(2,1)S(1)}, u32[]{:S(2)}, u32[]{:S(2)}) collective-permute-start(bf16[64,1024]{1,0:T(8,128)(2,1)S(1)} %shard_map.109.w_ref), channel_id=1, source_target_pairs={{0,4},{4,0},{8,12},{12,8},{16,20},{20,16},{24,28},{28,24},{1,5},{5... | collective-permute-start | bytes 393224 | tf_op jit(solution)/shard_map/ppermute | solution.py:246
  28.3 4.2 %copy-start = (bf16[128,256]{1,0:T(8,128)(2,1)S(1)}, bf16[128,256]{1,0:T(8,128)(2,1)}, u32[]{:S(2)}) copy-start(bf16[128,256]{1,0:T(8,128)(2,1)} %w_feat_ref.1) | copy-start | bytes 196612
  28.3 7.5 %copy-start.1 = (bf16[256,128]{1,0:T(8,128)(2,1)S(1)}, bf16[256,128]{1,0:T(8,128)(2,1)}, u32[]{:S(2)}) copy-start(bf16[256,128]{1,0:T(8,128)(2,1)} %w_out_ref.1) | copy-start | bytes 196612
  28.3 7.5 %copy-start.2 = (bf16[64,256]{1,0:T(8,128)(2,1)S(1)}, bf16[64,256]{1,0:T(8,128)(2,1)}, u32[]{:S(2)}) copy-start(bf16[64,256]{1,0:T(8,128)(2,1)} %w_pot_ref.1) | copy-start | bytes 98308
  29.0 5.3 %collective-permute-start.9 = (bf16[64,512]{1,0:T(8,128)(2,1)S(1)}, bf16[64,512]{1,0:T(8,128)(2,1)S(1)}, u32[]{:S(2)}, u32[]{:S(2)}) collective-permute-start(bf16[64,512]{1,0:T(8,128)(2,1)S(1)} %get-tuple-element.72), channel_id=1, source_target_pairs={{0,3},{1,2},{2,1},{3,0},{4,5},{5,4},{6,7},{7,6},{8,11},{9,10},{10,... | collective-permute-start | bytes 196616 | tf_op jit(solution)/shard_map/ppermute | solution.py:253
  30.6 5.1 %collective-permute-start.10 = (bf16[64,512]{1,0:T(8,128)(2,1)S(1)}, bf16[64,512]{1,0:T(8,128)(2,1)S(1)}, u32[]{:S(2)}, u32[]{:S(2)}) collective-permute-start(bf16[64,512]{1,0:T(8,128)(2,1)S(1)} %get-tuple-element.73), channel_id=1, source_target_pairs={{0,2},{1,3},{2,0},{3,1},{4,6},{5,7},{6,4},{7,5},{8,10},{9,11},{10,... | collective-permute-start | bytes 196616 | tf_op jit(solution)/shard_map/ppermute | solution.py:253
  31.5 4.3 %collective-permute-start.11 = (bf16[64,512]{1,0:T(8,128)(2,1)S(1)}, bf16[64,512]{1,0:T(8,128)(2,1)S(1)}, u32[]{:S(2)}, u32[]{:S(2)}) collective-permute-start(bf16[64,512]{1,0:T(8,128)(2,1)S(1)} %get-tuple-element.74), channel_id=1, source_target_pairs={{0,1},{1,0},{2,3},{3,2},{4,7},{5,6},{6,5},{7,4},{8,9},{9,8},{10,11... | collective-permute-start | bytes 196616 | tf_op jit(solution)/shard_map/ppermute | solution.py:253

commit v6 on v5

--- a/solution.py
+++ b/solution.py
@@ -332,7 +332,6 @@
         total, send = join([F32, BF16], total, got, offset=i * rows)
         sums.append(total)
         arrived.append(z_swap(send, 0))
-        n, sums[-1] = lax.optimization_barrier((n, sums[-1]))
     for step in range(1, zcount.bit_length() - 1):
         for i in range(pieces):
             sums[i], send = join([F32, BF16], sums[i], arrived[i])

time: 37 us -> 37 us (level)
  no operation moved by 1% of the time
where the time goes in v6:
time: 37 us; the launch traced here: 36.9 us
  starting transfers between devices  15.7 us (42%)
  Pallas kernels  11.6 us (31%)
  waiting for transfers between devices  9.45 us (26%)
    pallas_call x14, Pallas kernels, call(): pl.pallas_call(kernel, out_shape=outs, in_specs=[pl.BlockSpec(memory_spac...  11.6 us
    ppermute x4, starting transfers between devices, z_swap(): lax.ppermute(value, 'atom', [(i, i ^ bits[step if i % CORES == 0 else ste...  7.44 us
    ppermute x5, starting transfers between devices, swap(): return lax.ppermute(value, axis, [(i, i ^ bit) for i in range(count)])  4.74 us
    ppermute x4, waiting for transfers between devices, z_swap(): lax.ppermute(value, 'atom', [(i, i ^ bits[step if i % CORES == 0 else ste...  4.05 us
    ppermute x3, starting transfers between devices, wave_swap(): return lax.ppermute(value, ('atom', 'wave'), pairs)  3.55 us
    ppermute x3, waiting for transfers between devices, wave_swap(): return lax.ppermute(value, ('atom', 'wave'), pairs)  2.84 us
    ppermute x5, waiting for transfers between devices, swap(): return lax.ppermute(value, axis, [(i, i ^ bit) for i in range(count)])  2.57 us
  transfers between devices with their start and end apart: 12, of which 10 were waited for; matrix products, arithmetic and copies ran while one was open for 0% of the time, Pallas kernels for 17%

profile of v6, /device:TPU:0, one launch (start us, length us, event | category | flops | bytes accessed | tf_op | source)
XLA Modules:
  0.0 36.9 jit_solution(14499346439258224079)
XLA Ops:
  0.0 1.4 %shard_map.100 = (bf16[512,128]{1,0:T(8,128)(2,1)S(1)}, bf16[512,128]{1,0:T(8,128)(2,1)S(1)}, bf16[80,512]{1,0:T(8,128)(2,1)S(1)}, s32[3,1024]{1,0:T(4,128)S(1)}, f32[1,1024]{1,0:T(1,128)S(1)}) custom-call(bf16[512,128]{1,0:T(8,128)(2,1)} %features_ref.1, s32[1,512]{1,0:T(1,128)} %bitcast.5, f32[3,512]{1,0:T(4,128)} %coords_ref.1, s32[3,1024]{1,0:T(4,128)} %waves_ref.1, ...), custom_call_target="tpu_custom_call" | custom-call | bytes 536576 | tf_op jit(solution)/shard_map/pallas_call | solution.py:233
  1.4 4.0 %collective-permute-start.2 = (bf16[80,512]{1,0:T(8,128)(2,1)S(1)}, bf16[80,512]{1,0:T(8,128)(2,1)S(1)}, u32[]{:S(2)}, u32[]{:S(2)}) collective-permute-start(bf16[80,512]{1,0:T(8,128)(2,1)S(1)} %get-tuple-element.40.message_ref), channel_id=1, source_target_pairs={{0,3},{1,2},{2,1},{3,0},{4,7},{5,6},{6,5},{7,4},{8,11},{9,10},{10,... | collective-permute-start | bytes 245768 | tf_op jit(solution)/shard_map/ppermute | solution.py:246
  5.3 0.5 %collective-permute-start.1 = (bf16[80,512]{1,0:T(8,128)(2,1)S(1)}, bf16[80,512]{1,0:T(8,128)(2,1)S(1)}, u32[]{:S(2)}, u32[]{:S(2)}) collective-permute-start(bf16[80,512]{1,0:T(8,128)(2,1)S(1)} %get-tuple-element.40.message_ref), channel_id=1, source_target_pairs={{0,2},{1,3},{2,0},{3,1},{4,6},{5,7},{6,4},{7,5},{8,10},{9,11},{10,... | collective-permute-start | bytes 245768 | tf_op jit(solution)/shard_map/ppermute | solution.py:246
  5.8 0.1 collective-permute-start
  6.0 2.3 %shard_map.101 = (bf16[1024,16]{1,0:T(8,128)(2,1)S(1)}, f32[1,1024]{1,0:T(1,128)S(1)}, bf16[1024,512]{1,0:T(8,128)(2,1)S(1)}, bf16[1024,512]{1,0:T(8,128)(2,1)S(...) custom-call(s32[3,1024]{1,0:T(4,128)S(1)} %get-tuple-element.38.waves_ref, ...), custom_call_target="tpu_custom_call" | custom-call | flops 134217728 | bytes 2756608 | tf_op jit(solution)/shard_map/pallas_call | solution.py:233
  8.2 0.0 collective-permute-done.2.refs_4_
  8.3 1.5 %collective-permute-done.1.refs_3_ = bf16[80,512]{1,0:T(8,128)(2,1)S(1)} collective-permute-done((bf16[80,512]{1,0:T(8,128)(2,1)S(1)}, bf16[80,512]{1,0:T(8,128)(2,1)S(1)}, u32[]{:S(2)}, u32[]{:S(2)}) %collective-permute-start.1) | collective-permute-done | bytes 81952 | tf_op jit(solution)/shard_map/ppermute | solution.py:246
  9.8 0.5 %collective-permute-done.refs_2_ = bf16[80,512]{1,0:T(8,128)(2,1)S(1)} collective-permute-done((bf16[80,512]{1,0:T(8,128)(2,1)S(1)}, bf16[80,512]{1,0:T(8,128)(2,1)S(1)}, u32[]{:S(2)}, u32[]{:S(2)}) %collective-permute-start) | collective-permute-done | bytes 81952 | tf_op jit(solution)/shard_map/ppermute | solution.py:246
  10.3 2.3 %shard_map.103 = (bf16[1024,1536]{1,0:T(8,128)(2,1)S(1)}, bf16[64,1024]{1,0:T(8,128)(2,1)S(1)}) custom-call(bf16[1024,16]{1,0:T(8,128)(2,1)S(1)} %get-tuple-element.42.refs_0_, f32[64,1024]{1,0:T(8,128)S(1)} %get-tuple-element.45.refs_1_, bf16[80,512]{1,0:T(8,128)(2,1)S(1)} %collective-permute-done.refs_2_, ...), custom_call_target="tpu_custom_call" | custom-call | flops 201326592 | bytes 3817472 | tf_op jit(solution)/shard_map/pallas_call | solution.py:233
  12.6 0.1 collective-permute-start.3
  12.7 1.3 %shard_map.106 = (bf16[512,1536]{1,0:T(8,128)(2,1)S(1)}, f32[64,512]{1,0:T(8,128)S(1)}) custom-call(bf16[1024,16]{1,0:T(8,128)(2,1)S(1)} %get-tuple-element.42.refs_0_, f32[64,1024]{1,0:T(8,128)S(1)} %get-tuple-element.43.refs_1_, bf16[80,512]{1,0:T(8,128)(2,1)S(1)} %collective-permute-done.refs_2_, bf16[80,512]{1,0:T(8,128)(2,1)S(1)} %collective-permute-done.1.refs_3_, ...), custom_call_target="tpu_custom_call" | custom-call | flops 100663296 | bytes 2244608 | tf_op jit(solution)/shard_map/pallas_call | solution.py:233
  14.0 0.0 collective-permute-done.3.refs_1_
  14.0 1.6 %collective-permute-start.6 = (bf16[64,512]{1,0:T(8,128)(2,1)S(1)}, bf16[64,512]{1,0:T(8,128)(2,1)S(1)}, u32[]{:S(2)}, u32[]{:S(2)}) collective-permute-start(bf16[64,512]{1,0:T(8,128)(2,1)S(1)} %get-tuple-element.53), channel_id=1, source_target_pairs={{0,8},{4,20},{8,0},{12,28},{16,24},{20,4},{24,16},{28,12},{1,9},{5... | collective-permute-start | bytes 196616 | tf_op jit(solution)/shard_map/ppermute | solution.py:260
  15.6 1.3 %shard_map.102 = (bf16[512,1536]{1,0:T(8,128)(2,1)S(1)}, f32[64,512]{1,0:T(8,128)S(1)}) custom-call(bf16[1024,16]{1,0:T(8,128)(2,1)S(1)} %get-tuple-element.42.refs_0_, f32[64,1024]{1,0:T(8,128)S(1)} %get-tuple-element.43.refs_1_, bf16[80,512]{1,0:T(8,128)(2,1)S(1)} %collective-permute-done.refs_2_, bf16[80,512]{1,0:T(8,128)(2,1)S(1)} %collective-permute-done.1.refs_3_, ...), custom_call_target="tpu_custom_call" | custom-call | flops 100663296 | bytes 2244608 | tf_op jit(solution)/shard_map/pallas_call | solution.py:233
  17.0 0.5 %collective-permute-start.4 = (bf16[64,512]{1,0:T(8,128)(2,1)S(1)}, bf16[64,512]{1,0:T(8,128)(2,1)S(1)}, u32[]{:S(2)}, u32[]{:S(2)}) collective-permute-start(bf16[64,512]{1,0:T(8,128)(2,1)S(1)} %get-tuple-element.48), channel_id=1, source_target_pairs={{0,8},{4,20},{8,0},{12,28},{16,24},{20,4},{24,16},{28,12},{1,9},{5... | collective-permute-start | bytes 196616 | tf_op jit(solution)/shard_map/ppermute | solution.py:260
  17.5 1.5 %collective-permute-done.6.refs_1_ = bf16[64,512]{1,0:T(8,128)(2,1)S(1)} collective-permute-done((bf16[64,512]{1,0:T(8,128)(2,1)S(1)}, bf16[64,512]{1,0:T(8,128)(2,1)S(1)}, u32[]{:S(2)}, u32[]{:S(2)}) %collective-permute-start.6) | collective-permute-done | bytes 65568 | tf_op jit(solution)/shard_map/ppermute | solution.py:260
  19.1 2.1 %collective-permute-start.7 = (bf16[64,512]{1,0:T(8,128)(2,1)S(1)}, bf16[64,512]{1,0:T(8,128)(2,1)S(1)}, u32[]{:S(2)}, u32[]{:S(2)}) collective-permute-start(bf16[64,512]{1,0:T(8,128)(2,1)S(1)} %get-tuple-element.55), channel_id=1, source_target_pairs={{0,16},{4,12},{8,24},{12,4},{16,0},{20,28},{24,8},{28,20},{1,17},{... | collective-permute-start | bytes 196616 | tf_op jit(solution)/shard_map/ppermute | solution.py:260
  21.1 0.2 collective-permute-done.4.refs_1_
  21.3 3.2 %collective-permute-start.5 = (bf16[64,512]{1,0:T(8,128)(2,1)S(1)}, bf16[64,512]{1,0:T(8,128)(2,1)S(1)}, u32[]{:S(2)}, u32[]{:S(2)}) collective-permute-start(bf16[64,512]{1,0:T(8,128)(2,1)S(1)} %get-tuple-element.50), channel_id=1, source_target_pairs={{0,16},{4,12},{8,24},{12,4},{16,0},{20,28},{24,8},{28,20},{1,17},{... | collective-permute-start | bytes 196616 | tf_op jit(solution)/shard_map/ppermute | solution.py:260
  24.6 0.4 %collective-permute-done.7.refs_4_ = bf16[64,512]{1,0:T(8,128)(2,1)S(1)} collective-permute-done((bf16[64,512]{1,0:T(8,128)(2,1)S(1)}, bf16[64,512]{1,0:T(8,128)(2,1)S(1)}, u32[]{:S(2)}, u32[]{:S(2)}) %collective-permute-start.7) | collective-permute-done | bytes 65568 | tf_op jit(solution)/shard_map/ppermute | solution.py:260
  24.9 1.9 %collective-permute-done.5.refs_2_ = bf16[64,512]{1,0:T(8,128)(2,1)S(1)} collective-permute-done((bf16[64,512]{1,0:T(8,128)(2,1)S(1)}, bf16[64,512]{1,0:T(8,128)(2,1)S(1)}, u32[]{:S(2)}, u32[]{:S(2)}) %collective-permute-start.5) | collective-permute-done | bytes 65568 | tf_op jit(solution)/shard_map/ppermute | solution.py:260
  26.9 0.1 collective-permute-start.8
  27.0 0.8 %shard_map.110 = (f32[64,512]{1,0:T(8,128)S(1)}, f32[64,1536]{1,0:T(8,128)S(1)}) custom-call(bf16[64,1024]{1,0:T(8,128)(2,1)S(1)} %shard_map.109.w_ref, bf16[1024,512]{1,0:T(8,128)(2,1)S(1)} %get-tuple-element.57.p0_ref, bf16[512,1536]{1,0:T(8,128)(2,1)S(1)} %get-tuple-element.58.refs_0_, bf16[512,1536]{1,0:T(8,128)(2,1)S(1)} %get-tuple-element.59.refs_1_), custom_call_target="tpu_custom_call" | custom-call | flops 268435456 | bytes 4849664 | tf_op jit(solution)/shard_map/pallas_call | solution.py:233
  27.8 0.5 %collective-permute-done.8.w_ref = bf16[64,1024]{1,0:T(8,128)(2,1)S(1)} collective-permute-done((bf16[64,1024]{1,0:T(8,128)(2,1)S(1)}, bf16[64,1024]{1,0:T(8,128)(2,1)S(1)}, u32[]{:S(2)}, u32[]{:S(2)}) %collective-permute-start.8) | collective-permute-done | bytes 131104 | tf_op jit(solution)/shard_map/ppermute | solution.py:246
  28.3 0.0 copy-start
  28.3 0.0 copy-start.1
  28.3 0.0 copy-start.2
  28.3 0.7 %shard_map.112 = (bf16[64,512]{1,0:T(8,128)(2,1)S(1)}, bf16[64,512]{1,0:T(8,128)(2,1)S(1)}, bf16[64,512]{1,0:T(8,128)(2,1)S(1)}) custom-call(bf16[64,1024]{1,0:T(8,128)(2,1)S(1)} %collective-permute-done.8.w_ref, bf16[1024,1536]{1,0:T(8,128)(2,1)S(1)} %get-tuple-element.64.p_ref, f32[64,1536]{1,0:T(8,128)S(1)} %get-tuple-element.65.rest_ref), custom_call_target="tpu_custom_call" | custom-call | flops 201326592 | bytes 3866624 | tf_op jit(solution)/shard_map/pallas_call | solution.py:233
  29.0 1.6 %collective-permute-start.9 = (bf16[64,512]{1,0:T(8,128)(2,1)S(1)}, bf16[64,512]{1,0:T(8,128)(2,1)S(1)}, u32[]{:S(2)}, u32[]{:S(2)}) collective-permute-start(bf16[64,512]{1,0:T(8,128)(2,1)S(1)} %get-tuple-element.66), channel_id=1, source_target_pairs={{0,3},{1,2},{2,1},{3,0},{4,5},{5,4},{6,7},{7,6},{8,11},{9,10},{10,... | collective-permute-start | bytes 196616 | tf_op jit(solution)/shard_map/ppermute | solution.py:253
  30.6 1.0 %collective-permute-start.10 = (bf16[64,512]{1,0:T(8,128)(2,1)S(1)}, bf16[64,512]{1,0:T(8,128)(2,1)S(1)}, u32[]{:S(2)}, u32[]{:S(2)}) collective-permute-start(bf16[64,512]{1,0:T(8,128)(2,1)S(1)} %get-tuple-element.67), channel_id=1, source_target_pairs={{0,2},{1,3},{2,0},{3,1},{4,6},{5,7},{6,4},{7,5},{8,10},{9,11},{10,... | collective-permute-start | bytes 196616 | tf_op jit(solution)/shard_map/ppermute | solution.py:253
  31.5 1.0 %collective-permute-start.11 = (bf16[64,512]{1,0:T(8,128)(2,1)S(1)}, bf16[64,512]{1,0:T(8,128)(2,1)S(1)}, u32[]{:S(2)}, u32[]{:S(2)}) collective-permute-start(bf16[64,512]{1,0:T(8,128)(2,1)S(1)} %get-tuple-element.68), channel_id=1, source_target_pairs={{0,1},{1,0},{2,3},{3,2},{4,7},{5,6},{6,5},{7,4},{8,9},{9,8},{10,11... | collective-permute-start | bytes 196616 | tf_op jit(solution)/shard_map/ppermute | solution.py:253
  32.6 0.0 copy-done
  32.6 0.4 %shard_map.111 = (f32[64,512]{1,0:T(8,128)S(1)}, f32[512,256]{1,0:T(8,128)S(1)}) custom-call(bf16[64,1024]{1,0:T(8,128)(2,1)S(1)} %collective-permute-done.8.w_ref, bf16[1024,512]{1,0:T(8,128)(2,1)S(1)} %get-tuple-element.56.p0_ref, f32[64,512]{1,0:T(8,128)S(1)} %get-tuple-element.60.own_ref, bf16[512,128]{1,0:T(8,128)(2,1)S(1)} %get-tuple-element.61.mixed_ref, ...), custom_call_target="tpu_custom_call" | custom-call | flops 67108864 | bytes 2162688 | tf_op jit(solution)/shard_map/pallas_call | solution.py:233
  32.9 1.4 %collective-permute-done.9.refs_0_ = bf16[64,512]{1,0:T(8,128)(2,1)S(1)} collective-permute-done((bf16[64,512]{1,0:T(8,128)(2,1)S(1)}, bf16[64,512]{1,0:T(8,128)(2,1)S(1)}, u32[]{:S(2)}, u32[]{:S(2)}) %collective-permute-start.9) | collective-permute-done | bytes 65568 | tf_op jit(solution)/shard_map/ppermute | solution.py:253
  34.3 1.3 %collective-permute-done.10.refs_1_ = bf16[64,512]{1,0:T(8,128)(2,1)S(1)} collective-permute-done((bf16[64,512]{1,0:T(8,128)(2,1)S(1)}, bf16[64,512]{1,0:T(8,128)(2,1)S(1)}, u32[]{:S(2)}, u32[]{:S(2)}) %collective-permute-start.10) | collective-permute-done | bytes 65568 | tf_op jit(solution)/shard_map/ppermute | solution.py:253
  35.6 0.1 collective-permute-done.11.refs_2_
  35.8 0.0 copy-done.1
  35.8 0.0 copy-done.2
  35.8 1.1 %shard_map.113 = bf16[512,128]{1,0:T(8,128)(2,1)} custom-call(bf16[512,128]{1,0:T(8,128)(2,1)S(1)} %get-tuple-element.37.hidden_ref, f32[64,512]{1,0:T(8,128)S(1)} %get-tuple-element.62.total_ref, f32[512,256]{1,0:T(8,128)S(1)} %get-tuple-element.63.pre_ref, bf16[64,256]{1,0:T(8,128)(2,1)S(1)} %copy-done.2, bf16[256,128]{1,0:T(8,128)(2,1)S(1)} %copy-done.1, ...), custom_call_target="tpu_custom_call" | custom-call | bytes 1212416 | tf_op jit(solution)/shard_map/pallas_call | solution.py:233
  (5 shorter events, 0.1 us)
Async XLA Ops:
  1.4 6.9 %collective-permute-start.2 = (bf16[80,512]{1,0:T(8,128)(2,1)S(1)}, bf16[80,512]{1,0:T(8,128)(2,1)S(1)}, u32[]{:S(2)}, u32[]{:S(2)}) collective-permute-start(bf16[80,512]{1,0:T(8,128)(2,1)S(1)} %get-tuple-element.40.message_ref), channel_id=1, source_target_pairs={{0,3},{1,2},{2,1},{3,0},{4,7},{5,6},{6,5},{7,4},{8,11},{9,10},{10,... | collective-permute-start | bytes 245768 | tf_op jit(solution)/shard_map/ppermute | solution.py:246
  5.3 4.4 %collective-permute-start.1 = (bf16[80,512]{1,0:T(8,128)(2,1)S(1)}, bf16[80,512]{1,0:T(8,128)(2,1)S(1)}, u32[]{:S(2)}, u32[]{:S(2)}) collective-permute-start(bf16[80,512]{1,0:T(8,128)(2,1)S(1)} %get-tuple-element.40.message_ref), channel_id=1, source_target_pairs={{0,2},{1,3},{2,0},{3,1},{4,6},{5,7},{6,4},{7,5},{8,10},{9,11},{10,... | collective-permute-start | bytes 245768 | tf_op jit(solution)/shard_map/ppermute | solution.py:246
  5.8 4.4 %collective-permute-start = (bf16[80,512]{1,0:T(8,128)(2,1)S(1)}, bf16[80,512]{1,0:T(8,128)(2,1)S(1)}, u32[]{:S(2)}, u32[]{:S(2)}) collective-permute-start(bf16[80,512]{1,0:T(8,128)(2,1)S(1)} %get-tuple-element.40.message_ref), channel_id=1, source_target_pairs={{0,1},{1,0},{2,3},{3,2},{4,5},{5,4},{6,7},{7,6},{8,9},{9,8},{10,11... | collective-permute-start | bytes 245768 | tf_op jit(solution)/shard_map/ppermute | solution.py:246
  12.6 1.4 %collective-permute-start.3 = (bf16[64,1024]{1,0:T(8,128)(2,1)S(1)}, bf16[64,1024]{1,0:T(8,128)(2,1)S(1)}, u32[]{:S(2)}, u32[]{:S(2)}) collective-permute-start(bf16[64,1024]{1,0:T(8,128)(2,1)S(1)} %get-tuple-element.46), channel_id=1, source_target_pairs={{0,4},{4,0},{8,12},{12,8},{16,20},{20,16},{24,28},{28,24},{1,5},{5... | collective-permute-start | bytes 393224 | tf_op jit(solution)/shard_map/ppermute | solution.py:246
  14.0 5.0 %collective-permute-start.6 = (bf16[64,512]{1,0:T(8,128)(2,1)S(1)}, bf16[64,512]{1,0:T(8,128)(2,1)S(1)}, u32[]{:S(2)}, u32[]{:S(2)}) collective-permute-start(bf16[64,512]{1,0:T(8,128)(2,1)S(1)} %get-tuple-element.53), channel_id=1, source_target_pairs={{0,8},{4,20},{8,0},{12,28},{16,24},{20,4},{24,16},{28,12},{1,9},{5... | collective-permute-start | bytes 196616 | tf_op jit(solution)/shard_map/ppermute | solution.py:260
  17.0 4.3 %collective-permute-start.4 = (bf16[64,512]{1,0:T(8,128)(2,1)S(1)}, bf16[64,512]{1,0:T(8,128)(2,1)S(1)}, u32[]{:S(2)}, u32[]{:S(2)}) collective-permute-start(bf16[64,512]{1,0:T(8,128)(2,1)S(1)} %get-tuple-element.48), channel_id=1, source_target_pairs={{0,8},{4,20},{8,0},{12,28},{16,24},{20,4},{24,16},{28,12},{1,9},{5... | collective-permute-start | bytes 196616 | tf_op jit(solution)/shard_map/ppermute | solution.py:260
  19.1 5.9 %collective-permute-start.7 = (bf16[64,512]{1,0:T(8,128)(2,1)S(1)}, bf16[64,512]{1,0:T(8,128)(2,1)S(1)}, u32[]{:S(2)}, u32[]{:S(2)}) collective-permute-start(bf16[64,512]{1,0:T(8,128)(2,1)S(1)} %get-tuple-element.55), channel_id=1, source_target_pairs={{0,16},{4,12},{8,24},{12,4},{16,0},{20,28},{24,8},{28,20},{1,17},{... | collective-permute-start | bytes 196616 | tf_op jit(solution)/shard_map/ppermute | solution.py:260
  21.3 5.5 %collective-permute-start.5 = (bf16[64,512]{1,0:T(8,128)(2,1)S(1)}, bf16[64,512]{1,0:T(8,128)(2,1)S(1)}, u32[]{:S(2)}, u32[]{:S(2)}) collective-permute-start(bf16[64,512]{1,0:T(8,128)(2,1)S(1)} %get-tuple-element.50), channel_id=1, source_target_pairs={{0,16},{4,12},{8,24},{12,4},{16,0},{20,28},{24,8},{28,20},{1,17},{... | collective-permute-start | bytes 196616 | tf_op jit(solution)/shard_map/ppermute | solution.py:260
  26.9 1.4 %collective-permute-start.8 = (bf16[64,1024]{1,0:T(8,128)(2,1)S(1)}, bf16[64,1024]{1,0:T(8,128)(2,1)S(1)}, u32[]{:S(2)}, u32[]{:S(2)}) collective-permute-start(bf16[64,1024]{1,0:T(8,128)(2,1)S(1)} %shard_map.109.w_ref), channel_id=1, source_target_pairs={{0,4},{4,0},{8,12},{12,8},{16,20},{20,16},{24,28},{28,24},{1,5},{5... | collective-permute-start | bytes 393224 | tf_op jit(solution)/shard_map/ppermute | solution.py:246
  28.3 4.2 %copy-start = (bf16[128,256]{1,0:T(8,128)(2,1)S(1)}, bf16[128,256]{1,0:T(8,128)(2,1)}, u32[]{:S(2)}) copy-start(bf16[128,256]{1,0:T(8,128)(2,1)} %w_feat_ref.1) | copy-start | bytes 196612
  28.3 7.5 %copy-start.1 = (bf16[256,128]{1,0:T(8,128)(2,1)S(1)}, bf16[256,128]{1,0:T(8,128)(2,1)}, u32[]{:S(2)}) copy-start(bf16[256,128]{1,0:T(8,128)(2,1)} %w_out_ref.1) | copy-start | bytes 196612
  28.3 7.5 %copy-start.2 = (bf16[64,256]{1,0:T(8,128)(2,1)S(1)}, bf16[64,256]{1,0:T(8,128)(2,1)}, u32[]{:S(2)}) copy-start(bf16[64,256]{1,0:T(8,128)(2,1)} %w_pot_ref.1) | copy-start | bytes 98308
  29.0 5.3 %collective-permute-start.9 = (bf16[64,512]{1,0:T(8,128)(2,1)S(1)}, bf16[64,512]{1,0:T(8,128)(2,1)S(1)}, u32[]{:S(2)}, u32[]{:S(2)}) collective-permute-start(bf16[64,512]{1,0:T(8,128)(2,1)S(1)} %get-tuple-element.66), channel_id=1, source_target_pairs={{0,3},{1,2},{2,1},{3,0},{4,5},{5,4},{6,7},{7,6},{8,11},{9,10},{10,... | collective-permute-start | bytes 196616 | tf_op jit(solution)/shard_map/ppermute | solution.py:253
  30.6 5.1 %collective-permute-start.10 = (bf16[64,512]{1,0:T(8,128)(2,1)S(1)}, bf16[64,512]{1,0:T(8,128)(2,1)S(1)}, u32[]{:S(2)}, u32[]{:S(2)}) collective-permute-start(bf16[64,512]{1,0:T(8,128)(2,1)S(1)} %get-tuple-element.67), channel_id=1, source_target_pairs={{0,2},{1,3},{2,0},{3,1},{4,6},{5,7},{6,4},{7,5},{8,10},{9,11},{10,... | collective-permute-start | bytes 196616 | tf_op jit(solution)/shard_map/ppermute | solution.py:253
  31.5 4.3 %collective-permute-start.11 = (bf16[64,512]{1,0:T(8,128)(2,1)S(1)}, bf16[64,512]{1,0:T(8,128)(2,1)S(1)}, u32[]{:S(2)}, u32[]{:S(2)}) collective-permute-start(bf16[64,512]{1,0:T(8,128)(2,1)S(1)} %get-tuple-element.68), channel_id=1, source_target_pairs={{0,1},{1,0},{2,3},{3,2},{4,7},{5,6},{6,5},{7,4},{8,9},{9,8},{10,11... | collective-permute-start | bytes 196616 | tf_op jit(solution)/shard_map/ppermute | solution.py:253
